TPU v7x, 32 devices: a whole 2x2x4 slice. The times are simulated.
32 devices in a mesh: groups: 2 (over x), ctx: 16 (over z, y, core).
Axes of the slice: x: 2, y: 2, z: 4, core: 2. Of those that a mesh axis runs over, the one named last changes fastest.
Arguments:
- gate_short: bfloat16 [4096, 4096], P(('groups', 'ctx')), parts along dimension 0, may hold values from -6 to 6
- key_short: bfloat16 [4096, 4096], P(('groups', 'ctx')), parts along dimension 0, may hold values from -6 to 6
- value_short: bfloat16 [4096, 4096], P(('groups', 'ctx')), parts along dimension 0, may hold values from -6 to 6
- gate_long: bfloat16 [4096, 4096], P(('groups', 'ctx')), parts along dimension 0, may hold values from -6 to 6
- doc_ids: int32 [4096], P(('groups', 'ctx')), parts along dimension 0, may hold values from 0 to 7, never falling along the last dimension, each value on 1 to 512 neighbouring positions
- se_filter: float32 [7, 256], replicated, may hold values from -2 to 2
- long_filter: bfloat16 [256, 512], replicated, may hold values from -1.25 to 1.25
Outputs:
- scored: bfloat16 [4096, 4096], P(('groups', 'ctx')), parts along dimension 0
There are 2 independent parts, one for each index of `groups`. A program takes and returns all parts, laid end to end along the dimension named above; an argument that names none is the same for every part. Nothing has to cross between parts.
Inputs may be any that keep to these rules, and one draw needn't show every extreme that they name: doc_ids never falls along the rows of a group; each document holds 1 to 512 consecutive rows, and one holds exactly 512.
All inputs are finite; a program needn't handle non-finite values.
Results may differ from a plain program's by a relative error of at most 0.0057.
Values may be sent and summed in bfloat16 or wider, within the bound.
No kernel may reach another device: no remote copies, remote signals or barrier semaphores. Data moves between devices by JAX's collectives and lax.ppermute only.
A program may use at most 192 MiB of HBM per device.

v0:
```python
import jax
import jax.numpy as jnp
from jax import lax
from jax.sharding import PartitionSpec as P

STRETCH = 128
MAXDOC = 512
REACH = 4


def passed_along(value, axis, steps):
    count = lax.axis_size(axis)
    first, last = (max(0, -steps), min(count, count - steps))
    return lax.ppermute(value, axis, [(source, source + steps) for source in range(first, last)])


def shortened(value):

    def short(part):
        return part.astype(jnp.bfloat16) if part.dtype == jnp.float32 else part

    return jax.tree.map(short, value)


def short_mixing(key_value, rim_value, doc_ids, rim_doc, se_filter):
    row_count, chan_count = key_value.shape
    tap_count, filter_count = se_filter.shape
    widened = jnp.repeat(se_filter, chan_count // filter_count, axis=1)
    joined = jnp.concatenate([rim_value, key_value], 0)
    joined_doc = jnp.concatenate([rim_doc, doc_ids], 0)
    summed = jnp.zeros((row_count, chan_count), jnp.float32)
    for tap_index in range(tap_count):
        offset = tap_count - 1 - tap_index
        shifted = lax.slice_in_dim(joined, offset, offset + row_count, axis=0).astype(jnp.float32)
        agreeing = (
            lax.slice_in_dim(joined_doc, offset, offset + row_count, axis=0) == doc_ids
        ).astype(jnp.float32)
        summed = summed + widened[tap_index][None, :] * agreeing[:, None] * shifted
    return summed


def tile_product(operands):
    far_taps, gathered = operands
    return jnp.einsum("gtp,gkip->gkit", far_taps, gathered, preferred_element_type=jnp.float32)


def body(gate_short, key_short, value_short, gate_long, doc_ids, se_filter, long_filter):
    row_count, chan_count = gate_short.shape
    tap_count, filter_count = se_filter.shape
    group_width = chan_count // filter_count
    key_value = (key_short.astype(jnp.float32) * value_short.astype(jnp.float32)).astype(
        jnp.bfloat16
    )
    rim_value, rim_doc = passed_along(
        (key_value[row_count - (tap_count - 1) :], doc_ids[row_count - (tap_count - 1) :]), "ctx", 1
    )
    local_value = lax.optimization_barrier(key_value)
    short_mix = short_mixing(local_value, rim_value, doc_ids, rim_doc, se_filter)
    mixed = (gate_short.astype(jnp.float32) * short_mix).astype(jnp.bfloat16)
    mixed_cols = mixed.T
    per_device = row_count // STRETCH
    span_count = MAXDOC // STRETCH
    blocks = [(mixed_cols, doc_ids)]
    stride = 1
    while len(blocks) <= REACH:
        wanted = min(stride, REACH + 1 - len(blocks))
        sent_rows = jnp.stack([entry_pair[0] for entry_pair in blocks[:wanted]])
        sent_docs = jnp.stack([entry_pair[1] for entry_pair in blocks[:wanted]])
        got_rows, got_docs = (
            passed_along(sent_rows, "ctx", stride),
            passed_along(shortened(sent_docs), "ctx", stride).astype(sent_docs.dtype),
        )
        for position in range(wanted):
            blocks.append((got_rows[position], got_docs[position]))
        stride = stride * 2
    ordered = blocks[::-1]
    stack_rows = jnp.concatenate([entry_pair[0] for entry_pair in ordered], 1).reshape(
        filter_count, group_width, -1
    )
    stack_docs = jnp.concatenate([entry_pair[1] for entry_pair in ordered], 0)
    own_first = REACH * per_device
    own_rows = stack_rows[:, :, own_first * STRETCH :].reshape(
        filter_count, group_width, per_device, STRETCH
    )
    own_docs = doc_ids.reshape(per_device, STRETCH)
    leaders = own_docs[:, 0]
    padded_filter = jnp.concatenate(
        [long_filter, jnp.zeros((filter_count, STRETCH), jnp.bfloat16)], 1
    )
    target_pos = lax.broadcasted_iota(jnp.int32, (STRETCH, STRETCH), 0)
    source_pos = lax.broadcasted_iota(jnp.int32, (STRETCH, STRETCH), 1)
    near_lag = target_pos - source_pos
    near_taps = jnp.take(padded_filter, jnp.clip(near_lag, 0, STRETCH - 1), axis=1)
    tile_mask = (near_lag >= 0)[None] & (own_docs[:, :, None] == own_docs[:, None, :])
    masked_taps = jnp.where(tile_mask[None], near_taps[:, None], jnp.zeros((), jnp.bfloat16))
    near_total = jnp.einsum(
        "gits,gkis->gkit", masked_taps, own_rows, preferred_element_type=jnp.float32
    )
    far_width = span_count * STRETCH
    window_tgt = lax.broadcasted_iota(jnp.int32, (STRETCH, far_width), 0)
    window_pos = lax.broadcasted_iota(jnp.int32, (STRETCH, far_width), 1)
    far_lag = window_tgt - window_pos + far_width
    far_taps = jnp.take(padded_filter, far_lag, axis=1)
    matches = []
    lowest = (own_first - span_count) * STRETCH
    source_docs = stack_docs[lowest : lowest + far_width]
    agreeing = source_docs == leaders[0]
    matches.append(agreeing)
    source_rows = stack_rows[:, :, lowest : lowest + far_width]
    sources = [jnp.where(agreeing[None, None, :], source_rows, jnp.zeros_like(source_rows))]
    gathered = jnp.stack(sources, 2)
    far_total = tile_product((far_taps, gathered))
    target_mask = (own_docs == leaders[:, None]).astype(jnp.float32)
    long_sum = (near_total + far_total * target_mask[None, None]).reshape(chan_count, row_count).T
    return (gate_long.astype(jnp.float32) * long_sum).astype(jnp.bfloat16)


def solution(mesh):
    placed = (
        P(("groups", "ctx"), None),
        P(("groups", "ctx"), None),
        P(("groups", "ctx"), None),
        P(("groups", "ctx"), None),
        P(("groups", "ctx")),
        P(),
        P(),
    )
    return jax.shard_map(
        body, mesh=mesh, in_specs=placed, out_specs=P(("groups", "ctx"), None), check_vma=False
    )
```

profile of v0, /device:TPU:0, one launch (start us, length us, event | category | flops | bytes accessed | tf_op | source)
XLA Modules:
  0.0 472.3 jit_solution(6332125714934271169)
XLA Ops:
  0.0 1.7 copy.26
  1.7 0.7 copy.25
  2.4 0.3 multiply_convert_fusion.1
  2.7 0.4 slice.146
  3.1 0.4 copy.27
  3.4 2.4 collective-permute-start.1
  5.8 0.1 slice.113
  5.9 4.5 collective-permute-start
  10.4 0.7 copy.24
  11.1 0.1 broadcast_in_dim.96
  11.2 0.1 broadcast_in_dim.97
  11.3 0.1 broadcast_in_dim.94
  11.4 0.1 broadcast_in_dim.95
  11.5 0.1 broadcast_in_dim.92
  11.6 0.1 broadcast_in_dim.93
  11.8 0.1 broadcast_in_dim.90
  11.8 0.1 broadcast_in_dim.91
  12.0 0.1 broadcast_in_dim.88
  12.1 0.1 broadcast_in_dim.89
  12.2 0.1 broadcast_in_dim.86
  12.3 0.1 broadcast_in_dim.87
  12.4 0.1 broadcast_in_dim.84
  12.5 0.1 broadcast_in_dim.85
  12.6 0.1 pad_add_fusion
  12.7 0.1 compare_convert_fusion.6
  12.8 0.5 copy.28
  13.3 7.6 %multiply_convert_fusion = bf16[128,4096]{0,1:T(8,128)(2,1)S(1)} fusion(bf16[128,4096]{0,1:T(8,128)(2,1)S(1)} %multiply_convert_fusion.1, bf16[128,4096]{0,1:T(8,128)(2,1)S(1)} %copy.24, bf16[6,4096]{0,1:T(8,128)(2,1)S(1)} %copy.28, f32[128]{0:T(128)S(1)} %get-tuple-element.15, f32[4096]{0:T(1024)S(1)} %broadcast_in_dim.97, f32[128]{0:T(128)S(1)} %get-tuple-element.16, ...), kind=kLoop, calls=%fused_computation.38 | loop fusion | flops 24641536 | bytes 3312640 | tf_op jit(solution)/shard_map/convert_element_type | solution.py:59
  20.9 2.0 collective-permute-start.6
  22.9 3.5 collective-permute-start.3
  26.3 3.5 collective-permute-start.2
  29.9 0.1 copy.33
  30.0 1.7 pad_maximum_fusion
  31.6 10.6 %collective-permute-start.7 = (bf16[2,4096,128]{2,1,0:T(8,128)(2,1)}, bf16[2,4096,128]{2,1,0:T(8,128)(2,1)S(1)}, u32[]{:S(2)}, u32[]{:S(2)}) collective-permute-start(bf16[2,4096,128]{2,1,0:T(8,128)(2,1)} %pad_maximum_fusion), channel_id=1, source_target_pairs={{0,2},{1,3},{2,4},{3,5},{4,6},{5,7},{6,8},{7,9},{8,10},{9,11},{10,... | collective-permute-start | bytes 6291464 | tf_op jit(solution)/shard_map/ppermute | solution.py:14
  42.3 0.1 fusion.38
  42.4 4.3 collective-permute-start.4
  46.7 0.1 copy.29
  46.9 65.2 %gather_fusion = bf16[16384,256]{1,0:T(8,128)(2,1)} fusion(bf16[256,640]{0,1:T(8,128)(2,1)S(1)} %concatenate.39, s32[16384]{0:T(1024)S(1)} %fusion.34), kind=kCustom, calls=%fused_computation | custom fusion | bytes 16842752 | tf_op jit(solution)/shard_map/jit(_take)/gather | solution.py:93
  112.1 12.5 %copy.30 = bf16[128,128,256]{1,0,2:T(8,128)(2,1)} copy(bf16[128,128,256]{2,1,0:T(8,128)(2,1)} %bitcast.50) | data formatting | bytes 16777216 | tf_op jit(solution)/shard_map/jit(_take)/gather | solution.py:93
  124.5 257.8 %gather_fusion.1 = bf16[65536,256]{1,0:T(8,128)(2,1)} fusion(bf16[256,640]{0,1:T(8,128)(2,1)S(1)} %concatenate.39, s32[65536]{0:T(1024)S(1)} %broadcast_clamp_fusion), kind=kCustom, calls=%fused_computation.1 | custom fusion | bytes 67371008 | tf_op jit(solution)/shard_map/jit(_take)/gather | solution.py:103
  382.3 44.9 %copy.31 = bf16[128,512,256]{1,0,2:T(8,128)(2,1)} copy(bf16[128,512,256]{2,1,0:T(8,128)(2,1)} %bitcast.49) | data formatting | bytes 67108864 | tf_op jit(solution)/shard_map/jit(_take)/gather | solution.py:103
  427.3 3.6 collective-permute-start.5
  430.8 9.2 %fusion.5 = f32[256,16,128]{2,1,0:T(8,128)} fusion(bf16[256,16,128]{2,1,0:T(8,128)(2,1)S(1)} %bitcast.54, bf16[128,128,256]{1,0,2:T(8,128)(2,1)} %copy.30, pred[128,128]{1,0:T(8,128)(4,1)S(1)} %get-tuple-element.24, pred[128,128]{1,0:T(8,128)(4,1)S(1)} %get-tuple-element.23), kind=kOutput, calls=%fused_computation.7 | convolution fusion | flops 142606336 | bytes 11567104 | tf_op jit(solution)/shard_map/gits,gkis->gkit/dot_general | solution.py:96
  440.0 1.5 fusion.45
  441.5 9.5 %collective-permute-done.5 = bf16[1,4096,128]{2,1,0:T(8,128)(2,1)S(1)} collective-permute-done((bf16[1,4096,128]{2,1,0:T(8,128)(2,1)S(1)}, bf16[1,4096,128]{2,1,0:T(8,128)(2,1)S(1)}, u32[]{:S(2)}, u32[]{:S(2)}) %collective-permute-start.5) | collective-permute-done | bytes 1048608 | tf_op jit(solution)/shard_map/ppermute | solution.py:14
  451.0 1.0 copy-done.9
  452.0 17.1 %multiply_add_fusion = f32[256,16,128]{2,1,0:T(8,128)} fusion(f32[256,16,128]{2,1,0:T(8,128)} %fusion.5, bf16[128,512,256]{1,0,2:T(8,128)(2,1)} %copy.31, pred[128,512]{1,0:T(8,128)(4,1)S(1)} %fusion.32, bf16[256,16,128]{2,1,0:T(8,128)(2,1)} %bitcast.57, bf16[256,16,128]{2,1,0:T(8,128)(2,1)} %bitcast.59, bf16[256,16,128]{2,1,0:T(8,128)(2,1)} %bitcast.58, ...), kind=kOutput, calls=%fused_computation.36 | convolution fusion | flops 573571072 | bytes 42009600 | tf_op jit(solution)/shard_map/gtp,gkip->gkit/dot_general | solution.py:44
  469.1 2.0 copy.32
  471.1 1.2 fusion.20
  (35 shorter events, 0.3 us)
Async XLA Ops:
  0.0 1.7 copy-start.2
  2.7 3.1 copy-start.7
  2.7 7.7 %copy-start.3 = (bf16[128,4096]{1,0:T(8,128)(2,1)S(1)}, bf16[128,4096]{1,0:T(8,128)(2,1)}, u32[]{:S(2)}) copy-start(bf16[128,4096]{1,0:T(8,128)(2,1)} %param.7) | copy-start | bytes 3145732
  3.1 8.1 %copy-start.8 = (f32[7,256]{1,0:T(8,128)S(1)}, f32[7,256]{1,0:T(8,128)}, u32[]{:S(2)}) copy-start(f32[7,256]{1,0:T(8,128)} %param.12) | copy-start | bytes 21508
  3.4 9.3 %collective-permute-start.1 = (bf16[6,4096]{1,0:T(8,128)(2,1)S(1)}, bf16[6,4096]{1,0:T(8,128)(2,1)S(1)}, u32[]{:S(2)}, u32[]{:S(2)}) collective-permute-start(bf16[6,4096]{1,0:T(8,128)(2,1)S(1)} %copy.27), channel_id=1, source_target_pairs={{0,1},{1,2},{2,3},{3,4},{4,5},{5,6},{6,7},{7,8},{8,9},{9,10},{10,1... | collective-permute-start | bytes 147464 | tf_op jit(solution)/shard_map/ppermute | solution.py:14
  5.9 6.7 %collective-permute-start = (s32[6]{0:T(128)S(1)}, s32[6]{0:T(128)S(1)}, u32[]{:S(2)}, u32[]{:S(2)}) collective-permute-start(s32[6]{0:T(128)S(1)} %slice.113), channel_id=1, source_target_pairs={{0,1},{1,2},{2,3},{3,4},{4,5},{5,6},{6,7},{7,8},{8,9},{9,10},{10,1... | collective-permute-start | bytes 80 | tf_op jit(solution)/shard_map/ppermute | solution.py:14
  20.9 10.8 %copy-start = (bf16[128,4096]{0,1:T(8,128)(2,1)}, bf16[128,4096]{0,1:T(8,128)(2,1)S(1)}, u32[]{:S(2)}) copy-start(bf16[128,4096]{0,1:T(8,128)(2,1)S(1)} %multiply_convert_fusion) | copy-start | bytes 3145732
  20.9 9.1 %collective-permute-start.6 = (bf16[1,4096,128]{2,1,0:T(8,128)(2,1)S(1)}, bf16[1,4096,128]{2,1,0:T(8,128)(2,1)S(1)}, u32[]{:S(2)}, u32[]{:S(2)}) collective-permute-start(bf16[1,4096,128]{2,1,0:T(8,128)(2,1)S(1)} %bitcast.51), channel_id=1, source_target_pairs={{0,1},{1,2},{2,3},{3,4},{4,5},{5,6},{6,7},{7,8},{8,9},{9,10},{10,1... | collective-permute-start | bytes 3145736 | tf_op jit(solution)/shard_map/ppermute | solution.py:14
  22.9 19.5 %collective-permute-start.3 = (s32[1,128]{1,0:T(1,128)S(1)}, s32[1,128]{1,0:T(1,128)S(1)}, u32[]{:S(2)}, u32[]{:S(2)}) collective-permute-start(s32[1,128]{1,0:T(1,128)S(1)} %bitcast.61), channel_id=1, source_target_pairs={{0,1},{1,2},{2,3},{3,4},{4,5},{5,6},{6,7},{7,8},{8,9},{9,10},{10,1... | collective-permute-start | bytes 1544 | tf_op jit(solution)/shard_map/ppermute | solution.py:14
  26.3 400.9 %collective-permute-start.2 = (s32[1,128]{1,0:T(1,128)S(1)}, s32[1,128]{1,0:T(1,128)S(1)}, u32[]{:S(2)}, u32[]{:S(2)}) collective-permute-start(s32[1,128]{1,0:T(1,128)S(1)} %bitcast.62), channel_id=1, source_target_pairs={{0,4},{1,5},{2,6},{3,7},{4,8},{5,9},{6,10},{7,11},{8,12},{9,13},{1... | collective-permute-start | bytes 1544 | tf_op jit(solution)/shard_map/ppermute | solution.py:14
  29.9 16.8 %copy-start.6 = (bf16[256,512]{1,0:T(8,128)(2,1)S(1)}, bf16[256,512]{1,0:T(8,128)(2,1)}, u32[]{:S(2)}) copy-start(bf16[256,512]{1,0:T(8,128)(2,1)} %param.13) | copy-start | bytes 786436
  30.0 12.2 %copy-start.5 = (bf16[1,4096,128]{2,1,0:T(8,128)(2,1)}, bf16[1,4096,128]{2,1,0:T(8,128)(2,1)S(1)}, u32[]{:S(2)}) copy-start(bf16[1,4096,128]{2,1,0:T(8,128)(2,1)S(1)} %collective-permute-done.6) | copy-start | bytes 3145732
  31.6 408.4 %collective-permute-start.7 = (bf16[2,4096,128]{2,1,0:T(8,128)(2,1)}, bf16[2,4096,128]{2,1,0:T(8,128)(2,1)S(1)}, u32[]{:S(2)}, u32[]{:S(2)}) collective-permute-start(bf16[2,4096,128]{2,1,0:T(8,128)(2,1)} %pad_maximum_fusion), channel_id=1, source_target_pairs={{0,2},{1,3},{2,4},{3,5},{4,6},{5,7},{6,8},{7,9},{8,10},{9,11},{10,... | collective-permute-start | bytes 6291464 | tf_op jit(solution)/shard_map/ppermute | solution.py:14
  42.4 384.8 %collective-permute-start.4 = (s32[2,128]{1,0:T(2,128)S(1)}, s32[2,128]{1,0:T(2,128)S(1)}, u32[]{:S(2)}, u32[]{:S(2)}) collective-permute-start(s32[2,128]{1,0:T(2,128)S(1)} %pad_add_fusion.1), channel_id=1, source_target_pairs={{0,2},{1,3},{2,4},{3,5},{4,6},{5,7},{6,8},{7,9},{8,10},{9,11},{10,... | collective-permute-start | bytes 3080 | tf_op jit(solution)/shard_map/ppermute | solution.py:14
  382.3 44.9 %copy-start.1 = (bf16[128,4096]{0,1:T(8,128)(2,1)S(1)}, bf16[128,4096]{0,1:T(8,128)(2,1)}, u32[]{:S(2)}) copy-start(bf16[128,4096]{0,1:T(8,128)(2,1)} %copy-done) | copy-start | bytes 3145732
  427.3 23.7 %collective-permute-start.5 = (bf16[1,4096,128]{2,1,0:T(8,128)(2,1)S(1)}, bf16[1,4096,128]{2,1,0:T(8,128)(2,1)S(1)}, u32[]{:S(2)}, u32[]{:S(2)}) collective-permute-start(bf16[1,4096,128]{2,1,0:T(8,128)(2,1)S(1)} %bitcast.53), channel_id=1, source_target_pairs={{0,4},{1,5},{2,6},{3,7},{4,8},{5,9},{6,10},{7,11},{8,12},{9,13},{1... | collective-permute-start | bytes 3145736 | tf_op jit(solution)/shard_map/ppermute | solution.py:14
  451.0 1.0 copy-start.9
  469.1 2.0 copy-start.4
where the time goes:
time: 474 us; the launch traced here: 472 us
  local copies, waits for them, and re-layouts  391 us (82%)
  starting transfers between devices  34.2 us (7%)
  matrix products  26.3 us (6%)
  other arithmetic  11.1 us (2%)
  waiting for transfers between devices  9.52 us (2%)
    gather x2, local copies, waits for them, and re-layouts, body(): far_taps = jnp.take(padded_filter, far_lag, axis=1)  303 us
    gather x2, local copies, waits for them, and re-layouts, body(): jnp.take(padded_filter, jnp.clip(near_lag, 0, STRETCH - 1), axis=1)  77.7 us
    ppermute x8, starting transfers between devices, passed_along(): lax.ppermute(value, axis, [(source, source + steps) for source in range(f...  34.2 us
    dot_general x1, matrix products, tile_product(): jnp.einsum('gtp,gkip->gkit', far_taps, gathered, preferred_element_type=j...  17.1 us
    ppermute x8, waiting for transfers between devices, passed_along(): lax.ppermute(value, axis, [(source, source + steps) for source in range(f...  9.52 us
  transfers between devices with their start and end apart: 8, of which 1 were waited for; matrix products, arithmetic and copies ran while one was open for 84% of the time, Pallas kernels for 0%

commit v1 on v0

v1 whole, which is shorter than its diff:
```python
import functools

import jax
import jax.numpy as jnp
from jax import lax
from jax.experimental import pallas as pl
from jax.experimental.pallas import tpu as pltpu
from jax.sharding import PartitionSpec as P

F32 = jnp.float32
BF16 = jnp.bfloat16
SLAB = 16
LANES = 128
LIMIT = 40 * 1024 * 1024


def params():
    return pltpu.CompilerParams(vmem_limit_bytes=LIMIT)


def column(row):
    width = row.shape[1]
    return jnp.transpose(jnp.broadcast_to(row.astype(F32), (width, width)))


def pick(lane_group, parts):
    out = parts[0]
    for index in range(1, len(parts)):
        out = jnp.where(lane_group == index, parts[index], out)
    return out


def pack_kernel(core, key, value, gate, out):
    out[0] = (key[...].astype(F32) * value[...].astype(F32)).astype(BF16)
    out[1] = gate[...]


def short_kernel(core, docs_own, docs_sib, key, value, gate, sib, taps, mixed, mixed_a, mixed_b, tail, head,
                 kv_rows, gate_rows, agree, doc_rows):
    step = pl.program_id(0)
    rows, width = key.shape
    tap_count = taps.shape[0]
    mine = pl.multiple_of(core[0] * rows, rows)
    other = pl.multiple_of((1 - core[0]) * rows, rows)

    @pl.when(step == 0)
    def _():
        doc_rows[0:8, :] = jnp.full((8, LANES), -1.0, F32)
        doc_rows[pl.ds(8 + mine, rows), :] = column(docs_own[...])
        doc_rows[pl.ds(8 + other, rows), :] = column(docs_sib[...])
        here = doc_rows[8 : 8 + 2 * rows, :]
        for k in range(1, tap_count):
            agree[k] = (doc_rows[8 - k : 8 - k + 2 * rows, :] == here).astype(F32)
        kv_rows[0:8, :] = jnp.zeros((8, width), F32)

    kv_rows[pl.ds(8 + mine, rows), :] = (key[...].astype(F32) * value[...].astype(F32)).astype(BF16).astype(F32)
    kv_rows[pl.ds(8 + other, rows), :] = sib[0].astype(F32)
    gate_rows[pl.ds(mine, rows), :] = gate[...].astype(F32)
    gate_rows[pl.ds(other, rows), :] = sib[1].astype(F32)
    for at in range(0, width, LANES):
        cols = slice(at, at + LANES)
        total = kv_rows[8 : 8 + 2 * rows, cols] * taps[0:1, cols]
        for k in range(1, tap_count):
            total = total + agree[k] * kv_rows[8 - k : 8 - k + 2 * rows, cols] * taps[k : k + 1, cols]
        mixed[:, cols] = (gate_rows[:, cols] * total).astype(BF16)

    half = pl.num_programs(0) // 2

    @pl.when(step < half)
    def _():
        mixed_a[...] = mixed[...]

    @pl.when(step >= half)
    def _():
        mixed_b[...] = mixed[...]

    first = jnp.where(core[0] == 0, docs_own[...], docs_sib[...]).astype(F32)
    second = jnp.where(core[0] == 0, docs_sib[...], docs_own[...]).astype(F32)
    tail[0:SLAB, :] = kv_rows[8 + 2 * rows - SLAB : 8 + 2 * rows, :].astype(BF16)
    tail[SLAB : 2 * SLAB, :] = jnp.zeros((SLAB, width), BF16)
    tail[SLAB : 2 * SLAB, 0:rows] = jnp.broadcast_to(first, (SLAB, rows)).astype(BF16)
    tail[SLAB : 2 * SLAB, rows : 2 * rows] = jnp.broadcast_to(second, (SLAB, rows)).astype(BF16)
    head[0:SLAB, :] = kv_rows[8 : 8 + SLAB, :].astype(BF16)
    head[SLAB : 2 * SLAB, :] = gate_rows[0:SLAB, :].astype(BF16)


def head_kernel(tail, raw, docs, taps, out, kv_rows, doc_rows):
    rows = docs.shape[1] // 2
    tap_count = taps.shape[0]
    before = column(tail[SLAB : 2 * SLAB, rows : 2 * rows].astype(F32)[0:1])
    doc_rows[0:8, :] = before[rows - 8 :]
    doc_rows[8 : 8 + SLAB, :] = column(docs[0:1, 0:rows])[0:SLAB]
    kv_rows[0:8, :] = tail[0:SLAB, :].astype(F32)[SLAB - 8 :]
    kv_rows[8 : 8 + SLAB, :] = raw[0:SLAB, :].astype(F32)
    here = doc_rows[8 : 8 + SLAB, :]
    masks = [(doc_rows[8 - k : 8 - k + SLAB, :] == here).astype(F32) for k in range(tap_count)]
    for at in range(0, raw.shape[1], LANES):
        cols = slice(at, at + LANES)
        total = kv_rows[8 : 8 + SLAB, cols] * taps[0:1, cols]
        for k in range(1, tap_count):
            total = total + masks[k] * kv_rows[8 - k : 8 - k + SLAB, cols] * taps[k : k + 1, cols]
        out[0:SLAB, cols] = (raw[SLAB : 2 * SLAB, cols].astype(F32) * total).astype(BF16)
    out[SLAB : 2 * SLAB, :] = tail[SLAB : 2 * SLAB, :]


def strip_kernel(lags, out):
    count, width = lags.shape
    for g in range(count):
        out[g] = pltpu.roll(jnp.broadcast_to(lags[g : g + 1, :], (SLAB, width)), 0, 1, stride=1, stride_axis=0)


def far_kernel(strips, mixed, docs, out, taps, keep, groups):
    rows = docs.shape[1] // 2
    last = jnp.broadcast_to(docs[0:1, 2 * rows - 1 :].astype(F32), (rows, LANES))
    middle = jnp.broadcast_to(docs[0:1, rows - 1 : rows].astype(F32), (rows, LANES))
    summed = middle == last

    @pl.when(pl.program_id(0) == 0)
    def _():
        keep[0:rows, :] = (column(docs[0:1, 0:rows]) == last).astype(BF16)
        keep[rows:, :] = (column(docs[0:1, rows:]) == last).astype(BF16)

    lane_group = lax.broadcasted_iota(jnp.int32, (rows, LANES), 1) // (LANES // groups)
    for tile in range(mixed.shape[1] // LANES):
        cols = slice(tile * LANES, tile * LANES + LANES)
        for g in range(groups):
            for s in range(rows // SLAB):
                at = g * rows + s * SLAB
                lane = rows - SLAB * s
                taps[at : at + SLAB, :] = strips[tile * groups + g, :, lane : lane + 2 * rows]
        result = jnp.dot(taps[...], mixed[:, cols] * keep[...], preferred_element_type=F32)
        total = pick(lane_group, [result[g * rows : g * rows + rows] for g in range(groups)])
        out[:, cols] = jnp.where(summed, total, mixed[rows:, cols].astype(F32)).astype(BF16)


def own_kernel(strips, mixed, head, docs, out, diag, near, tri, keep, groups):
    rows = docs.shape[1] // 2

    @pl.when(pl.program_id(0) == 0)
    def _():
        target = lax.broadcasted_iota(jnp.int32, (rows, rows), 0)
        source = lax.broadcasted_iota(jnp.int32, (rows, rows), 1)
        lead = jnp.broadcast_to(docs[0:1, rows : rows + 1].astype(F32), (rows, rows))
        for b in range(2):
            row = docs[0:1, b * rows : b * rows + rows].astype(F32)
            col = column(row)
            tri[b] = jnp.where((col == jnp.broadcast_to(row, (rows, rows))) & (source <= target), 1.0, 0.0).astype(BF16)
            keep[b] = (col == lead).astype(F32)

    lane_group = lax.broadcasted_iota(jnp.int32, (rows, LANES), 1) // (LANES // groups)
    blank = jnp.zeros((rows, LANES), BF16)
    for tile in range(mixed.shape[1] // LANES):
        cols = slice(tile * LANES, tile * LANES + LANES)
        for g in range(groups):
            for s in range(rows // SLAB):
                at = g * rows + s * SLAB
                slab = slice(s * SLAB, s * SLAB + SLAB)
                lane = 4 * rows - SLAB * s
                both = strips[tile * groups + g, :, lane : lane + 2 * rows]
                near[at : at + SLAB, :] = both[:, 0:rows]
                diag[at : at + SLAB, 0:rows] = both[:, rows:] * tri[0, slab, :]
                diag[at : at + SLAB, rows:] = both[:, rows:] * tri[1, slab, :]
        lower = jnp.concatenate([head[0:SLAB, cols], mixed[SLAB:rows, cols]], 0)
        upper = mixed[rows:, cols]
        paired = jnp.concatenate(
            [jnp.concatenate([lower, blank], 0), jnp.concatenate([blank, upper], 0)], 1
        )
        inner = jnp.dot(diag[...], paired, preferred_element_type=F32)
        cross = jnp.dot(near[...], lower * keep[0].astype(BF16), preferred_element_type=F32)
        out[0:rows, cols] = pick(lane_group, [inner[g * rows : g * rows + rows, 0:LANES] for g in range(groups)])
        out[rows:, cols] = pick(
            lane_group, [inner[g * rows : g * rows + rows, LANES:] for g in range(groups)]
        ) + keep[1] * pick(lane_group, [cross[g * rows : g * rows + rows] for g in range(groups)])


def last_kernel(core, strips, near, fresh, prior, far, docs, own, gate_own, gate_sib, out_own, out_sib,
                taps, keep, target, total, groups):
    rows = docs.shape[1] // 2

    @pl.when(pl.program_id(0) == 0)
    def _():
        first = prior[SLAB : 2 * SLAB, 0 : 2 * rows].astype(F32)[0:1]
        second = fresh[SLAB : 2 * SLAB, 0 : 2 * rows].astype(F32)[0:1]
        end = jnp.broadcast_to(second[:, 2 * rows - 1 :], (rows, LANES))
        summed = jnp.broadcast_to(second[:, rows - 1 : rows], (rows, LANES)) == end
        for b in range(2):
            lead = jnp.broadcast_to(docs[0:1, b * rows : b * rows + 1].astype(F32), (rows, LANES))
            mine = column(docs[0:1, b * rows : b * rows + rows])
            keep[b, 0:rows, :] = ((column(second[:, rows:]) == lead) & ~summed).astype(BF16)
            keep[b, rows : 2 * rows, :] = (column(first[:, 0:rows]) == lead).astype(BF16)
            keep[b, 2 * rows :, :] = (column(first[:, rows:]) == lead).astype(BF16)
            target[b] = (mine == lead).astype(F32)
            if b == 0:
                target[2] = ((mine == end) & summed).astype(F32)

    lane_group = lax.broadcasted_iota(jnp.int32, (rows, LANES), 1) // (LANES // groups)
    blank = jnp.zeros((rows, LANES), BF16)
    for tile in range(near.shape[1] // LANES):
        cols = slice(tile * LANES, tile * LANES + LANES)
        for g in range(groups):
            for s in range(rows // SLAB):
                at = g * rows + s * SLAB
                lane = rows - SLAB * s
                taps[at : at + SLAB, :] = strips[tile * groups + g, :, lane : lane + 4 * rows]
        source = jnp.concatenate([far[:, cols], fresh[0:SLAB, cols], near[SLAB:, cols]], 0)
        paired = jnp.concatenate(
            [
                jnp.concatenate([blank, source * keep[0]], 0),
                jnp.concatenate([source * keep[1], blank], 0),
            ],
            1,
        )
        result = jnp.dot(taps[...], paired, preferred_element_type=F32)
        lower = pick(lane_group, [result[g * rows : g * rows + rows, 0:LANES] for g in range(groups)])
        upper = pick(lane_group, [result[g * rows : g * rows + rows, LANES:] for g in range(groups)])
        total[0:rows, cols] = own[0:rows, cols] + target[0] * lower + target[2] * far[:, cols].astype(F32)
        total[rows:, cols] = own[rows:, cols] + target[1] * upper
    mine = pl.multiple_of(core[0] * rows, rows)
    other = pl.multiple_of((1 - core[0]) * rows, rows)
    out_own[...] = (gate_own[...].astype(F32) * total[pl.ds(mine, rows), :]).astype(BF16)
    out_sib[...] = (gate_sib[...].astype(F32) * total[pl.ds(other, rows), :]).astype(BF16)


def body(gate_short, key_short, value_short, gate_long, doc_ids, se_filter, long_filter):
    rows, chans = gate_short.shape
    tap_count, filters = se_filter.shape
    reach = long_filter.shape[1]
    count = lax.axis_size("ctx")
    half, quarter = chans // 2, chans // 4
    group_width = chans // filters
    groups = LANES // group_width
    block = quarter // 2
    steps = half // block
    core = lax.rem(lax.axis_index("ctx"), 2)
    odd_chip = lax.rem(lax.axis_index("ctx") // 2, 2)
    core_arg = core.astype(jnp.int32).reshape(1)

    swap = [(i, i ^ 1) for i in range(count)]
    ahead = [(i, i + 2) for i in range(count - 2)]
    ahead_two = [(i, i + 4) for i in range(count - 4)]
    odd_ahead = [(i, i + 4) for i in range(count - 4) if (i // 2) % 2 == 1]
    pair = [(i, i ^ 2) for i in range(count)]

    def send(value, links):
        return lax.ppermute(value, "ctx", links)

    def full(shape):
        return pl.BlockSpec(shape, lambda i, *_: (0,) * len(shape))

    packed = pl.pallas_call(
        pack_kernel,
        grid_spec=pltpu.PrefetchScalarGridSpec(
            num_scalar_prefetch=1,
            grid=(steps,),
            in_specs=[pl.BlockSpec((rows, block), lambda i, c: (0, (1 - c[0]) * steps + i))] * 3,
            out_specs=pl.BlockSpec((2, rows, block), lambda i, c: (0, 0, i)),
        ),
        out_shape=jax.ShapeDtypeStruct((2, rows, half), BF16),
        compiler_params=params(),
        name="pack",
    )(core_arg, key_short, value_short, gate_short)
    sibling = send(packed, swap)
    docs_own = doc_ids.reshape(1, rows)
    docs_sib = send(docs_own, swap)
    docs = jnp.where(core == 0, jnp.concatenate([docs_own, docs_sib], 1), jnp.concatenate([docs_sib, docs_own], 1))

    wide_taps = jnp.repeat(
        lax.dynamic_slice_in_dim(se_filter, core * (filters // 2), filters // 2, 1), group_width, axis=1
    )
    half_filter = lax.dynamic_slice_in_dim(long_filter, core * (filters // 2), filters // 2, 0)
    lags = jnp.pad(jnp.flip(half_filter, 1), ((0, 0), (rows + 1, rows - 1)))
    strip_block = filters // 4
    strips = pl.pallas_call(
        strip_kernel,
        grid=(2,),
        in_specs=[pl.BlockSpec((strip_block, reach + 2 * rows), lambda i: (i, 0))],
        out_specs=pl.BlockSpec((strip_block, SLAB, reach + 2 * rows), lambda i: (i, 0, 0)),
        out_shape=jax.ShapeDtypeStruct((filters // 2, SLAB, reach + 2 * rows), BF16),
        compiler_params=params(),
        name="strips",
    )(lags)

    mine = pl.BlockSpec((rows, block), lambda i, c: (0, c[0] * steps + i))
    mixed, mixed_a, mixed_b, tail, raw_head = pl.pallas_call(
        short_kernel,
        grid_spec=pltpu.PrefetchScalarGridSpec(
            num_scalar_prefetch=1,
            grid=(steps,),
            in_specs=[
                full((1, rows)),
                full((1, rows)),
                mine,
                mine,
                mine,
                pl.BlockSpec((2, rows, block), lambda i, c: (0, 0, i)),
                pl.BlockSpec((tap_count, block), lambda i, c: (0, i)),
            ],
            out_specs=[
                pl.BlockSpec((2 * rows, block), lambda i, c: (0, i)),
                pl.BlockSpec((2 * rows, block), lambda i, c: (0, jnp.minimum(i, steps // 2 - 1))),
                pl.BlockSpec((2 * rows, block), lambda i, c: (0, jnp.maximum(i - steps // 2, 0))),
                pl.BlockSpec((2 * SLAB, block), lambda i, c: (0, i)),
                pl.BlockSpec((2 * SLAB, block), lambda i, c: (0, i)),
            ],
            scratch_shapes=[
                pltpu.VMEM((8 + 2 * rows, block), F32),
                pltpu.VMEM((2 * rows, block), F32),
                pltpu.VMEM((tap_count, 2 * rows, LANES), F32),
                pltpu.VMEM((8 + 2 * rows, LANES), F32),
            ],
        ),
        out_shape=[
            jax.ShapeDtypeStruct((2 * rows, half), BF16),
            jax.ShapeDtypeStruct((2 * rows, quarter), BF16),
            jax.ShapeDtypeStruct((2 * rows, quarter), BF16),
            jax.ShapeDtypeStruct((2 * SLAB, half), BF16),
            jax.ShapeDtypeStruct((2 * SLAB, half), BF16),
        ],
        compiler_params=params(),
        name="short",
    )(core_arg, docs_own, docs_sib, key_short, value_short, gate_short, sibling, wide_taps)

    relayed = send(mixed_a, odd_ahead)
    near_b = send(mixed_b, ahead)
    prior = send(tail, ahead)

    strip_spec = pl.BlockSpec((block // group_width, SLAB, reach + 2 * rows), lambda i, *_: (i, 0, 0))
    far_packet = pl.pallas_call(
        functools.partial(far_kernel, groups=groups),
        grid=(steps,),
        in_specs=[strip_spec, pl.BlockSpec((2 * rows, block), lambda i: (0, i)), full((1, 2 * rows))],
        out_specs=pl.BlockSpec((rows, block), lambda i: (0, i)),
        out_shape=jax.ShapeDtypeStruct((rows, half), BF16),
        scratch_shapes=[
            pltpu.VMEM((groups * rows, 2 * rows), BF16),
            pltpu.VMEM((2 * rows, LANES), BF16),
        ],
        compiler_params=params(),
        name="far",
    )(strips, mixed, docs)
    far = send(far_packet, ahead_two)

    head = pl.pallas_call(
        head_kernel,
        out_shape=jax.ShapeDtypeStruct((2 * SLAB, half), BF16),
        scratch_shapes=[pltpu.VMEM((8 + SLAB, half), F32), pltpu.VMEM((8 + SLAB, LANES), F32)],
        compiler_params=params(),
        name="head",
    )(prior, raw_head, docs, wide_taps)
    fresh = send(head, ahead)

    near_a = send(jnp.where(odd_chip == 1, relayed, mixed_a), pair)

    own = pl.pallas_call(
        functools.partial(own_kernel, groups=groups),
        grid=(steps,),
        in_specs=[
            strip_spec,
            pl.BlockSpec((2 * rows, block), lambda i: (0, i)),
            pl.BlockSpec((2 * SLAB, block), lambda i: (0, i)),
            full((1, 2 * rows)),
        ],
        out_specs=pl.BlockSpec((2 * rows, block), lambda i: (0, i)),
        out_shape=jax.ShapeDtypeStruct((2 * rows, half), F32),
        scratch_shapes=[
            pltpu.VMEM((groups * rows, 2 * rows), BF16),
            pltpu.VMEM((groups * rows, rows), BF16),
            pltpu.VMEM((2, rows, rows), BF16),
            pltpu.VMEM((2, rows, LANES), F32),
        ],
        compiler_params=params(),
        name="own",
    )(strips, mixed, head, docs)

    gate_sib = send(lax.dynamic_slice_in_dim(gate_long, (1 - core) * half, half, 1), swap)

    def finish(part, near):
        skip = part * (steps // 2)
        return pl.pallas_call(
            functools.partial(last_kernel, groups=groups),
            grid_spec=pltpu.PrefetchScalarGridSpec(
                num_scalar_prefetch=1,
                grid=(steps // 2,),
                in_specs=[
                    pl.BlockSpec((block // group_width, SLAB, reach + 2 * rows), lambda i, c: (i + skip, 0, 0)),
                    pl.BlockSpec((2 * rows, block), lambda i, c: (0, i)),
                    pl.BlockSpec((2 * SLAB, block), lambda i, c: (0, i + skip)),
                    full((2 * SLAB, 2 * rows)),
                    pl.BlockSpec((rows, block), lambda i, c: (0, i + skip)),
                    full((1, 2 * rows)),
                    pl.BlockSpec((2 * rows, block), lambda i, c: (0, i + skip)),
                    pl.BlockSpec((rows, block), lambda i, c: (0, c[0] * steps + i + skip)),
                    pl.BlockSpec((rows, block), lambda i, c: (0, i + skip)),
                ],
                out_specs=[pl.BlockSpec((rows, block), lambda i, c: (0, i))] * 2,
                scratch_shapes=[
                    pltpu.VMEM((groups * rows, 4 * rows), BF16),
                    pltpu.VMEM((2, 3 * rows, LANES), BF16),
                    pltpu.VMEM((3, rows, LANES), F32),
                    pltpu.VMEM((2 * rows, block), F32),
                ],
            ),
            out_shape=[jax.ShapeDtypeStruct((rows, quarter), BF16)] * 2,
            compiler_params=params(),
            name="last",
        )(core_arg, strips, near, fresh, prior, far, docs, own, gate_long, gate_sib)

    own_b, sib_b = finish(1, near_b)
    got_b = send(sib_b, swap)
    own_a, sib_a = finish(0, near_a)
    got_a = send(sib_a, swap)
    return jnp.where(
        core == 0,
        jnp.concatenate([own_a, own_b, got_a, got_b], 1),
        jnp.concatenate([got_a, got_b, own_a, own_b], 1),
    )


def solution(mesh):
    placed = (
        P(("groups", "ctx"), None),
        P(("groups", "ctx"), None),
        P(("groups", "ctx"), None),
        P(("groups", "ctx"), None),
        P(("groups", "ctx")),
        P(),
        P(),
    )
    return jax.shard_map(
        body, mesh=mesh, in_specs=placed, out_specs=P(("groups", "ctx"), None), check_vma=False
    )
```

time: 474 us -> 89.6 us (0.19)
  local copies, waits for them, and re-layouts: 391 us -> 11.1 us
  Pallas kernels: 0 us -> 30 us
  matrix products: 26.3 us -> 0 us
  waiting for transfers between devices: 9.52 us -> 23.7 us
  starting transfers between devices: 34.2 us -> 21.6 us
  other arithmetic: 11.1 us -> 2.34 us
    gather x4 -> x0, local copies, waits for them, and re-layouts: 380 us -> none  [the longest x2 303 us: body(): far_taps = jnp.take(padded_filter, far_lag, axis=1)]
    pallas_call x0 -> x8, Pallas kernels: none -> 30 us  [the longest x2 9.7 us: finish(): pl.pallas_call(functools.partial(last_kernel, groups=groups), grid_spec=p...]
    dot_general x2 -> x0, matrix products: 26.3 us -> none  [the longest x1 17.1 us: tile_product(): jnp.einsum('gtp,gkip->gkit', far_taps, gathered, preferred_element_type=j...]
    ppermute x8 -> x11, waiting for transfers between devices: 9.52 us -> 23.7 us  [send(): return lax.ppermute(value, 'ctx', links)]
    ppermute x8 -> x11, starting transfers between devices: 34.2 us -> 21.6 us  [send(): return lax.ppermute(value, 'ctx', links)]
    convert_element_type x4 -> x0, other arithmetic: 9.12 us -> none  [the longest x1 7.56 us: body(): mixed = (gate_short.astype(jnp.float32) * short_mix).astype(jnp.bfloat16)]
    unnamed x25 -> x40, local copies, waits for them, and re-layouts: 4.29 us -> 9.26 us
  transfers between devices with their start and end apart: 8 -> 11, of which waited for: 1 -> 4; matrix products, arithmetic and copies ran while one was open for 84% -> 3% of each run, Pallas kernels for 0% -> 25%
where the time goes in v1:
time: 89.6 us; the launch traced here: 89.1 us
  Pallas kernels  30 us (33%)
  waiting for transfers between devices  23.7 us (26%)
  starting transfers between devices  21.6 us (24%)
  local copies, waits for them, and re-layouts  11.1 us (12%)
  other arithmetic  2.34 us (3%)
    ppermute x11, waiting for transfers between devices, send(): return lax.ppermute(value, 'ctx', links)  23.7 us
    ppermute x11, starting transfers between devices, send(): return lax.ppermute(value, 'ctx', links)  21.6 us
    pallas_call x2, Pallas kernels, finish(): pl.pallas_call(functools.partial(last_kernel, groups=groups), grid_spec=p...  9.7 us
    unnamed x40, local copies, waits for them, and re-layouts  9.26 us
    pallas_call x1, Pallas kernels, body(): pl.pallas_call(functools.partial(own_kernel, groups=groups), grid=(steps,...  6.26 us
    pallas_call x1, Pallas kernels, body(): pl.pallas_call(short_kernel, grid_spec=pltpu.PrefetchScalarGridSpec(num_s...  6.04 us
    pallas_call x1, Pallas kernels, body(): pl.pallas_call(functools.partial(far_kernel, groups=groups), grid=(steps,...  5.09 us
  transfers between devices with their start and end apart: 11, of which 4 were waited for; matrix products, arithmetic and copies ran while one was open for 3% of the time, Pallas kernels for 25%

profile of v1, /device:TPU:0, one launch (start us, length us, event | category | flops | bytes accessed | tf_op | source)
XLA Modules:
  0.0 89.1 jit_solution(9860741908078963101)
XLA Ops:
  0.0 1.3 %copy-done.3 = bf16[128,4096]{1,0:T(8,128)(2,1)S(1)} copy-done((bf16[128,4096]{1,0:T(8,128)(2,1)S(1)}, bf16[128,4096]{1,0:T(8,128)(2,1)}, u32[]{:S(2)}) %copy-start.3) | copy-done | bytes 1048600
  1.3 1.2 %copy-done.5 = bf16[128,4096]{1,0:T(8,128)(2,1)S(1)} copy-done((bf16[128,4096]{1,0:T(8,128)(2,1)S(1)}, bf16[128,4096]{1,0:T(8,128)(2,1)}, u32[]{:S(2)}) %copy-start.5) | copy-done | bytes 1048600
  2.5 1.2 %copy-done.7 = bf16[128,4096]{1,0:T(8,128)(2,1)S(1)} copy-done((bf16[128,4096]{1,0:T(8,128)(2,1)S(1)}, bf16[128,4096]{1,0:T(8,128)(2,1)}, u32[]{:S(2)}) %copy-start.7) | copy-done | bytes 1048600
  3.7 1.7 %pack.1 = bf16[2,128,2048]{2,1,0:T(8,128)(2,1)} custom-call(s32[1]{0:T(128)} %bitcast.core, bf16[128,4096]{1,0:T(8,128)(2,1)S(1)} %copy-done.3, bf16[128,4096]{1,0:T(8,128)(2,1)S(1)} %copy-done.5, bf16[128,4096]{1,0:T(8,128)(2,1)S(1)} %copy-done.7), custom_call_target="tpu_custom_call" | custom-call | tf_op jit(solution)/shard_map/pack/pallas_call | solution.py:250
  5.5 0.5 collective-permute-start.1
  5.9 0.1 collective-permute-start
  6.0 0.2 broadcast_in_dim.3
  6.2 0.3 reshape.71.taps
  6.4 0.0 copy-start.1
  6.4 1.7 %collective-permute-done.docs_sib = s32[1,128]{1,0:T(1,128)S(1)} collective-permute-done((s32[1,128]{1,0:T(1,128)S(1)}, s32[1,128]{1,0:T(1,128)S(1)}, u32[]{:S(2)}, u32[]{:S(2)}) %collective-permute-start) | collective-permute-done | bytes 544 | tf_op jit(solution)/shard_map/ppermute | solution.py:245
  8.1 0.5 collective-permute-done.1.sib
  8.5 1.2 %copy-done.8 = bf16[128,4096]{1,0:T(8,128)(2,1)S(1)} copy-done((bf16[128,4096]{1,0:T(8,128)(2,1)S(1)}, bf16[128,4096]{1,0:T(8,128)(2,1)}, u32[]{:S(2)}) %copy-start.8) | copy-done | bytes 1048600
  9.8 6.0 %short.1 = (bf16[256,2048]{1,0:T(8,128)(2,1)S(1)}, bf16[256,1024]{1,0:T(8,128)(2,1)}, bf16[256,1024]{1,0:T(8,128)(2,1)S(1)}, bf16[32,2048]{1,0:T(8,128)(2,1)S(1)}, bf16[32,2048]{1,0:T(8,128)(2,1)S(1)}) custom-call(s32[1]{0:T(128)} %bitcast.core, s32[1,128]{1,0:T(1,128)S(1)} %bitcast.3, s32[1,128]{1,0:T(1,128)S(1)} %collective-permute-done.docs_sib, ...), custom_call_target="tpu_custom_call" | custom-call | tf_op jit(solution)/shard_map/short/pallas_call | solution.py:284
  15.8 1.0 %copy-done.9 = bf16[256,2048]{1,0:T(8,128)(2,1)} copy-done((bf16[256,2048]{1,0:T(8,128)(2,1)}, bf16[256,2048]{1,0:T(8,128)(2,1)S(1)}, u32[]{:S(2)}) %copy-start.9) | copy-done | bytes 1048600
  16.8 0.6 copy-done.12
  17.4 0.8 copy-done.15
  18.2 0.6 copy-done.17
  18.9 1.5 %collective-permute-start.2 = (bf16[256,1024]{1,0:T(8,128)(2,1)}, bf16[256,1024]{1,0:T(8,128)(2,1)}, u32[]{:S(2)}, u32[]{:S(2)}) collective-permute-start(bf16[256,1024]{1,0:T(8,128)(2,1)} %get-tuple-element.14), channel_id=1, source_target_pairs={{2,6},{3,7},{6,10},{7,11},{10,14},{11,15},{18,22},{19,23},{22,26},... | collective-permute-start | bytes 1572872 | tf_op jit(solution)/shard_map/ppermute | solution.py:245
  20.3 0.8 constant_dynamic-slice_fusion
  21.2 0.4 collective-permute-start.7
  21.6 0.4 rev.4
  22.0 0.1 pad.4.lags
  22.1 1.0 %strips.1 = bf16[128,16,768]{2,1,0:T(8,128)(2,1)S(1)} custom-call(bf16[128,768]{1,0:T(8,128)(2,1)S(1)} %pad.4.lags), custom_call_target="tpu_custom_call" | custom-call | tf_op jit(solution)/shard_map/strips/pallas_call | solution.py:273
  23.1 0.0 copy-start.10
  23.2 1.2 %copy-done.10 = bf16[256,2048]{1,0:T(8,128)(2,1)S(1)} copy-done((bf16[256,2048]{1,0:T(8,128)(2,1)S(1)}, bf16[256,2048]{1,0:T(8,128)(2,1)}, u32[]{:S(2)}) %copy-start.10) | copy-done | bytes 1048600
  24.4 5.1 %far.1 = bf16[128,2048]{1,0:T(8,128)(2,1)S(1)} custom-call(bf16[128,16,768]{2,1,0:T(8,128)(2,1)S(1)} %strips.1, bf16[256,2048]{1,0:T(8,128)(2,1)S(1)} %copy-done.10, s32[1,256]{1,0:T(1,128)S(1)} %broadcast_select_fusion.1.docs), custom_call_target="tpu_custom_call" | custom-call | tf_op jit(solution)/shard_map/far/pallas_call | solution.py:328
  29.5 0.0 copy-start.11
  29.5 4.8 %collective-permute-start.6 = (bf16[128,2048]{1,0:T(8,128)(2,1)S(1)}, bf16[128,2048]{1,0:T(8,128)(2,1)S(1)}, u32[]{:S(2)}, u32[]{:S(2)}) collective-permute-start(bf16[128,2048]{1,0:T(8,128)(2,1)S(1)} %far.1), channel_id=1, source_target_pairs={{0,4},{1,5},{2,6},{3,7},{4,8},{5,9},{6,10},{7,11},{8,12},{9,13},{1... | collective-permute-start | bytes 1572872 | tf_op jit(solution)/shard_map/ppermute | solution.py:245
  34.3 5.3 %collective-permute-start.8 = (bf16[256,1024]{1,0:T(8,128)(2,1)S(1)}, bf16[256,1024]{1,0:T(8,128)(2,1)S(1)}, u32[]{:S(2)}, u32[]{:S(2)}) collective-permute-start(bf16[256,1024]{1,0:T(8,128)(2,1)S(1)} %copy-done.16), channel_id=1, source_target_pairs={{0,2},{1,3},{2,4},{3,5},{4,6},{5,7},{6,8},{7,9},{8,10},{9,11},{10,... | collective-permute-start | bytes 1572872 | tf_op jit(solution)/shard_map/ppermute | solution.py:245
  39.7 1.1 %broadcast_select_fusion = bf16[256,1024]{1,0:T(8,128)(2,1)S(1)} fusion(bf16[256,1024]{1,0:T(8,128)(2,1)} %collective-permute-done.2, bf16[256,1024]{1,0:T(8,128)(2,1)} %get-tuple-element.14, pred[]{:T(512)S(6)} %eq.8), kind=kLoop, calls=%fused_computation.1 | loop fusion | flops 262144 | bytes 1572865 | tf_op jit(solution)/shard_map/jit(_where)/select_n | solution.py:352
  40.8 0.1 collective-permute-start.3
  40.9 3.9 %collective-permute-start.4 = (bf16[32,2048]{1,0:T(8,128)(2,1)S(1)}, bf16[32,2048]{1,0:T(8,128)(2,1)S(1)}, u32[]{:S(2)}, u32[]{:S(2)}) collective-permute-start(bf16[32,2048]{1,0:T(8,128)(2,1)S(1)} %copy-done.18), channel_id=1, source_target_pairs={{0,2},{1,3},{2,4},{3,5},{4,6},{5,7},{6,8},{7,9},{8,10},{9,11},{10,... | collective-permute-start | bytes 393224 | tf_op jit(solution)/shard_map/ppermute | solution.py:245
  44.8 20.4 %collective-permute-done.4.tail.prior = bf16[32,2048]{1,0:T(8,128)(2,1)S(1)} collective-permute-done((bf16[32,2048]{1,0:T(8,128)(2,1)S(1)}, bf16[32,2048]{1,0:T(8,128)(2,1)S(1)}, u32[]{:S(2)}, u32[]{:S(2)}) %collective-permute-start.4) | collective-permute-done | bytes 131104 | tf_op jit(solution)/shard_map/ppermute | solution.py:245
  65.2 0.2 head.1
  65.5 0.0 copy-start.2
  65.5 4.5 %collective-permute-start.5 = (bf16[32,2048]{1,0:T(8,128)(2,1)S(1)}, bf16[32,2048]{1,0:T(8,128)(2,1)S(1)}, u32[]{:S(2)}, u32[]{:S(2)}) collective-permute-start(bf16[32,2048]{1,0:T(8,128)(2,1)S(1)} %head.1), channel_id=1, source_target_pairs={{0,2},{1,3},{2,4},{3,5},{4,6},{5,7},{6,8},{7,9},{8,10},{9,11},{10,... | collective-permute-start | bytes 393224 | tf_op jit(solution)/shard_map/ppermute | solution.py:245
  70.0 6.3 %own.1 = f32[256,2048]{1,0:T(8,128)S(1)} custom-call(bf16[128,16,768]{2,1,0:T(8,128)(2,1)S(1)} %strips.1, bf16[256,2048]{1,0:T(8,128)(2,1)S(1)} %copy-done.11, bf16[32,2048]{1,0:T(8,128)(2,1)S(1)} %head.1, s32[1,256]{1,0:T(1,128)S(1)} %broadcast_select_fusion.1.docs), custom_call_target="tpu_custom_call" | custom-call | tf_op jit(solution)/shard_map/own/pallas_call | solution.py:354
  76.3 0.0 collective-permute-done.7.gate_sib
  76.3 0.0 collective-permute-done.6.far
  76.3 0.0 collective-permute-done.8.near
  76.3 4.9 %last.3 = (bf16[128,1024]{1,0:T(8,128)(2,1)S(1)}, bf16[128,1024]{1,0:T(8,128)(2,1)S(1)}) custom-call(s32[1]{0:T(128)} %bitcast.core, bf16[128,16,768]{2,1,0:T(8,128)(2,1)S(1)} %strips.1, bf16[256,1024]{1,0:T(8,128)(2,1)S(1)} %collective-permute-done.8.near, bf16[32,2048]{1,0:T(8,128)(2,1)S(1)} %collective-permute-done.5.fresh, ...), custom_call_target="tpu_custom_call" | custom-call | tf_op jit(solution)/shard_map/last/pallas_call | solution.py:379
  81.2 0.1 collective-permute-start.10
  81.3 0.0 collective-permute-done.3.near
  81.3 4.8 %last.2 = (bf16[128,1024]{1,0:T(8,128)(2,1)S(1)}, bf16[128,1024]{1,0:T(8,128)(2,1)S(1)}) custom-call(s32[1]{0:T(128)} %bitcast.core, bf16[128,16,768]{2,1,0:T(8,128)(2,1)S(1)} %strips.1, bf16[256,1024]{1,0:T(8,128)(2,1)S(1)} %collective-permute-done.3.near, bf16[32,2048]{1,0:T(8,128)(2,1)S(1)} %collective-permute-done.5.fresh, ...), custom_call_target="tpu_custom_call" | custom-call | tf_op jit(solution)/shard_map/last/pallas_call | solution.py:379
  86.1 0.5 collective-permute-start.9
  86.7 0.0 collective-permute-done.10
  86.7 1.2 %collective-permute-done.9 = bf16[128,1024]{1,0:T(8,128)(2,1)S(1)} collective-permute-done((bf16[128,1024]{1,0:T(8,128)(2,1)S(1)}, bf16[128,1024]{1,0:T(8,128)(2,1)S(1)}, u32[]{:S(2)}, u32[]{:S(2)}) %collective-permute-start.9) | collective-permute-done | bytes 262176 | tf_op jit(solution)/shard_map/ppermute | solution.py:245
  87.8 1.2 %maximum_select_fusion = bf16[128,4096]{1,0:T(8,128)(2,1)} fusion(bf16[128,1024]{1,0:T(8,128)(2,1)S(1)} %collective-permute-done.10, bf16[128,1024]{1,0:T(8,128)(2,1)S(1)} %collective-permute-done.9, bf16[128,1024]{1,0:T(8,128)(2,1)S(1)} %get-tuple-element.20, bf16[128,1024]{1,0:T(8,128)(2,1)S(1)} %get-tuple-element.18, pred[]{:T(512)S(6)} %eq.7), kind=kLoop, calls=%fused_computation | loop fusion | flops 8912896 | bytes 2097153 | tf_op jit(solution)/shard_map/jit(_where)/select_n | solution.py:412
  (32 shorter events, 0.1 us)
Async XLA Ops:
  0.0 21.6 %copy-start = (bf16[256,512]{1,0:T(8,128)(2,1)S(1)}, bf16[256,512]{1,0:T(8,128)(2,1)}, u32[]{:S(2)}) copy-start(bf16[256,512]{1,0:T(8,128)(2,1)} %param.13) | copy-start | bytes 786436
  0.0 1.3 %copy-start.3 = (bf16[128,4096]{1,0:T(8,128)(2,1)S(1)}, bf16[128,4096]{1,0:T(8,128)(2,1)}, u32[]{:S(2)}) copy-start(bf16[128,4096]{1,0:T(8,128)(2,1)} %key.3) | copy-start | bytes 3145732
  1.3 1.2 %copy-start.5 = (bf16[128,4096]{1,0:T(8,128)(2,1)S(1)}, bf16[128,4096]{1,0:T(8,128)(2,1)}, u32[]{:S(2)}) copy-start(bf16[128,4096]{1,0:T(8,128)(2,1)} %value.3) | copy-start | bytes 3145732
  2.5 1.2 %copy-start.7 = (bf16[128,4096]{1,0:T(8,128)(2,1)S(1)}, bf16[128,4096]{1,0:T(8,128)(2,1)}, u32[]{:S(2)}) copy-start(bf16[128,4096]{1,0:T(8,128)(2,1)} %gate.3) | copy-start | bytes 3145732
  3.7 2.2 %copy-start.14 = (s32[128]{0:T(128)S(1)}, s32[128]{0:T(128)}, u32[]{:S(2)}) copy-start(s32[128]{0:T(128)} %param.11) | copy-start | bytes 1540
  3.7 2.2 %copy-start.19 = (f32[7,256]{1,0:T(8,128)S(1)}, f32[7,256]{1,0:T(8,128)}, u32[]{:S(2)}) copy-start(f32[7,256]{1,0:T(8,128)} %param.12) | copy-start | bytes 21508
  3.7 4.8 %copy-start.4 = (bf16[128,4096]{1,0:T(8,128)(2,1)S(1)}, bf16[128,4096]{1,0:T(8,128)(2,1)}, u32[]{:S(2)}) copy-start(bf16[128,4096]{1,0:T(8,128)(2,1)} %key.3) | copy-start | bytes 3145732
  3.7 4.8 %copy-start.6 = (bf16[128,4096]{1,0:T(8,128)(2,1)S(1)}, bf16[128,4096]{1,0:T(8,128)(2,1)}, u32[]{:S(2)}) copy-start(bf16[128,4096]{1,0:T(8,128)(2,1)} %value.3) | copy-start | bytes 3145732
  5.5 3.1 %collective-permute-start.1 = (bf16[2,128,2048]{2,1,0:T(8,128)(2,1)}, bf16[2,128,2048]{2,1,0:T(8,128)(2,1)}, u32[]{:S(2)}, u32[]{:S(2)}) collective-permute-start(bf16[2,128,2048]{2,1,0:T(8,128)(2,1)} %pack.1), channel_id=1, source_target_pairs={{0,1},{1,0},{2,3},{3,2},{4,5},{5,4},{6,7},{7,6},{8,9},{9,8},{10,11... | collective-permute-start | bytes 3145736 | tf_op jit(solution)/shard_map/ppermute | solution.py:245
  5.9 2.2 %collective-permute-start = (s32[1,128]{1,0:T(1,128)S(1)}, s32[1,128]{1,0:T(1,128)S(1)}, u32[]{:S(2)}, u32[]{:S(2)}) collective-permute-start(s32[1,128]{1,0:T(1,128)S(1)} %bitcast.2), channel_id=1, source_target_pairs={{0,1},{1,0},{2,3},{3,2},{4,5},{5,4},{6,7},{7,6},{8,9},{9,8},{10,11... | collective-permute-start | bytes 1544 | tf_op jit(solution)/shard_map/ppermute | solution.py:245
  6.4 13.9 %copy-start.1 = (bf16[128,4096]{1,0:T(8,128)(2,1)S(1)}, bf16[128,4096]{1,0:T(8,128)(2,1)}, u32[]{:S(2)}) copy-start(bf16[128,4096]{1,0:T(8,128)(2,1)} %gate_own.3) | copy-start | bytes 3145732
  8.5 1.2 %copy-start.8 = (bf16[128,4096]{1,0:T(8,128)(2,1)S(1)}, bf16[128,4096]{1,0:T(8,128)(2,1)}, u32[]{:S(2)}) copy-start(bf16[128,4096]{1,0:T(8,128)(2,1)} %gate.3) | copy-start | bytes 3145732
  15.8 1.0 %copy-start.9 = (bf16[256,2048]{1,0:T(8,128)(2,1)}, bf16[256,2048]{1,0:T(8,128)(2,1)S(1)}, u32[]{:S(2)}) copy-start(bf16[256,2048]{1,0:T(8,128)(2,1)S(1)} %get-tuple-element.17.mixed) | copy-start | bytes 3145732
  16.8 0.6 copy-start.12
  17.4 0.8 copy-start.15
  18.2 0.7 copy-start.17
  18.9 20.8 %collective-permute-start.2 = (bf16[256,1024]{1,0:T(8,128)(2,1)}, bf16[256,1024]{1,0:T(8,128)(2,1)}, u32[]{:S(2)}, u32[]{:S(2)}) collective-permute-start(bf16[256,1024]{1,0:T(8,128)(2,1)} %get-tuple-element.14), channel_id=1, source_target_pairs={{2,6},{3,7},{6,10},{7,11},{10,14},{11,15},{18,22},{19,23},{22,26},... | collective-permute-start | bytes 1572872 | tf_op jit(solution)/shard_map/ppermute | solution.py:245
  21.2 55.1 %collective-permute-start.7 = (bf16[128,2048]{1,0:T(8,128)(2,1)}, bf16[128,2048]{1,0:T(8,128)(2,1)}, u32[]{:S(2)}, u32[]{:S(2)}) collective-permute-start(bf16[128,2048]{1,0:T(8,128)(2,1)} %constant_dynamic-slice_fusion), channel_id=1, source_target_pairs={{0,1},{1,0},{2,3},{3,2},{4,5},{5,4},{6,7},{7,6},{8,9},{9,8},{10,11... | collective-permute-start | bytes 1572872 | tf_op jit(solution)/shard_map/ppermute | solution.py:245
  23.1 1.2 %copy-start.10 = (bf16[256,2048]{1,0:T(8,128)(2,1)S(1)}, bf16[256,2048]{1,0:T(8,128)(2,1)}, u32[]{:S(2)}) copy-start(bf16[256,2048]{1,0:T(8,128)(2,1)} %copy-done.9) | copy-start | bytes 3145732
  24.4 9.9 %copy-start.16 = (bf16[256,1024]{1,0:T(8,128)(2,1)S(1)}, bf16[256,1024]{1,0:T(8,128)(2,1)}, u32[]{:S(2)}) copy-start(bf16[256,1024]{1,0:T(8,128)(2,1)} %copy-done.15) | copy-start | bytes 1572868
  24.4 16.5 %copy-start.18 = (bf16[32,2048]{1,0:T(8,128)(2,1)S(1)}, bf16[32,2048]{1,0:T(8,128)(2,1)}, u32[]{:S(2)}) copy-start(bf16[32,2048]{1,0:T(8,128)(2,1)} %copy-done.17) | copy-start | bytes 393220
  24.4 40.8 %copy-start.13 = (bf16[32,2048]{1,0:T(8,128)(2,1)S(1)}, bf16[32,2048]{1,0:T(8,128)(2,1)}, u32[]{:S(2)}) copy-start(bf16[32,2048]{1,0:T(8,128)(2,1)} %copy-done.12) | copy-start | bytes 393220
  29.5 40.5 %copy-start.11 = (bf16[256,2048]{1,0:T(8,128)(2,1)S(1)}, bf16[256,2048]{1,0:T(8,128)(2,1)}, u32[]{:S(2)}) copy-start(bf16[256,2048]{1,0:T(8,128)(2,1)} %copy-done.9) | copy-start | bytes 3145732
  29.5 46.8 %collective-permute-start.6 = (bf16[128,2048]{1,0:T(8,128)(2,1)S(1)}, bf16[128,2048]{1,0:T(8,128)(2,1)S(1)}, u32[]{:S(2)}, u32[]{:S(2)}) collective-permute-start(bf16[128,2048]{1,0:T(8,128)(2,1)S(1)} %far.1), channel_id=1, source_target_pairs={{0,4},{1,5},{2,6},{3,7},{4,8},{5,9},{6,10},{7,11},{8,12},{9,13},{1... | collective-permute-start | bytes 1572872 | tf_op jit(solution)/shard_map/ppermute | solution.py:245
  34.3 42.0 %collective-permute-start.8 = (bf16[256,1024]{1,0:T(8,128)(2,1)S(1)}, bf16[256,1024]{1,0:T(8,128)(2,1)S(1)}, u32[]{:S(2)}, u32[]{:S(2)}) collective-permute-start(bf16[256,1024]{1,0:T(8,128)(2,1)S(1)} %copy-done.16), channel_id=1, source_target_pairs={{0,2},{1,3},{2,4},{3,5},{4,6},{5,7},{6,8},{7,9},{8,10},{9,11},{10,... | collective-permute-start | bytes 1572872 | tf_op jit(solution)/shard_map/ppermute | solution.py:245
  40.8 40.5 %collective-permute-start.3 = (bf16[256,1024]{1,0:T(8,128)(2,1)S(1)}, bf16[256,1024]{1,0:T(8,128)(2,1)S(1)}, u32[]{:S(2)}, u32[]{:S(2)}) collective-permute-start(bf16[256,1024]{1,0:T(8,128)(2,1)S(1)} %broadcast_select_fusion), channel_id=1, source_target_pairs={{0,2},{1,3},{2,0},{3,1},{4,6},{5,7},{6,4},{7,5},{8,10},{9,11},{10,... | collective-permute-start | bytes 1572872 | tf_op jit(solution)/shard_map/ppermute | solution.py:245
  40.9 24.4 %collective-permute-start.4 = (bf16[32,2048]{1,0:T(8,128)(2,1)S(1)}, bf16[32,2048]{1,0:T(8,128)(2,1)S(1)}, u32[]{:S(2)}, u32[]{:S(2)}) collective-permute-start(bf16[32,2048]{1,0:T(8,128)(2,1)S(1)} %copy-done.18), channel_id=1, source_target_pairs={{0,2},{1,3},{2,4},{3,5},{4,6},{5,7},{6,8},{7,9},{8,10},{9,11},{10,... | collective-permute-start | bytes 393224 | tf_op jit(solution)/shard_map/ppermute | solution.py:245
  65.5 10.9 %copy-start.2 = (bf16[128,4096]{1,0:T(8,128)(2,1)S(1)}, bf16[128,4096]{1,0:T(8,128)(2,1)}, u32[]{:S(2)}) copy-start(bf16[128,4096]{1,0:T(8,128)(2,1)} %gate_own.3) | copy-start | bytes 3145732
  65.5 10.8 %collective-permute-start.5 = (bf16[32,2048]{1,0:T(8,128)(2,1)S(1)}, bf16[32,2048]{1,0:T(8,128)(2,1)S(1)}, u32[]{:S(2)}, u32[]{:S(2)}) collective-permute-start(bf16[32,2048]{1,0:T(8,128)(2,1)S(1)} %head.1), channel_id=1, source_target_pairs={{0,2},{1,3},{2,4},{3,5},{4,6},{5,7},{6,8},{7,9},{8,10},{9,11},{10,... | collective-permute-start | bytes 393224 | tf_op jit(solution)/shard_map/ppermute | solution.py:245
  81.2 5.5 %collective-permute-start.10 = (bf16[128,1024]{1,0:T(8,128)(2,1)S(1)}, bf16[128,1024]{1,0:T(8,128)(2,1)S(1)}, u32[]{:S(2)}, u32[]{:S(2)}) collective-permute-start(bf16[128,1024]{1,0:T(8,128)(2,1)S(1)} %get-tuple-element.22), channel_id=1, source_target_pairs={{0,1},{1,0},{2,3},{3,2},{4,5},{5,4},{6,7},{7,6},{8,9},{9,8},{10,11... | collective-permute-start | bytes 786440 | tf_op jit(solution)/shard_map/ppermute | solution.py:245
  86.1 1.7 %collective-permute-start.9 = (bf16[128,1024]{1,0:T(8,128)(2,1)S(1)}, bf16[128,1024]{1,0:T(8,128)(2,1)S(1)}, u32[]{:S(2)}, u32[]{:S(2)}) collective-permute-start(bf16[128,1024]{1,0:T(8,128)(2,1)S(1)} %get-tuple-element.21), channel_id=1, source_target_pairs={{0,1},{1,0},{2,3},{3,2},{4,5},{5,4},{6,7},{7,6},{8,9},{9,8},{10,11... | collective-permute-start | bytes 786440 | tf_op jit(solution)/shard_map/ppermute | solution.py:245

commit v2 on v0

v2 whole, which is shorter than its diff:
```python
import functools

import jax
import jax.numpy as jnp
from jax import lax
from jax.experimental import pallas as pl
from jax.experimental.pallas import tpu as pltpu
from jax.sharding import PartitionSpec as P

F32 = jnp.float32
BF16 = jnp.bfloat16
SLAB = 16
LANES = 128
LIMIT = 32 * 1024 * 1024
PARTS = 2


def column(row):
    width = row.shape[1]
    return jnp.transpose(jnp.broadcast_to(row.astype(F32), (width, width)))


def pick(parts):
    lane_group = lax.broadcasted_iota(jnp.int32, parts[0].shape, 1) // (LANES // len(parts))
    out = parts[0]
    for index in range(1, len(parts)):
        out = jnp.where(lane_group == index, parts[index], out)
    return out


def widen(short_filter, first, groups):
    taps = short_filter.shape[0]
    lane = lax.broadcasted_iota(jnp.int32, (8, LANES), 1) // (LANES // groups)
    padded = jnp.concatenate([short_filter[...], jnp.zeros((8 - taps, LANES), F32)], 0)
    return jnp.take_along_axis(padded, lane + first, axis=1, mode="promise_in_bounds")


def rim_sum(tail, tail_docs, docs, taps, tap_count):
    line = lax.broadcasted_iota(jnp.int32, (8, LANES), 0)
    total = jnp.zeros((8, LANES), F32)
    for k in range(1, tap_count):
        same = (pltpu.roll(tail_docs, k, 0) == docs) & (line < k)
        total = total + jnp.where(same, pltpu.roll(tail, k, 0), 0.0) * taps[k : k + 1, :]
    return total


def build(taps, strips, tile, groups, rows, width):
    for g in range(groups):
        for s in range(rows // SLAB):
            at = g * rows + s * SLAB
            begin = rows - SLAB * s
            taps[at : at + SLAB, 0:width] = strips[tile * groups + g, :, begin : begin + width]


def pack_kernel(core, key, value, gate, out):
    out[0] = (key[...].astype(F32) * value[...].astype(F32)).astype(BF16)
    out[1] = gate[...]


def copy_kernel(core, source, after, out):
    out[...] = source[...]


def strip_kernel(core, filters, after, out):
    count, reach = filters.shape
    lane = lax.broadcasted_iota(jnp.int32, (count, LANES), 1)
    turned = []
    for at in range(reach - LANES, -1, -LANES):
        piece = filters[:, at : at + LANES].astype(F32)
        turned.append(jnp.take_along_axis(piece, LANES - 1 - lane, axis=1, mode="promise_in_bounds"))
    blank = jnp.zeros((count, LANES), F32)
    lags = jnp.concatenate([blank] + turned + [blank], 1).astype(BF16)
    for g in range(count):
        row = jnp.broadcast_to(lags[g : g + 1, :], (SLAB, lags.shape[1]))
        out[g] = pltpu.roll(row, 1, 1, stride=1, stride_axis=0)


def short_kernel(core, docs_own, docs_sib, key, value, gate, sib, short_filter, packet,
                 kv_rows, gate_rows, agree, doc_rows, groups, first_group):
    step = pl.program_id(0)
    rows, width = key.shape
    tap_count = short_filter.shape[0]
    mine = pl.multiple_of(core[0] * rows, rows)
    other = pl.multiple_of((1 - core[0]) * rows, rows)

    @pl.when(step == 0)
    def _():
        doc_rows[0:8, :] = jnp.full((8, LANES), -1.0, F32)
        doc_rows[pl.ds(8 + mine, rows), :] = column(docs_own[...])
        doc_rows[pl.ds(8 + other, rows), :] = column(docs_sib[...])
        here = doc_rows[8 : 8 + 2 * rows, :]
        for k in range(1, tap_count):
            agree[k] = (doc_rows[8 - k : 8 - k + 2 * rows, :] == here).astype(F32)
        kv_rows[0:8, :] = jnp.zeros((8, width), F32)

    kv_rows[pl.ds(8 + mine, rows), :] = (key[...].astype(F32) * value[...].astype(F32)).astype(BF16).astype(F32)
    kv_rows[pl.ds(8 + other, rows), :] = sib[0].astype(F32)
    gate_rows[pl.ds(mine, rows), :] = gate[...].astype(F32)
    gate_rows[pl.ds(other, rows), :] = sib[1].astype(F32)
    for tile in range(width // LANES):
        cols = slice(tile * LANES, tile * LANES + LANES)
        taps = widen(short_filter, first_group + (step * (width // LANES) + tile) * groups, groups)
        total = kv_rows[8 : 8 + 2 * rows, cols] * taps[0:1]
        for k in range(1, tap_count):
            total = total + agree[k] * kv_rows[8 - k : 8 - k + 2 * rows, cols] * taps[k : k + 1]
        packet[0 : 2 * rows, cols] = (gate_rows[:, cols] * total).astype(BF16)
    first = jnp.where(core[0] == 0, docs_own[...], docs_sib[...]).astype(F32)
    second = jnp.where(core[0] == 0, docs_sib[...], docs_own[...]).astype(F32)
    line = lax.broadcasted_iota(jnp.int32, (8, width), 0)
    doc_line = jnp.concatenate([first, second, jnp.zeros((1, width - 2 * rows), F32)], 1)
    tail = jnp.where(line == 0, jnp.broadcast_to(doc_line, (8, width)), kv_rows[2 * rows : 2 * rows + 8, :])
    packet[2 * rows :, :] = jnp.concatenate([tail, gate_rows[0:8, :]], 0).astype(BF16)


def far_kernel(core, strips, packet, out, taps, keep, groups):
    rows = packet.shape[0] // 2 - SLAB // 2
    docs = packet[2 * rows :, 0 : 2 * rows].astype(F32)[0:1]
    last = jnp.broadcast_to(docs[:, 2 * rows - 1 :], (rows, LANES))
    summed = jnp.broadcast_to(docs[:, rows - 1 : rows], (rows, LANES)) == last

    @pl.when(pl.program_id(0) == 0)
    def _():
        keep[0:rows, :] = (column(docs[:, 0:rows]) == last).astype(BF16)
        keep[rows:, :] = (column(docs[:, rows:]) == last).astype(BF16)

    for tile in range(out.shape[1] // LANES):
        cols = slice(tile * LANES, tile * LANES + LANES)
        build(taps.at[tile], strips, tile, groups, rows, 2 * rows)
        mixed = packet[0 : 2 * rows, cols]
        result = jnp.dot(taps[tile], mixed * keep[...], preferred_element_type=F32)
        total = pick([result[g * rows : g * rows + rows] for g in range(groups)])
        out[0:rows, cols] = jnp.where(summed, total, mixed[rows:].astype(F32)).astype(BF16)
    out[rows:, :] = packet[2 * rows :, :]


def last_kernel(core, strips, packet, near, far, short_filter, gate_own, gate_sib, *refs, groups, first_group):
    out_own, out_sib, taps, diag, tri, keep, target, total, doc_ends = refs[-9:]
    rows = far.shape[0] - SLAB
    tap_count = short_filter.shape[0]
    step = pl.program_id(0)

    @pl.when(step == 0)
    def _():
        position = lax.broadcasted_iota(jnp.int32, (rows, rows), 0)
        source = lax.broadcasted_iota(jnp.int32, (rows, rows), 1)
        docs = packet[2 * rows :, 0 : 2 * rows].astype(F32)[0:1]
        near_docs = near[2 * rows :, 0 : 2 * rows].astype(F32)[0:1]
        far_docs = far[rows:, 0 : 2 * rows].astype(F32)[0:1]
        end = jnp.broadcast_to(far_docs[:, 2 * rows - 1 :], (rows, LANES))
        summed = jnp.broadcast_to(far_docs[:, rows - 1 : rows], (rows, LANES)) == end
        here = [column(docs[:, 0:rows]), column(docs[:, rows:])]
        before = [column(far_docs[:, rows:]), column(near_docs[:, 0:rows]), column(near_docs[:, rows:])]
        for b in range(2):
            row = docs[:, b * rows : b * rows + rows]
            lead = jnp.broadcast_to(row[:, 0:1], (rows, LANES))
            same = here[b] == jnp.broadcast_to(row, (rows, rows))
            tri[b] = jnp.where(same & (source <= position), 1.0, 0.0).astype(BF16)
            keep[b, 0:rows, :] = ((before[0] == lead) & ~summed).astype(BF16)
            keep[b, rows : 2 * rows, :] = (before[1] == lead).astype(BF16)
            keep[b, 2 * rows : 3 * rows, :] = (before[2] == lead).astype(BF16)
            if b == 1:
                keep[b, 3 * rows :, :] = (here[0] == lead).astype(BF16)
            target[b] = (here[b] == lead).astype(F32)
        target[2] = ((here[0] == end) & summed).astype(F32)
        doc_ends[0] = before[2][rows - 8 :]
        doc_ends[1] = here[0][0:8]
        doc_ends[2] = before[0][rows - 8 :]
        doc_ends[3] = before[1][0:8]

    blank = jnp.zeros((rows, LANES), BF16)
    own_rim = packet[2 * rows :, :].astype(F32)
    near_rim = near[2 * rows :, :].astype(F32)
    far_rim = far[rows:, :].astype(F32)
    tiles = far.shape[1] // LANES
    for tile in range(tiles):
        cols = slice(tile * LANES, tile * LANES + LANES)
        scratch = taps.at[tile % taps.shape[0]]
        masked = diag.at[tile % taps.shape[0]]
        build(scratch, strips, tile, groups, rows, 5 * rows)
        for g in range(groups):
            here = slice(g * rows, g * rows + rows)
            masked[here, 0:rows] = scratch[here, 4 * rows :] * tri[0]
            masked[here, rows:] = scratch[here, 4 * rows :] * tri[1]
        short = widen(short_filter, first_group + (step * tiles + tile) * groups, groups)
        added = own_rim[8:, cols] * rim_sum(near_rim[0:8, cols], doc_ends[0], doc_ends[1], short, tap_count)
        lower = packet[0:rows, cols].astype(F32)
        lower = jnp.concatenate([lower[0:8] + added, lower[8:]], 0).astype(BF16)
        upper = packet[rows : 2 * rows, cols]
        added = near_rim[8:, cols] * rim_sum(far_rim[0:8, cols], doc_ends[2], doc_ends[3], short, tap_count)
        behind = near[0 : 2 * rows, cols].astype(F32)
        behind = jnp.concatenate([behind[0:8] + added, behind[8:]], 0).astype(BF16)
        source = jnp.concatenate([far[0:rows, cols], behind], 0)
        paired = jnp.concatenate(
            [jnp.concatenate([lower, blank], 0), jnp.concatenate([blank, upper], 0)], 1
        )
        inner = jnp.dot(masked[...], paired, preferred_element_type=F32)
        paired = jnp.concatenate(
            [
                jnp.concatenate([blank, source * keep[0, 0 : 3 * rows]], 0),
                jnp.concatenate([source, lower], 0) * keep[1],
            ],
            1,
        )
        outer = jnp.dot(scratch[:, 0 : 4 * rows], paired, preferred_element_type=F32)
        for b in range(2):
            side = slice(b * LANES, b * LANES + LANES)
            total[b * rows : b * rows + rows, cols] = pick(
                [inner[g * rows : g * rows + rows, side] for g in range(groups)]
            ) + target[b] * pick([outer[g * rows : g * rows + rows, side] for g in range(groups)])
        total[0:rows, cols] += target[2] * far[0:rows, cols].astype(F32)
    mine = pl.multiple_of(core[0] * rows, rows)
    other = pl.multiple_of((1 - core[0]) * rows, rows)
    out_own[...] = (gate_own[...].astype(F32) * total[pl.ds(mine, rows), :]).astype(BF16)
    out_sib[...] = (gate_sib[...].astype(F32) * total[pl.ds(other, rows), :]).astype(BF16)


def join_kernel(core, got, begun, out):
    out[...] = got[...]


def body(gate_short, key_short, value_short, gate_long, doc_ids, se_filter, long_filter):
    rows, chans = gate_short.shape
    tap_count, filters = se_filter.shape
    reach = long_filter.shape[1]
    count = lax.axis_size("ctx")
    half = chans // 2
    share = half // PARTS
    group_width = chans // filters
    groups = LANES // group_width
    block = share // 2
    steps = share // block
    width = reach + 2 * rows
    core = lax.rem(lax.axis_index("ctx"), 2).astype(jnp.int32).reshape(1)

    swap = [(i, i ^ 1) for i in range(count)]
    ahead = [(i, i + 2) for i in range(count - 2)]
    ahead_two = [(i, i + 4) for i in range(count - 4)]

    def send(value, links):
        return lax.ppermute(value, "ctx", links)

    def shape(*sizes):
        return pltpu.HBM(sizes, BF16)

    def stay(value):
        return pltpu.with_memory_space_constraint(value, pltpu.HBM)

    def whole(sizes):
        return pl.BlockSpec(sizes, lambda i, c: (0,) * len(sizes))

    def mine(height, part):
        return pl.BlockSpec((height, block), lambda i, c: (0, (PARTS * c[0] + part) * steps + i))

    def local(height):
        return pl.BlockSpec((height, block), lambda i, c: (0, i))

    def strip_part(lanes, part):
        return pl.BlockSpec((block // group_width, SLAB, lanes), lambda i, c: (part * steps + i, 0, 0))

    anywhere = pl.BlockSpec(memory_space=pl.ANY)
    short_spec = pl.BlockSpec((tap_count, filters // 2), lambda i, c: (0, c[0]))

    def call(kernel, name, grid, in_specs, out_specs, out_shape, scratch=(), aliases=None):
        return functools.partial(
            pl.pallas_call(
                kernel,
                grid_spec=pltpu.PrefetchScalarGridSpec(
                    num_scalar_prefetch=1, grid=grid, in_specs=in_specs, out_specs=out_specs, scratch_shapes=scratch
                ),
                out_shape=out_shape,
                input_output_aliases=aliases or {},
                compiler_params=pltpu.CompilerParams(vmem_limit_bytes=LIMIT),
                name=name,
            ),
            core,
        )

    gate_short, key_short, value_short, gate_long = map(stay, (gate_short, key_short, value_short, gate_long))
    docs_own = doc_ids.reshape(1, rows)
    docs_sib = send(docs_own, swap)

    def begin(part):
        return send(
            call(
                pack_kernel,
                "pack",
                (steps,),
                [pl.BlockSpec((rows, block), lambda i, c: (0, (PARTS * (1 - c[0]) + part) * steps + i))] * 3,
                pl.BlockSpec((2, rows, block), lambda i, c: (0, 0, i)),
                shape(2, rows, share),
            )(key_short, value_short, gate_short),
            swap,
        )

    def short(part, sibling):
        return call(
            functools.partial(short_kernel, groups=groups, first_group=part * (share // group_width)),
            "short",
            (steps,),
            [
                whole((1, rows)),
                whole((1, rows)),
                mine(rows, part),
                mine(rows, part),
                mine(rows, part),
                pl.BlockSpec((2, rows, block), lambda i, c: (0, 0, i)),
                short_spec,
            ],
            local(2 * rows + SLAB),
            shape(2 * rows + SLAB, share),
            [
                pltpu.VMEM((8 + 2 * rows, block), F32),
                pltpu.VMEM((2 * rows, block), F32),
                pltpu.VMEM((tap_count, 2 * rows, LANES), F32),
                pltpu.VMEM((8 + 2 * rows, LANES), F32),
            ],
        )(docs_own, docs_sib, key_short, value_short, gate_short, sibling, se_filter)

    def far_packet(part, strips, packet):
        return call(
            functools.partial(far_kernel, groups=groups),
            "far",
            (steps,),
            [strip_part(3 * rows, part), local(2 * rows + SLAB)],
            local(rows + SLAB),
            shape(rows + SLAB, share),
            [
                pltpu.VMEM((block // LANES, groups * rows, 2 * rows), BF16),
                pltpu.VMEM((2 * rows, LANES), BF16),
            ],
        )(strips, stay(packet))

    def finish(part, strips, packet, near, far, gate_sib, begun):
        return call(
            functools.partial(last_kernel, groups=groups, first_group=part * (share // group_width)),
            "last",
            (steps,),
            [
                strip_part(width, part),
                local(2 * rows + SLAB),
                local(2 * rows + SLAB),
                local(rows + SLAB),
                short_spec,
                mine(rows, part),
                pl.BlockSpec((rows, block), lambda i, c: (0, part * steps + i)),
            ]
            + [anywhere] * len(begun),
            [mine(rows, part), local(rows)],
            [shape(rows, chans), shape(rows, share)],
            [
                pltpu.VMEM((2, groups * rows, 5 * rows), BF16),
                pltpu.VMEM((2, groups * rows, 2 * rows), BF16),
                pltpu.VMEM((2, rows, rows), BF16),
                pltpu.VMEM((2, 4 * rows, LANES), BF16),
                pltpu.VMEM((3, rows, LANES), F32),
                pltpu.VMEM((2 * rows, block), F32),
                pltpu.VMEM((4, 8, LANES), F32),
            ],
            aliases={8: 0} if begun else None,
        )(strips, stay(packet), near, far, se_filter, gate_long, gate_sib, *begun)

    def join(part, got, begun):
        return call(
            join_kernel,
            "join",
            (steps,),
            [local(rows), anywhere],
            pl.BlockSpec((rows, block), lambda i, c: (0, (PARTS * (1 - c[0]) + part) * steps + i)),
            shape(rows, chans),
            aliases={2: 0},
        )(got, begun)

    siblings = [begin(part) for part in range(PARTS)]
    packets, nears, fars = [], [], []
    for part in range(PARTS):
        packet = short(part, siblings[part])
        nears.append(send(packet, ahead))
        if part == 0:
            strips = call(
                strip_kernel,
                "strips",
                (2,),
                [pl.BlockSpec((filters // 4, reach), lambda i, c: (2 * c[0] + i, 0)), anywhere],
                pl.BlockSpec((filters // 4, SLAB, width), lambda i, c: (i, 0, 0)),
                jax.ShapeDtypeStruct((filters // 2, SLAB, width), BF16),
            )(stay(long_filter), stay(packet))
        beyond = far_packet(part, strips, packet)
        fars.append(send(beyond, ahead_two))
        packets.append(packet)
    gate_sib = send(
        call(
            copy_kernel,
            "gates",
            (2,),
            [pl.BlockSpec((rows, half // 2), lambda i, c: (0, 2 * (1 - c[0]) + i)), anywhere],
            pl.BlockSpec((rows, half // 2), lambda i, c: (0, i)),
            shape(rows, half),
        )(gate_long, stay(beyond)),
        swap,
    )
    begun = ()
    for part in range(PARTS):
        out, other = finish(part, strips, packets[part], nears[part], fars[part], gate_sib, begun)
        begun = (join(part, send(other, swap), out),)
    return begun[0]


def solution(mesh):
    placed = (
        P(("groups", "ctx"), None),
        P(("groups", "ctx"), None),
        P(("groups", "ctx"), None),
        P(("groups", "ctx"), None),
        P(("groups", "ctx")),
        P(),
        P(),
    )
    return jax.shard_map(
        body, mesh=mesh, in_specs=placed, out_specs=P(("groups", "ctx"), None), check_vma=False
    )
```

time: 474 us -> 69.4 us (0.15)
  the two profiles are of different devices: /device:TPU:0 before, /device:TPU:21 now
where the time goes in v2:
time: 69.4 us; the launch traced here: 69 us
  Pallas kernels  39.8 us (57%)
  waiting for transfers between devices  15.7 us (23%)
  starting transfers between devices  13.4 us (19%)
    ppermute x10, waiting for transfers between devices, send(): return lax.ppermute(value, 'ctx', links)  15.7 us
    pallas_call x2, Pallas kernels, finish(): call(functools.partial(last_kernel, groups=groups, first_group=part * (sh...  14.6 us
    ppermute x10, starting transfers between devices, send(): return lax.ppermute(value, 'ctx', links)  13.4 us
    pallas_call x2, Pallas kernels, far_packet(): call(functools.partial(far_kernel, groups=groups), 'far', (steps,), [stri...  8.43 us
    pallas_call x2, Pallas kernels, short(): call(functools.partial(short_kernel, groups=groups, first_group=part * (s...  7.69 us
    pallas_call x2, Pallas kernels, begin(): call(pack_kernel, 'pack', (steps,), [pl.BlockSpec((rows, block), lambda i...  3.94 us
    pallas_call x1, Pallas kernels, body(): call(copy_kernel, 'gates', (2,), [pl.BlockSpec((rows, half // 2), lambda...  1.84 us
    pallas_call x1, Pallas kernels, body(): call(strip_kernel, 'strips', (2,), [pl.BlockSpec((filters // 4, reach), l...  1.74 us
  transfers between devices with their start and end apart: 10, of which 5 were waited for; matrix products, arithmetic and copies ran while one was open for 0% of the time, Pallas kernels for 43%

profile of v2, /device:TPU:21, one launch (start us, length us, event | category | flops | bytes accessed | tf_op | source)
XLA Modules:
  0.0 69.0 jit_solution(8804431387321843965)
XLA Ops:
  0.0 0.0 copy-start.1
  0.0 0.0 copy-start
  0.0 2.0 %pack.2 = bf16[2,128,1024]{2,1,0:T(8,128)(2,1)} custom-call(s32[1]{0:T(128)} %bitcast.core, bf16[128,4096]{1,0:T(8,128)(2,1)} %key.7, bf16[128,4096]{1,0:T(8,128)(2,1)} %value.7, bf16[128,4096]{1,0:T(8,128)(2,1)} %gate.7), custom_call_target="tpu_custom_call" | custom-call | tf_op jit(solution)/shard_map/pack/pallas_call | solution.py:284
  2.0 0.7 collective-permute-start.1
  2.7 2.0 %pack.3 = bf16[2,128,1024]{2,1,0:T(8,128)(2,1)} custom-call(s32[1]{0:T(128)} %bitcast.core, bf16[128,4096]{1,0:T(8,128)(2,1)} %key.7, bf16[128,4096]{1,0:T(8,128)(2,1)} %value.7, bf16[128,4096]{1,0:T(8,128)(2,1)} %gate.7), custom_call_target="tpu_custom_call" | custom-call | tf_op jit(solution)/shard_map/pack/pallas_call | solution.py:284
  4.6 0.0 collective-permute-start.2
  4.7 0.0 copy-done.1
  4.7 0.5 collective-permute-start
  5.1 1.3 %collective-permute-done.docs_sib = s32[1,128]{1,0:T(1,128)S(1)} collective-permute-done((s32[1,128]{1,0:T(1,128)S(1)}, s32[1,128]{1,0:T(1,128)S(1)}, u32[]{:S(2)}, u32[]{:S(2)}) %collective-permute-start) | collective-permute-done | bytes 544 | tf_op jit(solution)/shard_map/ppermute | solution.py:240
  6.5 0.0 collective-permute-done.1.sib
  6.5 0.0 copy-done
  6.5 3.8 %short.2.after.packet = bf16[272,1024]{1,0:T(8,128)(2,1)} custom-call(s32[1]{0:T(128)} %bitcast.core, s32[1,128]{1,0:T(1,128)S(1)} %bitcast.3, s32[1,128]{1,0:T(1,128)S(1)} %collective-permute-done.docs_sib, bf16[128,4096]{1,0:T(8,128)(2,1)} %key.7, bf16[128,4096]{1,0:T(8,128)(2,1)} %value.7, bf16[128,4096]{1,0:T(8,128)(2,1)} %gate.7, ...), custom_call_target="tpu_custom_call" | custom-call | tf_op jit(solution)/shard_map/short/pallas_call | solution.py:296
  10.3 3.1 %collective-permute-start.6 = (bf16[272,1024]{1,0:T(8,128)(2,1)}, bf16[272,1024]{1,0:T(8,128)(2,1)S(1)}, u32[]{:S(2)}, u32[]{:S(2)}) collective-permute-start(bf16[272,1024]{1,0:T(8,128)(2,1)} %short.2.after.packet), channel_id=1, source_target_pairs={{0,2},{1,3},{2,4},{3,5},{4,6},{5,7},{6,8},{7,9},{8,10},{9,11},{10,... | collective-permute-start | bytes 1671176 | tf_op jit(solution)/shard_map/ppermute | solution.py:240
  13.5 1.7 %strips.1 = bf16[128,16,768]{2,1,0:T(8,128)(2,1)S(1)} custom-call(s32[1]{0:T(128)} %bitcast.core, bf16[256,512]{1,0:T(8,128)(2,1)} %filters.1, bf16[272,1024]{1,0:T(8,128)(2,1)} %short.2.after.packet), custom_call_target="tpu_custom_call" | custom-call | tf_op jit(solution)/shard_map/strips/pallas_call | solution.py:379
  15.2 0.0 collective-permute-done.2.sib
  15.2 3.9 %short.3.packet = bf16[272,1024]{1,0:T(8,128)(2,1)} custom-call(s32[1]{0:T(128)} %bitcast.core, s32[1,128]{1,0:T(1,128)S(1)} %bitcast.4, s32[1,128]{1,0:T(1,128)S(1)} %collective-permute-done.docs_sib, bf16[128,4096]{1,0:T(8,128)(2,1)} %key.7, bf16[128,4096]{1,0:T(8,128)(2,1)} %value.7, bf16[128,4096]{1,0:T(8,128)(2,1)} %gate.7, ...), custom_call_target="tpu_custom_call" | custom-call | tf_op jit(solution)/shard_map/short/pallas_call | solution.py:296
  19.1 4.2 %far.2.after = bf16[144,1024]{1,0:T(8,128)(2,1)} custom-call(s32[1]{0:T(128)} %bitcast.core, bf16[128,16,768]{2,1,0:T(8,128)(2,1)S(1)} %strips.1, bf16[272,1024]{1,0:T(8,128)(2,1)} %short.3.packet), custom_call_target="tpu_custom_call" | custom-call | tf_op jit(solution)/shard_map/far/pallas_call | solution.py:320
  23.3 0.0 copy-start.2
  23.3 0.0 copy-start.3
  23.3 1.8 %gates.1 = bf16[128,2048]{1,0:T(8,128)(2,1)} custom-call(s32[1]{0:T(128)} %bitcast.core, bf16[128,4096]{1,0:T(8,128)(2,1)} %gate_own.3, bf16[144,1024]{1,0:T(8,128)(2,1)} %far.2.after), custom_call_target="tpu_custom_call" | custom-call | tf_op jit(solution)/shard_map/gates/pallas_call | solution.py:391
  25.2 0.4 collective-permute-start.5
  25.6 4.2 %far.3 = bf16[144,1024]{1,0:T(8,128)(2,1)} custom-call(s32[1]{0:T(128)} %bitcast.core, bf16[128,16,768]{2,1,0:T(8,128)(2,1)S(1)} %strips.1, bf16[272,1024]{1,0:T(8,128)(2,1)} %short.2.after.packet), custom_call_target="tpu_custom_call" | custom-call | tf_op jit(solution)/shard_map/far/pallas_call | solution.py:320
  29.8 1.9 %collective-permute-start.7 = (bf16[144,1024]{1,0:T(8,128)(2,1)}, bf16[144,1024]{1,0:T(8,128)(2,1)S(1)}, u32[]{:S(2)}, u32[]{:S(2)}) collective-permute-start(bf16[144,1024]{1,0:T(8,128)(2,1)} %far.3), channel_id=1, source_target_pairs={{0,4},{1,5},{2,6},{3,7},{4,8},{5,9},{6,10},{7,11},{8,12},{9,13},{1... | collective-permute-start | bytes 884744 | tf_op jit(solution)/shard_map/ppermute | solution.py:240
  31.7 0.0 copy-done.2
  31.7 2.5 %collective-permute-start.3 = (bf16[272,1024]{1,0:T(8,128)(2,1)S(1)}, bf16[272,1024]{1,0:T(8,128)(2,1)S(1)}, u32[]{:S(2)}, u32[]{:S(2)}) collective-permute-start(bf16[272,1024]{1,0:T(8,128)(2,1)S(1)} %copy-done.2), channel_id=1, source_target_pairs={{0,2},{1,3},{2,4},{3,5},{4,6},{5,7},{6,8},{7,9},{8,10},{9,11},{10,... | collective-permute-start | bytes 1671176 | tf_op jit(solution)/shard_map/ppermute | solution.py:240
  34.3 0.0 copy-done.3
  34.3 2.1 %collective-permute-start.4 = (bf16[144,1024]{1,0:T(8,128)(2,1)S(1)}, bf16[144,1024]{1,0:T(8,128)(2,1)S(1)}, u32[]{:S(2)}, u32[]{:S(2)}) collective-permute-start(bf16[144,1024]{1,0:T(8,128)(2,1)S(1)} %copy-done.3), channel_id=1, source_target_pairs={{0,4},{1,5},{2,6},{3,7},{4,8},{5,9},{6,10},{7,11},{8,12},{9,13},{1... | collective-permute-start | bytes 884744 | tf_op jit(solution)/shard_map/ppermute | solution.py:240
  36.4 4.1 %collective-permute-done.7.far = bf16[144,1024]{1,0:T(8,128)(2,1)S(1)} collective-permute-done((bf16[144,1024]{1,0:T(8,128)(2,1)}, bf16[144,1024]{1,0:T(8,128)(2,1)S(1)}, u32[]{:S(2)}, u32[]{:S(2)}) %collective-permute-start.7) | collective-permute-done | bytes 294944 | tf_op jit(solution)/shard_map/ppermute | solution.py:240
  40.5 0.0 collective-permute-done.5.gate_sib
  40.5 0.0 collective-permute-done.6.near
  40.5 7.3 %last.2 = (bf16[128,4096]{1,0:T(8,128)(2,1)}, bf16[128,1024]{1,0:T(8,128)(2,1)}) custom-call(s32[1]{0:T(128)} %bitcast.core, bf16[128,16,768]{2,1,0:T(8,128)(2,1)S(1)} %strips.1, bf16[272,1024]{1,0:T(8,128)(2,1)} %short.2.after.packet, bf16[272,1024]{1,0:T(8,128)(2,1)S(1)} %collective-permute-done.6.near, bf16[144,1024]{1,0:T(8,128)(2,1)S(1)} %collective-permute-done.7.far, ...), custom_call_target="tpu_custom_call" | custom-call | tf_op jit(solution)/shard_map/last/pallas_call | solution.py:334
  47.8 1.3 %collective-permute-start.8 = (bf16[128,1024]{1,0:T(8,128)(2,1)}, bf16[128,1024]{1,0:T(8,128)(2,1)S(1)}, u32[]{:S(2)}, u32[]{:S(2)}) collective-permute-start(bf16[128,1024]{1,0:T(8,128)(2,1)} %get-tuple-element.9), channel_id=1, source_target_pairs={{0,1},{1,0},{2,3},{3,2},{4,5},{5,4},{6,7},{7,6},{8,9},{9,8},{10,11... | collective-permute-start | bytes 786440 | tf_op jit(solution)/shard_map/ppermute | solution.py:240
  49.1 1.4 %collective-permute-done.8.got = bf16[128,1024]{1,0:T(8,128)(2,1)S(1)} collective-permute-done((bf16[128,1024]{1,0:T(8,128)(2,1)}, bf16[128,1024]{1,0:T(8,128)(2,1)S(1)}, u32[]{:S(2)}, u32[]{:S(2)}) %collective-permute-start.8) | collective-permute-done | bytes 262176 | tf_op jit(solution)/shard_map/ppermute | solution.py:240
  50.5 0.7 %join.2.refs_0_ = bf16[128,4096]{1,0:T(8,128)(2,1)} custom-call(s32[1]{0:T(128)} %bitcast.core, bf16[128,1024]{1,0:T(8,128)(2,1)S(1)} %collective-permute-done.8.got, bf16[128,4096]{1,0:T(8,128)(2,1)} %get-tuple-element.10.begun), custom_call_target="tpu_custom_call", output_to_operand_aliasing={{}: (2, {})} | custom-call | tf_op jit(solution)/shard_map/join/pallas_call | solution.py:363
  51.2 7.5 %collective-permute-done.4.far = bf16[144,1024]{1,0:T(8,128)(2,1)S(1)} collective-permute-done((bf16[144,1024]{1,0:T(8,128)(2,1)S(1)}, bf16[144,1024]{1,0:T(8,128)(2,1)S(1)}, u32[]{:S(2)}, u32[]{:S(2)}) %collective-permute-start.4) | collective-permute-done | bytes 294944 | tf_op jit(solution)/shard_map/ppermute | solution.py:240
  58.7 0.0 collective-permute-done.3.near
  58.7 7.3 %last.3 = (bf16[128,4096]{1,0:T(8,128)(2,1)}, bf16[128,1024]{1,0:T(8,128)(2,1)}) custom-call(s32[1]{0:T(128)} %bitcast.core, bf16[128,16,768]{2,1,0:T(8,128)(2,1)S(1)} %strips.1, bf16[272,1024]{1,0:T(8,128)(2,1)} %short.3.packet, bf16[272,1024]{1,0:T(8,128)(2,1)S(1)} %collective-permute-done.3.near, ...), custom_call_target="tpu_custom_call", output_to_operand_aliasing={{0}: (8, {})} | custom-call | tf_op jit(solution)/shard_map/last/pallas_call | solution.py:334
  66.1 0.8 %collective-permute-start.9 = (bf16[128,1024]{1,0:T(8,128)(2,1)}, bf16[128,1024]{1,0:T(8,128)(2,1)S(1)}, u32[]{:S(2)}, u32[]{:S(2)}) collective-permute-start(bf16[128,1024]{1,0:T(8,128)(2,1)} %get-tuple-element.11), channel_id=1, source_target_pairs={{0,1},{1,0},{2,3},{3,2},{4,5},{5,4},{6,7},{7,6},{8,9},{9,8},{10,11... | collective-permute-start | bytes 786440 | tf_op jit(solution)/shard_map/ppermute | solution.py:240
  66.9 1.4 %collective-permute-done.9.got = bf16[128,1024]{1,0:T(8,128)(2,1)S(1)} collective-permute-done((bf16[128,1024]{1,0:T(8,128)(2,1)}, bf16[128,1024]{1,0:T(8,128)(2,1)S(1)}, u32[]{:S(2)}, u32[]{:S(2)}) %collective-permute-start.9) | collective-permute-done | bytes 262176 | tf_op jit(solution)/shard_map/ppermute | solution.py:240
  68.3 0.7 %join.3 = bf16[128,4096]{1,0:T(8,128)(2,1)} custom-call(s32[1]{0:T(128)} %bitcast.core, bf16[128,1024]{1,0:T(8,128)(2,1)S(1)} %collective-permute-done.9.got, bf16[128,4096]{1,0:T(8,128)(2,1)} %get-tuple-element.12.begun), custom_call_target="tpu_custom_call", output_to_operand_aliasing={{}: (2, {})} | custom-call | tf_op jit(solution)/shard_map/join/pallas_call | solution.py:363
Async XLA Ops:
  0.0 4.7 %copy-start.1 = (s32[128]{0:T(128)S(1)}, s32[128]{0:T(128)}, u32[]{:S(2)}) copy-start(s32[128]{0:T(128)} %param.11) | copy-start | bytes 1540
  0.0 6.5 %copy-start = (f32[7,256]{1,0:T(8,128)S(1)}, f32[7,256]{1,0:T(8,128)}, u32[]{:S(2)}) copy-start(f32[7,256]{1,0:T(8,128)} %short_filter.7) | copy-start | bytes 21508
  2.0 4.5 %collective-permute-start.1 = (bf16[2,128,1024]{2,1,0:T(8,128)(2,1)}, bf16[2,128,1024]{2,1,0:T(8,128)(2,1)S(1)}, u32[]{:S(2)}, u32[]{:S(2)}) collective-permute-start(bf16[2,128,1024]{2,1,0:T(8,128)(2,1)} %pack.2), channel_id=1, source_target_pairs={{0,1},{1,0},{2,3},{3,2},{4,5},{5,4},{6,7},{7,6},{8,9},{9,8},{10,11... | collective-permute-start | bytes 1572872 | tf_op jit(solution)/shard_map/ppermute | solution.py:240
  4.6 10.6 %collective-permute-start.2 = (bf16[2,128,1024]{2,1,0:T(8,128)(2,1)}, bf16[2,128,1024]{2,1,0:T(8,128)(2,1)S(1)}, u32[]{:S(2)}, u32[]{:S(2)}) collective-permute-start(bf16[2,128,1024]{2,1,0:T(8,128)(2,1)} %pack.3), channel_id=1, source_target_pairs={{0,1},{1,0},{2,3},{3,2},{4,5},{5,4},{6,7},{7,6},{8,9},{9,8},{10,11... | collective-permute-start | bytes 1572872 | tf_op jit(solution)/shard_map/ppermute | solution.py:240
  4.7 1.8 %collective-permute-start = (s32[1,128]{1,0:T(1,128)S(1)}, s32[1,128]{1,0:T(1,128)S(1)}, u32[]{:S(2)}, u32[]{:S(2)}) collective-permute-start(s32[1,128]{1,0:T(1,128)S(1)} %bitcast.2), channel_id=1, source_target_pairs={{0,1},{1,0},{2,3},{3,2},{4,5},{5,4},{6,7},{7,6},{8,9},{9,8},{10,11... | collective-permute-start | bytes 1544 | tf_op jit(solution)/shard_map/ppermute | solution.py:240
  10.3 30.2 %collective-permute-start.6 = (bf16[272,1024]{1,0:T(8,128)(2,1)}, bf16[272,1024]{1,0:T(8,128)(2,1)S(1)}, u32[]{:S(2)}, u32[]{:S(2)}) collective-permute-start(bf16[272,1024]{1,0:T(8,128)(2,1)} %short.2.after.packet), channel_id=1, source_target_pairs={{0,2},{1,3},{2,4},{3,5},{4,6},{5,7},{6,8},{7,9},{8,10},{9,11},{10,... | collective-permute-start | bytes 1671176 | tf_op jit(solution)/shard_map/ppermute | solution.py:240
  23.3 8.4 %copy-start.2 = (bf16[272,1024]{1,0:T(8,128)(2,1)S(1)}, bf16[272,1024]{1,0:T(8,128)(2,1)}, u32[]{:S(2)}) copy-start(bf16[272,1024]{1,0:T(8,128)(2,1)} %short.3.packet) | copy-start | bytes 1671172
  23.3 11.0 %copy-start.3 = (bf16[144,1024]{1,0:T(8,128)(2,1)S(1)}, bf16[144,1024]{1,0:T(8,128)(2,1)}, u32[]{:S(2)}) copy-start(bf16[144,1024]{1,0:T(8,128)(2,1)} %far.2.after) | copy-start | bytes 884740
  25.2 15.3 %collective-permute-start.5 = (bf16[128,2048]{1,0:T(8,128)(2,1)}, bf16[128,2048]{1,0:T(8,128)(2,1)S(1)}, u32[]{:S(2)}, u32[]{:S(2)}) collective-permute-start(bf16[128,2048]{1,0:T(8,128)(2,1)} %gates.1), channel_id=1, source_target_pairs={{0,1},{1,0},{2,3},{3,2},{4,5},{5,4},{6,7},{7,6},{8,9},{9,8},{10,11... | collective-permute-start | bytes 1572872 | tf_op jit(solution)/shard_map/ppermute | solution.py:240
  29.8 10.7 %collective-permute-start.7 = (bf16[144,1024]{1,0:T(8,128)(2,1)}, bf16[144,1024]{1,0:T(8,128)(2,1)S(1)}, u32[]{:S(2)}, u32[]{:S(2)}) collective-permute-start(bf16[144,1024]{1,0:T(8,128)(2,1)} %far.3), channel_id=1, source_target_pairs={{0,4},{1,5},{2,6},{3,7},{4,8},{5,9},{6,10},{7,11},{8,12},{9,13},{1... | collective-permute-start | bytes 884744 | tf_op jit(solution)/shard_map/ppermute | solution.py:240
  31.7 27.0 %collective-permute-start.3 = (bf16[272,1024]{1,0:T(8,128)(2,1)S(1)}, bf16[272,1024]{1,0:T(8,128)(2,1)S(1)}, u32[]{:S(2)}, u32[]{:S(2)}) collective-permute-start(bf16[272,1024]{1,0:T(8,128)(2,1)S(1)} %copy-done.2), channel_id=1, source_target_pairs={{0,2},{1,3},{2,4},{3,5},{4,6},{5,7},{6,8},{7,9},{8,10},{9,11},{10,... | collective-permute-start | bytes 1671176 | tf_op jit(solution)/shard_map/ppermute | solution.py:240
  34.3 24.5 %collective-permute-start.4 = (bf16[144,1024]{1,0:T(8,128)(2,1)S(1)}, bf16[144,1024]{1,0:T(8,128)(2,1)S(1)}, u32[]{:S(2)}, u32[]{:S(2)}) collective-permute-start(bf16[144,1024]{1,0:T(8,128)(2,1)S(1)} %copy-done.3), channel_id=1, source_target_pairs={{0,4},{1,5},{2,6},{3,7},{4,8},{5,9},{6,10},{7,11},{8,12},{9,13},{1... | collective-permute-start | bytes 884744 | tf_op jit(solution)/shard_map/ppermute | solution.py:240
  47.8 2.7 %collective-permute-start.8 = (bf16[128,1024]{1,0:T(8,128)(2,1)}, bf16[128,1024]{1,0:T(8,128)(2,1)S(1)}, u32[]{:S(2)}, u32[]{:S(2)}) collective-permute-start(bf16[128,1024]{1,0:T(8,128)(2,1)} %get-tuple-element.9), channel_id=1, source_target_pairs={{0,1},{1,0},{2,3},{3,2},{4,5},{5,4},{6,7},{7,6},{8,9},{9,8},{10,11... | collective-permute-start | bytes 786440 | tf_op jit(solution)/shard_map/ppermute | solution.py:240
  66.1 2.2 %collective-permute-start.9 = (bf16[128,1024]{1,0:T(8,128)(2,1)}, bf16[128,1024]{1,0:T(8,128)(2,1)S(1)}, u32[]{:S(2)}, u32[]{:S(2)}) collective-permute-start(bf16[128,1024]{1,0:T(8,128)(2,1)} %get-tuple-element.11), channel_id=1, source_target_pairs={{0,1},{1,0},{2,3},{3,2},{4,5},{5,4},{6,7},{7,6},{8,9},{9,8},{10,11... | collective-permute-start | bytes 786440 | tf_op jit(solution)/shard_map/ppermute | solution.py:240

commit v3 on v2

v3 whole, which is shorter than its diff:
```python
import functools

import jax
import jax.numpy as jnp
from jax import lax
from jax.experimental import pallas as pl
from jax.experimental.pallas import tpu as pltpu
from jax.sharding import PartitionSpec as P

F32 = jnp.float32
BF16 = jnp.bfloat16
SLAB = 16
LANES = 128
LIMIT = 32 * 1024 * 1024
PARTS = 2
STEPS = 1


def column(row):
    width = row.shape[1]
    return jnp.transpose(jnp.broadcast_to(row.astype(F32), (width, width)))


def pick(parts):
    lane_group = lax.broadcasted_iota(jnp.int32, parts[0].shape, 1) // (LANES // len(parts))
    out = parts[0]
    for index in range(1, len(parts)):
        out = jnp.where(lane_group == index, parts[index], out)
    return out


def widen(short_filter, first, groups):
    taps = short_filter.shape[0]
    lane = lax.broadcasted_iota(jnp.int32, (8, LANES), 1) // (LANES // groups)
    padded = jnp.concatenate([short_filter[...], jnp.zeros((8 - taps, LANES), F32)], 0)
    return jnp.take_along_axis(padded, lane + first, axis=1, mode="promise_in_bounds")


def rim_sum(tail, tail_docs, docs, taps, tap_count):
    line = lax.broadcasted_iota(jnp.int32, (8, LANES), 0)
    total = jnp.zeros((8, LANES), F32)
    for k in range(1, tap_count):
        same = (pltpu.roll(tail_docs, k, 0) == docs) & (line < k)
        total = total + jnp.where(same, pltpu.roll(tail, k, 0), 0.0) * taps[k : k + 1, :]
    return total


def build(taps, strips, tile, groups, rows, width, nearer=0):
    for g in range(groups):
        for s in range(rows // SLAB):
            at = g * rows + s * SLAB
            begin = (1 + nearer) * rows - SLAB * s
            taps[at : at + SLAB, 0:width] = strips[tile * groups + g, :, begin : begin + width]


def pack_kernel(core, key, value, gate, docs, out):
    rows, width = key.shape
    out[0:rows, :] = (key[...].astype(F32) * value[...].astype(F32)).astype(BF16)
    out[rows : 2 * rows, :] = gate[...]
    out[2 * rows :, 0:rows] = jnp.broadcast_to(docs[...].astype(F32), (SLAB, rows)).astype(BF16)
    out[2 * rows :, rows:] = jnp.zeros((SLAB, width - rows), BF16)


def strip_kernel(core, filters, after, out):
    count, reach = filters.shape
    lane = lax.broadcasted_iota(jnp.int32, (count, LANES), 1)
    turned = []
    for at in range(reach - LANES, -1, -LANES):
        piece = filters[:, at : at + LANES].astype(F32)
        turned.append(jnp.take_along_axis(piece, LANES - 1 - lane, axis=1, mode="promise_in_bounds"))
    blank = jnp.zeros((count, LANES), F32)
    lags = jnp.concatenate([blank] + turned + [blank], 1).astype(BF16)
    for g in range(count):
        row = jnp.broadcast_to(lags[g : g + 1, :], (SLAB, lags.shape[1]))
        out[g] = pltpu.roll(row, 1, 1, stride=1, stride_axis=0)


def short_kernel(core, docs, key, value, gate, sib, short_filter, *refs, groups, first_group):
    packet, kv_rows, gate_rows, agree, doc_rows = refs[-5:]
    step = pl.program_id(0)
    rows, width = key.shape
    tap_count = short_filter.shape[0]
    docs_own = docs[...].astype(F32)
    docs_sib = sib[2 * rows :, 0:rows].astype(F32)[0:1]
    mine = pl.multiple_of(core[0] * rows, rows)
    other = pl.multiple_of((1 - core[0]) * rows, rows)

    @pl.when(step == 0)
    def _():
        doc_rows[0:8, :] = jnp.full((8, LANES), -1.0, F32)
        doc_rows[pl.ds(8 + mine, rows), :] = column(docs_own)
        doc_rows[pl.ds(8 + other, rows), :] = column(docs_sib)
        here = doc_rows[8 : 8 + 2 * rows, :]
        for k in range(1, tap_count):
            agree[k] = (doc_rows[8 - k : 8 - k + 2 * rows, :] == here).astype(F32)
        kv_rows[0:8, :] = jnp.zeros((8, width), F32)

    kv_rows[pl.ds(8 + mine, rows), :] = (key[...].astype(F32) * value[...].astype(F32)).astype(BF16).astype(F32)
    kv_rows[pl.ds(8 + other, rows), :] = sib[0:rows, :].astype(F32)
    gate_rows[pl.ds(mine, rows), :] = gate[...].astype(F32)
    gate_rows[pl.ds(other, rows), :] = sib[rows : 2 * rows, :].astype(F32)
    for tile in range(width // LANES):
        cols = slice(tile * LANES, tile * LANES + LANES)
        taps = widen(short_filter, first_group + (step * (width // LANES) + tile) * groups, groups)
        total = kv_rows[8 : 8 + 2 * rows, cols] * taps[0:1]
        for k in range(1, tap_count):
            total = total + agree[k] * kv_rows[8 - k : 8 - k + 2 * rows, cols] * taps[k : k + 1]
        packet[0 : 2 * rows, cols] = (gate_rows[:, cols] * total).astype(BF16)
    first = jnp.where(core[0] == 0, docs_own, docs_sib)
    second = jnp.where(core[0] == 0, docs_sib, docs_own)
    line = lax.broadcasted_iota(jnp.int32, (8, width), 0)
    doc_line = jnp.concatenate([first, second, jnp.zeros((1, width - 2 * rows), F32)], 1)
    tail = jnp.where(line == 0, jnp.broadcast_to(doc_line, (8, width)), kv_rows[2 * rows : 2 * rows + 8, :])
    packet[2 * rows :, :] = jnp.concatenate([tail, gate_rows[0:8, :]], 0).astype(BF16)


def far_kernel(core, strips, packet, *refs, groups):
    out, taps, keep = refs[-3:]
    rows = packet.shape[0] // 2 - SLAB // 2
    docs = packet[2 * rows :, 0 : 2 * rows].astype(F32)[0:1]
    last = jnp.broadcast_to(docs[:, 2 * rows - 1 :], (rows, LANES))
    summed = jnp.broadcast_to(docs[:, rows - 1 : rows], (rows, LANES)) == last

    @pl.when(pl.program_id(0) == 0)
    def _():
        keep[0:rows, :] = (column(docs[:, 0:rows]) == last).astype(BF16)
        keep[rows:, :] = (column(docs[:, rows:]) == last).astype(BF16)

    for tile in range(out.shape[1] // LANES):
        cols = slice(tile * LANES, tile * LANES + LANES)
        build(taps.at[tile], strips, tile, groups, rows, 2 * rows)
        mixed = packet[0 : 2 * rows, cols]
        result = jnp.dot(taps[tile], mixed * keep[...], preferred_element_type=F32)
        total = pick([result[g * rows : g * rows + rows] for g in range(groups)])
        out[0:rows, cols] = jnp.where(summed, total, mixed[rows:].astype(F32)).astype(BF16)
    out[rows:, :] = packet[2 * rows :, :]


def block_masks(docs, near_docs, far_docs):
    rows = docs.shape[1] // 2
    here = [column(docs[:, 0:rows]), column(docs[:, rows:])]
    before = [None if far_docs is None else column(far_docs[:, rows:])]
    before += [column(near_docs[:, 0:rows]), column(near_docs[:, rows:])]
    lead = [jnp.broadcast_to(docs[:, b * rows : b * rows + 1], (rows, LANES)) for b in range(2)]
    return here, before, lead


def same_and_past(docs, col):
    rows = docs.shape[1]
    position = lax.broadcasted_iota(jnp.int32, (rows, rows), 0)
    source = lax.broadcasted_iota(jnp.int32, (rows, rows), 1)
    same = col == jnp.broadcast_to(docs, (rows, rows))
    return jnp.where(same & (source <= position), 1.0, 0.0).astype(BF16)


def far_state(far_docs):
    rows = far_docs.shape[1] // 2
    end = jnp.broadcast_to(far_docs[:, 2 * rows - 1 :], (rows, LANES))
    return end, jnp.broadcast_to(far_docs[:, rows - 1 : rows], (rows, LANES)) == end


def own_products(scratch, at, masked, tri, packet, added, cols, groups, rows):
    for g in range(groups):
        here = slice(g * rows, g * rows + rows)
        masked[here, 0:rows] = scratch[here, at:] * tri[0]
        masked[here, rows:] = scratch[here, at:] * tri[1]
    lower = packet[0:rows, cols].astype(F32)
    lower = jnp.concatenate([lower[0:8] + added, lower[8:]], 0).astype(BF16)
    blank = jnp.zeros((rows, LANES), BF16)
    paired = jnp.concatenate(
        [jnp.concatenate([lower, blank], 0), jnp.concatenate([blank, packet[rows : 2 * rows, cols]], 0)], 1
    )
    return lower, jnp.dot(masked[...], paired, preferred_element_type=F32)


def picked(result, b, groups, rows):
    side = slice(b * LANES, b * LANES + LANES)
    return pick([result[g * rows : g * rows + rows, side] for g in range(groups)])


def hand_out(core, total, gate_own, out_own, out_sib):
    rows = gate_own.shape[0]
    mine = pl.multiple_of(core[0] * rows, rows)
    other = pl.multiple_of((1 - core[0]) * rows, rows)
    out_own[...] = (gate_own[...].astype(F32) * total[pl.ds(mine, rows), :]).astype(BF16)
    out_sib[...] = total[pl.ds(other, rows), :].astype(BF16)


def middle_kernel(core, strips, packet, near, short_filter, *refs, groups, first_group):
    out, taps, diag, tri, keep, target, doc_ends = refs[-7:]
    rows = out.shape[0] // 2
    tap_count = short_filter.shape[0]
    step = pl.program_id(0)

    @pl.when(step == 0)
    def _():
        docs = packet[2 * rows :, 0 : 2 * rows].astype(F32)[0:1]
        here, before, lead = block_masks(docs, near[2 * rows :, 0 : 2 * rows].astype(F32)[0:1], None)
        for b in range(2):
            tri[b] = same_and_past(docs[:, b * rows : b * rows + rows], here[b])
            keep[b, 0:rows, :] = (before[1] == lead[b]).astype(BF16)
            keep[b, rows : 2 * rows, :] = (before[2] == lead[b]).astype(BF16)
            target[b] = (here[b] == lead[b]).astype(F32)
        keep[1, 2 * rows :, :] = (here[0] == lead[1]).astype(BF16)
        doc_ends[0] = before[2][rows - 8 :]
        doc_ends[1] = here[0][0:8]

    blank = jnp.zeros((rows, LANES), BF16)
    own_rim = packet[2 * rows :, :].astype(F32)
    near_rim = near[2 * rows :, :].astype(F32)
    tiles = out.shape[1] // LANES
    for tile in range(tiles):
        cols = slice(tile * LANES, tile * LANES + LANES)
        scratch = taps.at[tile % taps.shape[0]]
        build(scratch, strips, tile, groups, rows, 4 * rows, 1)
        short = widen(short_filter, first_group + (step * tiles + tile) * groups, groups)
        added = own_rim[8:, cols] * rim_sum(near_rim[0:8, cols], doc_ends[0], doc_ends[1], short, tap_count)
        lower, inner = own_products(
            scratch, 3 * rows, diag.at[tile % taps.shape[0]], tri, packet, added, cols, groups, rows
        )
        source = near[0 : 2 * rows, cols]
        paired = jnp.concatenate(
            [
                jnp.concatenate([blank, source * keep[0, 0 : 2 * rows]], 0),
                jnp.concatenate([source, lower], 0) * keep[1],
            ],
            1,
        )
        outer = jnp.dot(scratch[:, 0 : 3 * rows], paired, preferred_element_type=F32)
        for b in range(2):
            out[b * rows : b * rows + rows, cols] = (
                picked(inner, b, groups, rows) + target[b] * picked(outer, b, groups, rows)
            )


def rest_kernel(core, strips, packet, near, far, short_filter, gate_own, sums, *refs, groups, first_group):
    out_own, out_sib, taps, keep, target, total, doc_ends = refs[-7:]
    rows = far.shape[0] - SLAB
    tap_count = short_filter.shape[0]
    step = pl.program_id(0)

    @pl.when(step == 0)
    def _():
        docs = packet[0:SLAB, 0 : 2 * rows].astype(F32)[0:1]
        far_docs = far[rows:, 0 : 2 * rows].astype(F32)[0:1]
        here, before, lead = block_masks(docs, near[0:SLAB, 0 : 2 * rows].astype(F32)[0:1], far_docs)
        end, summed = far_state(far_docs)
        for b in range(2):
            keep[b, 0:rows, :] = ((before[0] == lead[b]) & ~summed).astype(BF16)
            keep[b, rows:, :] = (before[1] == lead[b]).astype(BF16)
            target[b] = (here[b] == lead[b]).astype(F32)
        target[2] = ((here[0] == end) & summed).astype(F32)
        doc_ends[0] = before[0][rows - 8 :]
        doc_ends[1] = before[1][0:8]

    blank = jnp.zeros((rows, LANES), BF16)
    near_rim = near[...].astype(F32)
    far_rim = far[rows:, :].astype(F32)
    tiles = far.shape[1] // LANES
    for tile in range(tiles):
        cols = slice(tile * LANES, tile * LANES + LANES)
        scratch = taps.at[tile % taps.shape[0]]
        build(scratch, strips, tile, groups, rows, 3 * rows)
        short = widen(short_filter, first_group + (step * tiles + tile) * groups, groups)
        added = near_rim[8:, cols] * rim_sum(far_rim[0:8, cols], doc_ends[0], doc_ends[1], short, tap_count)
        added = jnp.concatenate([added, jnp.zeros((rows - 8, LANES), F32)], 0).astype(BF16)
        source = jnp.concatenate([far[0:rows, cols], added], 0)
        paired = jnp.concatenate(
            [
                jnp.concatenate([blank, source * keep[0]], 0),
                jnp.concatenate([source * keep[1], blank], 0),
            ],
            1,
        )
        result = jnp.dot(scratch[...], paired, preferred_element_type=F32)
        total[0:rows, cols] = (
            sums[0:rows, cols]
            + target[0] * picked(result, 0, groups, rows)
            + target[2] * far[0:rows, cols].astype(F32)
        )
        total[rows:, cols] = sums[rows:, cols] + target[1] * picked(result, 1, groups, rows)
    hand_out(core, total, gate_own, out_own, out_sib)


def join_kernel(core, *refs):
    out = refs[-1]
    step = pl.program_id(0)
    for part in range(PARTS):

        @pl.when(step // (pl.num_programs(0) // PARTS) == part)
        def _():
            out[...] = (refs[PARTS][...].astype(F32) * refs[part][...].astype(F32)).astype(BF16)


def body(gate_short, key_short, value_short, gate_long, doc_ids, se_filter, long_filter):
    rows, chans = gate_short.shape
    tap_count, filters = se_filter.shape
    reach = long_filter.shape[1]
    count = lax.axis_size("ctx")
    half = chans // 2
    share = half // PARTS
    group_width = chans // filters
    groups = LANES // group_width
    block = share // STEPS
    steps = share // block
    width = reach + 2 * rows
    core = lax.rem(lax.axis_index("ctx"), 2).astype(jnp.int32).reshape(1)

    swap = [(i, i ^ 1) for i in range(count)]
    ahead = [(i, i + 2) for i in range(count - 2)]
    ahead_two = [(i, i + 4) for i in range(count - 4)]

    def send(value, links):
        return lax.ppermute(value, "ctx", links)

    def shape(*sizes):
        return pltpu.HBM(sizes, BF16)

    def stay(value):
        return pltpu.with_memory_space_constraint(value, pltpu.HBM)

    ahead_of = pl.Buffered(1)

    def whole(sizes):
        return pl.BlockSpec(sizes, lambda i, c: (0,) * len(sizes))

    def mine(height, part):
        return pl.BlockSpec(
            (height, block), lambda i, c: (0, (PARTS * c[0] + part) * steps + i), pipeline_mode=ahead_of
        )

    def local(height):
        return pl.BlockSpec((height, block), lambda i, c: (0, i))

    def strip_part(lanes, part):
        return pl.BlockSpec((block // group_width, SLAB, lanes), lambda i, c: (part * steps + i, 0, 0))

    anywhere = pl.BlockSpec(memory_space=pl.ANY)
    short_spec = pl.BlockSpec((tap_count, filters // 2), lambda i, c: (0, c[0]))

    def call(kernel, name, grid, in_specs, out_specs, out_shape, scratch=(), aliases=None):
        return functools.partial(
            pl.pallas_call(
                kernel,
                grid_spec=pltpu.PrefetchScalarGridSpec(
                    num_scalar_prefetch=1, grid=grid, in_specs=in_specs, out_specs=out_specs, scratch_shapes=scratch
                ),
                out_shape=out_shape,
                input_output_aliases=aliases or {},
                compiler_params=pltpu.CompilerParams(vmem_limit_bytes=LIMIT),
                name=name,
            ),
            core,
        )

    gate_short, key_short, value_short, gate_long = map(stay, (gate_short, key_short, value_short, gate_long))
    docs = stay(doc_ids.reshape(1, rows))
    se_filter = stay(se_filter)

    def begin(part):
        return send(
            call(
                pack_kernel,
                "pack",
                (steps,),
                [
                    pl.BlockSpec(
                        (rows, block),
                        lambda i, c: (0, (PARTS * (1 - c[0]) + part) * steps + i),
                        pipeline_mode=ahead_of,
                    )
                ]
                * 3
                + [whole((1, rows))],
                local(2 * rows + SLAB),
                shape(2 * rows + SLAB, share),
            )(key_short, value_short, gate_short, docs),
            swap,
        )

    def short(part, sibling, after):
        return call(
            functools.partial(short_kernel, groups=groups, first_group=part * (share // group_width)),
            "short",
            (steps,),
            [
                whole((1, rows)),
                mine(rows, part),
                mine(rows, part),
                mine(rows, part),
                local(2 * rows + SLAB),
                short_spec,
            ]
            + [anywhere] * len(after),
            local(2 * rows + SLAB),
            shape(2 * rows + SLAB, share),
            [
                pltpu.VMEM((8 + 2 * rows, block), F32),
                pltpu.VMEM((2 * rows, block), F32),
                pltpu.VMEM((tap_count, 2 * rows, LANES), F32),
                pltpu.VMEM((8 + 2 * rows, LANES), F32),
            ],
        )(docs, key_short, value_short, gate_short, sibling, se_filter, *after)

    def far_packet(part, strips, packet, after):
        return call(
            functools.partial(far_kernel, groups=groups),
            "far",
            (steps,),
            [strip_part(3 * rows, part), local(2 * rows + SLAB)] + [anywhere] * len(after),
            local(rows + SLAB),
            shape(rows + SLAB, share),
            [
                pltpu.VMEM((block // LANES, groups * rows, 2 * rows), BF16),
                pltpu.VMEM((2 * rows, LANES), BF16),
            ],
        )(strips, stay(packet), *after)

    def out_spec(part):
        return pl.BlockSpec((rows, block), lambda i, c: (0, (PARTS * c[0] + part) * steps + i))

    def middle(part, strips, packet, near):
        return call(
            functools.partial(middle_kernel, groups=groups, first_group=part * (share // group_width)),
            "middle",
            (steps,),
            [strip_part(width, part), local(2 * rows + SLAB), local(2 * rows + SLAB), short_spec],
            local(2 * rows),
            jax.ShapeDtypeStruct((2 * rows, share), F32),
            [
                pltpu.VMEM((2, groups * rows, 4 * rows), BF16),
                pltpu.VMEM((2, groups * rows, 2 * rows), BF16),
                pltpu.VMEM((2, rows, rows), BF16),
                pltpu.VMEM((2, 3 * rows, LANES), BF16),
                pltpu.VMEM((2, rows, LANES), F32),
                pltpu.VMEM((2, 8, LANES), F32),
            ],
        )(strips, stay(packet), near, se_filter)

    def rest(part, strips, packet, near, far, sums, begun, after):
        rim = pl.BlockSpec((SLAB, block), lambda i, c: (2 * rows // SLAB, i))
        return call(
            functools.partial(rest_kernel, groups=groups, first_group=part * (share // group_width)),
            "rest",
            (steps,),
            [
                strip_part(4 * rows, part),
                rim,
                rim,
                local(rows + SLAB),
                short_spec,
                mine(rows, part),
                local(2 * rows),
            ]
            + [anywhere] * len(begun + after),
            [out_spec(part), local(rows)],
            [shape(rows, chans), shape(rows, share)],
            [
                pltpu.VMEM((2, groups * rows, 3 * rows), BF16),
                pltpu.VMEM((2, 2 * rows, LANES), BF16),
                pltpu.VMEM((3, rows, LANES), F32),
                pltpu.VMEM((2 * rows, block), F32),
                pltpu.VMEM((2, 8, LANES), F32),
            ],
            aliases={8: 0} if begun else None,
        )(strips, stay(packet), near, far, se_filter, gate_long, sums, *begun, *after)

    def join(got, begun):
        there = pl.BlockSpec((rows, block), lambda i, c: (0, PARTS * steps * (1 - c[0]) + i))

        def got_spec(part):
            return pl.BlockSpec((rows, block), lambda i, c: (0, jnp.clip(i - part * steps, 0, steps - 1)))

        return call(
            join_kernel,
            "join",
            (PARTS * steps,),
            [got_spec(part) for part in range(PARTS)] + [there, anywhere],
            there,
            shape(rows, chans),
            aliases={2 + PARTS: 0},
        )(*got, gate_long, begun)

    siblings = [begin(part) for part in range(PARTS)]
    packets = [short(part, siblings[part], []) for part in range(PARTS)]
    nears = [send(packet, ahead) for packet in packets]
    strips = call(
        strip_kernel,
        "strips",
        (2,),
        [pl.BlockSpec((filters // 4, reach), lambda i, c: (2 * c[0] + i, 0)), anywhere],
        pl.BlockSpec((filters // 4, SLAB, width), lambda i, c: (i, 0, 0)),
        jax.ShapeDtypeStruct((filters // 2, SLAB, width), BF16),
    )(stay(long_filter), stay(packets[-1]))
    fars = []
    for part in range(PARTS):
        beyond = far_packet(part, strips, packets[part], [])
        fars.append(send(beyond, ahead_two))
    sums = [middle(part, strips, packets[part], nears[part]) for part in range(PARTS)]
    got, begun = [], ()
    for part in range(PARTS):
        out, other = rest(part, strips, packets[part], nears[part], fars[part], sums[part], begun, tuple(sums[part + 1 :]))
        got.append(send(other, swap))
        begun = (out,)
    return join(got, out)


def solution(mesh):
    placed = (
        P(("groups", "ctx"), None),
        P(("groups", "ctx"), None),
        P(("groups", "ctx"), None),
        P(("groups", "ctx"), None),
        P(("groups", "ctx")),
        P(),
        P(),
    )
    return jax.shard_map(
        body, mesh=mesh, in_specs=placed, out_specs=P(("groups", "ctx"), None), check_vma=False
    )
```

time: 69.4 us -> 62.9 us (0.906)
  the two profiles are of different devices: /device:TPU:21 before, /device:TPU:0 now
where the time goes in v3:
time: 62.9 us; the launch traced here: 62.4 us
  Pallas kernels  44.5 us (71%)
  starting transfers between devices  16.4 us (26%)
  waiting for transfers between devices  1.41 us (2%)
    ppermute x8, starting transfers between devices, send(): return lax.ppermute(value, 'ctx', links)  16.4 us
    pallas_call x2, Pallas kernels, middle(): call(functools.partial(middle_kernel, groups=groups, first_group=part * (...  11.8 us
    pallas_call x2, Pallas kernels, rest(): call(functools.partial(rest_kernel, groups=groups, first_group=part * (sh...  8.94 us
    pallas_call x2, Pallas kernels, far_packet(): call(functools.partial(far_kernel, groups=groups), 'far', (steps,), [stri...  8.1 us
    pallas_call x2, Pallas kernels, short(): call(functools.partial(short_kernel, groups=groups, first_group=part * (s...  8.07 us
    pallas_call x2, Pallas kernels, begin(): call(pack_kernel, 'pack', (steps,), [pl.BlockSpec((rows, block), lambda i...  3.97 us
    pallas_call x1, Pallas kernels, join(): call(join_kernel, 'join', (PARTS * steps,), [got_spec(part) for part in r...  1.82 us
    pallas_call x1, Pallas kernels, body(): call(strip_kernel, 'strips', (2,), [pl.BlockSpec((filters // 4, reach), l...  1.74 us
  transfers between devices with their start and end apart: 8, of which 2 were waited for; matrix products, arithmetic and copies ran while one was open for 0% of the time, Pallas kernels for 58%

profile of v3, /device:TPU:0, one launch (start us, length us, event | category | flops | bytes accessed | tf_op | source)
XLA Modules:
  0.0 62.4 jit_solution(2319218608001808482)
XLA Ops:
  0.0 2.0 %pack.2 = bf16[272,1024]{1,0:T(8,128)(2,1)} custom-call(s32[1]{0:T(128)} %bitcast.core, bf16[128,4096]{1,0:T(8,128)(2,1)} %key.7, bf16[128,4096]{1,0:T(8,128)(2,1)} %value.7, bf16[128,4096]{1,0:T(8,128)(2,1)} %gate.7, s32[1,128]{1,0:T(1,128)} %bitcast.2), custom_call_target="tpu_custom_call" | custom-call | tf_op jit(solution)/shard_map/pack/pallas_call | solution.py:362
  2.0 0.5 collective-permute-start
  2.4 2.0 %pack.3 = bf16[272,1024]{1,0:T(8,128)(2,1)} custom-call(s32[1]{0:T(128)} %bitcast.core, bf16[128,4096]{1,0:T(8,128)(2,1)} %key.7, bf16[128,4096]{1,0:T(8,128)(2,1)} %value.7, bf16[128,4096]{1,0:T(8,128)(2,1)} %gate.7, s32[1,128]{1,0:T(1,128)} %bitcast.3), custom_call_target="tpu_custom_call" | custom-call | tf_op jit(solution)/shard_map/pack/pallas_call | solution.py:362
  4.4 0.1 collective-permute-start.1
  4.5 0.0 collective-permute-done.sib
  4.5 4.0 %short.2.after.packet = bf16[272,1024]{1,0:T(8,128)(2,1)} custom-call(s32[1]{0:T(128)} %bitcast.core, s32[1,128]{1,0:T(1,128)} %bitcast.4, bf16[128,4096]{1,0:T(8,128)(2,1)} %key.7, bf16[128,4096]{1,0:T(8,128)(2,1)} %value.7, bf16[128,4096]{1,0:T(8,128)(2,1)} %gate.7, bf16[272,1024]{1,0:T(8,128)(2,1)S(1)} %collective-permute-done.sib, f32[7,256]{1,0:T(8,128)} %short_filter.11), custom_call_target="tpu_custom_call" | custom-call | tf_op jit(solution)/shard_map/short/pallas_call | solution.py:382
  8.5 4.9 %collective-permute-start.4 = (bf16[272,1024]{1,0:T(8,128)(2,1)}, bf16[272,1024]{1,0:T(8,128)(2,1)S(1)}, u32[]{:S(2)}, u32[]{:S(2)}) collective-permute-start(bf16[272,1024]{1,0:T(8,128)(2,1)} %short.2.after.packet), channel_id=1, source_target_pairs={{0,2},{1,3},{2,4},{3,5},{4,6},{5,7},{6,8},{7,9},{8,10},{9,11},{10,... | collective-permute-start | bytes 1671176 | tf_op jit(solution)/shard_map/ppermute | solution.py:314
  13.4 0.0 collective-permute-done.1.sib
  13.4 4.0 %short.3.packet = bf16[272,1024]{1,0:T(8,128)(2,1)} custom-call(s32[1]{0:T(128)} %bitcast.core, s32[1,128]{1,0:T(1,128)} %bitcast.5, bf16[128,4096]{1,0:T(8,128)(2,1)} %key.7, bf16[128,4096]{1,0:T(8,128)(2,1)} %value.7, bf16[128,4096]{1,0:T(8,128)(2,1)} %gate.7, bf16[272,1024]{1,0:T(8,128)(2,1)S(1)} %collective-permute-done.1.sib, f32[7,256]{1,0:T(8,128)} %short_filter.11), custom_call_target="tpu_custom_call" | custom-call | tf_op jit(solution)/shard_map/short/pallas_call | solution.py:382
  17.5 3.4 %collective-permute-start.2 = (bf16[272,1024]{1,0:T(8,128)(2,1)}, bf16[272,1024]{1,0:T(8,128)(2,1)S(1)}, u32[]{:S(2)}, u32[]{:S(2)}) collective-permute-start(bf16[272,1024]{1,0:T(8,128)(2,1)} %short.3.packet), channel_id=1, source_target_pairs={{0,2},{1,3},{2,4},{3,5},{4,6},{5,7},{6,8},{7,9},{8,10},{9,11},{10,... | collective-permute-start | bytes 1671176 | tf_op jit(solution)/shard_map/ppermute | solution.py:314
  20.9 1.7 %strips.1 = bf16[128,16,768]{2,1,0:T(8,128)(2,1)S(1)} custom-call(s32[1]{0:T(128)} %bitcast.core, bf16[256,512]{1,0:T(8,128)(2,1)} %filters.1, bf16[272,1024]{1,0:T(8,128)(2,1)} %short.2.after.packet), custom_call_target="tpu_custom_call" | custom-call | tf_op jit(solution)/shard_map/strips/pallas_call | solution.py:487
  22.6 4.0 %far.2 = bf16[144,1024]{1,0:T(8,128)(2,1)} custom-call(s32[1]{0:T(128)} %bitcast.core, bf16[128,16,768]{2,1,0:T(8,128)(2,1)S(1)} %strips.1, bf16[272,1024]{1,0:T(8,128)(2,1)} %short.3.packet), custom_call_target="tpu_custom_call" | custom-call | tf_op jit(solution)/shard_map/far/pallas_call | solution.py:406
  26.7 3.5 %collective-permute-start.3 = (bf16[144,1024]{1,0:T(8,128)(2,1)}, bf16[144,1024]{1,0:T(8,128)(2,1)S(1)}, u32[]{:S(2)}, u32[]{:S(2)}) collective-permute-start(bf16[144,1024]{1,0:T(8,128)(2,1)} %far.2), channel_id=1, source_target_pairs={{0,4},{1,5},{2,6},{3,7},{4,8},{5,9},{6,10},{7,11},{8,12},{9,13},{1... | collective-permute-start | bytes 884744 | tf_op jit(solution)/shard_map/ppermute | solution.py:314
  30.1 4.1 %far.3 = bf16[144,1024]{1,0:T(8,128)(2,1)} custom-call(s32[1]{0:T(128)} %bitcast.core, bf16[128,16,768]{2,1,0:T(8,128)(2,1)S(1)} %strips.1, bf16[272,1024]{1,0:T(8,128)(2,1)} %short.2.after.packet), custom_call_target="tpu_custom_call" | custom-call | tf_op jit(solution)/shard_map/far/pallas_call | solution.py:406
  34.2 3.7 %collective-permute-start.6 = (bf16[144,1024]{1,0:T(8,128)(2,1)}, bf16[144,1024]{1,0:T(8,128)(2,1)S(1)}, u32[]{:S(2)}, u32[]{:S(2)}) collective-permute-start(bf16[144,1024]{1,0:T(8,128)(2,1)} %far.3), channel_id=1, source_target_pairs={{0,4},{1,5},{2,6},{3,7},{4,8},{5,9},{6,10},{7,11},{8,12},{9,13},{1... | collective-permute-start | bytes 884744 | tf_op jit(solution)/shard_map/ppermute | solution.py:314
  37.9 0.0 collective-permute-done.4.near
  37.9 5.9 %middle.3.refs_0_.sums = f32[256,1024]{1,0:T(8,128)S(1)} custom-call(s32[1]{0:T(128)} %bitcast.core, bf16[128,16,768]{2,1,0:T(8,128)(2,1)S(1)} %strips.1, bf16[272,1024]{1,0:T(8,128)(2,1)} %short.2.after.packet, bf16[272,1024]{1,0:T(8,128)(2,1)S(1)} %collective-permute-done.4.near, f32[7,256]{1,0:T(8,128)} %short_filter.11), custom_call_target="tpu_custom_call" | custom-call | tf_op jit(solution)/shard_map/middle/pallas_call | solution.py:423
  43.8 0.0 collective-permute-done.2.near
  43.8 5.9 %middle.2.sums = f32[256,1024]{1,0:T(8,128)S(1)} custom-call(s32[1]{0:T(128)} %bitcast.core, bf16[128,16,768]{2,1,0:T(8,128)(2,1)S(1)} %strips.1, bf16[272,1024]{1,0:T(8,128)(2,1)} %short.3.packet, bf16[272,1024]{1,0:T(8,128)(2,1)S(1)} %collective-permute-done.2.near, f32[7,256]{1,0:T(8,128)} %short_filter.11), custom_call_target="tpu_custom_call" | custom-call | tf_op jit(solution)/shard_map/middle/pallas_call | solution.py:423
  49.8 0.0 collective-permute-done.3.far
  49.8 4.4 %rest.2 = (bf16[128,4096]{1,0:T(8,128)(2,1)}, bf16[128,1024]{1,0:T(8,128)(2,1)}) custom-call(s32[1]{0:T(128)} %bitcast.core, bf16[128,16,768]{2,1,0:T(8,128)(2,1)S(1)} %strips.1, bf16[272,1024]{1,0:T(8,128)(2,1)} %short.3.packet, bf16[272,1024]{1,0:T(8,128)(2,1)S(1)} %collective-permute-done.2.near, bf16[144,1024]{1,0:T(8,128)(2,1)S(1)} %collective-permute-done.3.far, ...), custom_call_target="tpu_custom_call" | custom-call | tf_op jit(solution)/shard_map/rest/pallas_call | solution.py:442
  54.1 0.0 collective-permute-done.6.far
  54.1 0.0 copy-start
  54.1 4.6 %rest.3 = (bf16[128,4096]{1,0:T(8,128)(2,1)}, bf16[128,1024]{1,0:T(8,128)(2,1)}) custom-call(s32[1]{0:T(128)} %bitcast.core, bf16[128,16,768]{2,1,0:T(8,128)(2,1)S(1)} %strips.1, bf16[272,1024]{1,0:T(8,128)(2,1)} %short.2.after.packet, bf16[272,1024]{1,0:T(8,128)(2,1)S(1)} %collective-permute-done.4.near, ...), custom_call_target="tpu_custom_call", output_to_operand_aliasing={{0}: (8, {})} | custom-call | tf_op jit(solution)/shard_map/rest/pallas_call | solution.py:442
  58.7 0.0 collective-permute-start.7
  58.7 0.0 copy-done
  58.7 0.5 collective-permute-start.5
  59.2 1.2 %collective-permute-done.7.refs_1_ = bf16[128,1024]{1,0:T(8,128)(2,1)S(1)} collective-permute-done((bf16[128,1024]{1,0:T(8,128)(2,1)}, bf16[128,1024]{1,0:T(8,128)(2,1)S(1)}, u32[]{:S(2)}, u32[]{:S(2)}) %collective-permute-start.7) | collective-permute-done | bytes 262176 | tf_op jit(solution)/shard_map/ppermute | solution.py:314
  60.5 0.2 collective-permute-done.5.refs_0_
  60.6 1.8 %join.1 = bf16[128,4096]{1,0:T(8,128)(2,1)} custom-call(s32[1]{0:T(128)} %bitcast.core, bf16[128,1024]{1,0:T(8,128)(2,1)S(1)} %collective-permute-done.5.refs_0_, bf16[128,1024]{1,0:T(8,128)(2,1)S(1)} %collective-permute-done.7.refs_1_, bf16[128,4096]{1,0:T(8,128)(2,1)} %refs_2_.1, ...), custom_call_target="tpu_custom_call", output_to_operand_aliasing={{}: (4, {})} | custom-call | tf_op jit(solution)/shard_map/join/pallas_call | solution.py:474
Async XLA Ops:
  2.0 2.5 %collective-permute-start = (bf16[272,1024]{1,0:T(8,128)(2,1)}, bf16[272,1024]{1,0:T(8,128)(2,1)S(1)}, u32[]{:S(2)}, u32[]{:S(2)}) collective-permute-start(bf16[272,1024]{1,0:T(8,128)(2,1)} %pack.2), channel_id=1, source_target_pairs={{0,1},{1,0},{2,3},{3,2},{4,5},{5,4},{6,7},{7,6},{8,9},{9,8},{10,11... | collective-permute-start | bytes 1671176 | tf_op jit(solution)/shard_map/ppermute | solution.py:314
  4.4 9.0 %collective-permute-start.1 = (bf16[272,1024]{1,0:T(8,128)(2,1)}, bf16[272,1024]{1,0:T(8,128)(2,1)S(1)}, u32[]{:S(2)}, u32[]{:S(2)}) collective-permute-start(bf16[272,1024]{1,0:T(8,128)(2,1)} %pack.3), channel_id=1, source_target_pairs={{0,1},{1,0},{2,3},{3,2},{4,5},{5,4},{6,7},{7,6},{8,9},{9,8},{10,11... | collective-permute-start | bytes 1671176 | tf_op jit(solution)/shard_map/ppermute | solution.py:314
  8.5 29.3 %collective-permute-start.4 = (bf16[272,1024]{1,0:T(8,128)(2,1)}, bf16[272,1024]{1,0:T(8,128)(2,1)S(1)}, u32[]{:S(2)}, u32[]{:S(2)}) collective-permute-start(bf16[272,1024]{1,0:T(8,128)(2,1)} %short.2.after.packet), channel_id=1, source_target_pairs={{0,2},{1,3},{2,4},{3,5},{4,6},{5,7},{6,8},{7,9},{8,10},{9,11},{10,... | collective-permute-start | bytes 1671176 | tf_op jit(solution)/shard_map/ppermute | solution.py:314
  17.5 26.3 %collective-permute-start.2 = (bf16[272,1024]{1,0:T(8,128)(2,1)}, bf16[272,1024]{1,0:T(8,128)(2,1)S(1)}, u32[]{:S(2)}, u32[]{:S(2)}) collective-permute-start(bf16[272,1024]{1,0:T(8,128)(2,1)} %short.3.packet), channel_id=1, source_target_pairs={{0,2},{1,3},{2,4},{3,5},{4,6},{5,7},{6,8},{7,9},{8,10},{9,11},{10,... | collective-permute-start | bytes 1671176 | tf_op jit(solution)/shard_map/ppermute | solution.py:314
  26.7 23.1 %collective-permute-start.3 = (bf16[144,1024]{1,0:T(8,128)(2,1)}, bf16[144,1024]{1,0:T(8,128)(2,1)S(1)}, u32[]{:S(2)}, u32[]{:S(2)}) collective-permute-start(bf16[144,1024]{1,0:T(8,128)(2,1)} %far.2), channel_id=1, source_target_pairs={{0,4},{1,5},{2,6},{3,7},{4,8},{5,9},{6,10},{7,11},{8,12},{9,13},{1... | collective-permute-start | bytes 884744 | tf_op jit(solution)/shard_map/ppermute | solution.py:314
  34.2 19.9 %collective-permute-start.6 = (bf16[144,1024]{1,0:T(8,128)(2,1)}, bf16[144,1024]{1,0:T(8,128)(2,1)S(1)}, u32[]{:S(2)}, u32[]{:S(2)}) collective-permute-start(bf16[144,1024]{1,0:T(8,128)(2,1)} %far.3), channel_id=1, source_target_pairs={{0,4},{1,5},{2,6},{3,7},{4,8},{5,9},{6,10},{7,11},{8,12},{9,13},{1... | collective-permute-start | bytes 884744 | tf_op jit(solution)/shard_map/ppermute | solution.py:314
  54.1 4.6 %copy-start = (bf16[128,1024]{1,0:T(8,128)(2,1)S(1)}, bf16[128,1024]{1,0:T(8,128)(2,1)}, u32[]{:S(2)}) copy-start(bf16[128,1024]{1,0:T(8,128)(2,1)} %get-tuple-element.9) | copy-start | bytes 786436
  58.7 1.7 %collective-permute-start.7 = (bf16[128,1024]{1,0:T(8,128)(2,1)}, bf16[128,1024]{1,0:T(8,128)(2,1)S(1)}, u32[]{:S(2)}, u32[]{:S(2)}) collective-permute-start(bf16[128,1024]{1,0:T(8,128)(2,1)} %get-tuple-element.11), channel_id=1, source_target_pairs={{0,1},{1,0},{2,3},{3,2},{4,5},{5,4},{6,7},{7,6},{8,9},{9,8},{10,11... | collective-permute-start | bytes 786440 | tf_op jit(solution)/shard_map/ppermute | solution.py:314
  58.7 1.9 %collective-permute-start.5 = (bf16[128,1024]{1,0:T(8,128)(2,1)S(1)}, bf16[128,1024]{1,0:T(8,128)(2,1)S(1)}, u32[]{:S(2)}, u32[]{:S(2)}) collective-permute-start(bf16[128,1024]{1,0:T(8,128)(2,1)S(1)} %copy-done), channel_id=1, source_target_pairs={{0,1},{1,0},{2,3},{3,2},{4,5},{5,4},{6,7},{7,6},{8,9},{9,8},{10,11... | collective-permute-start | bytes 786440 | tf_op jit(solution)/shard_map/ppermute | solution.py:314

commit v4 on v3

--- a/solution.py
+++ b/solution.py
@@ -13,7 +13,6 @@
 LANES = 128
 LIMIT = 32 * 1024 * 1024
 PARTS = 2
-STEPS = 1
 
 
 def column(row):
@@ -45,12 +44,12 @@
     return total
 
 
-def build(taps, strips, tile, groups, rows, width, nearer=0):
+def build(taps, strips, first, groups, rows, width, nearer=0):
     for g in range(groups):
         for s in range(rows // SLAB):
             at = g * rows + s * SLAB
             begin = (1 + nearer) * rows - SLAB * s
-            taps[at : at + SLAB, 0:width] = strips[tile * groups + g, :, begin : begin + width]
+            taps[at : at + SLAB, 0:width] = strips[first + g, :, begin : begin + width]
 
 
 def pack_kernel(core, key, value, gate, docs, out):
@@ -76,7 +75,7 @@
 
 
 def short_kernel(core, docs, key, value, gate, sib, short_filter, *refs, groups, first_group):
-    packet, kv_rows, gate_rows, agree, doc_rows = refs[-5:]
+    out, packet, kv_rows, gate_rows, agree, doc_rows = refs[-6:]
     step = pl.program_id(0)
     rows, width = key.shape
     tap_count = short_filter.shape[0]
@@ -101,7 +100,7 @@
     gate_rows[pl.ds(other, rows), :] = sib[rows : 2 * rows, :].astype(F32)
     for tile in range(width // LANES):
         cols = slice(tile * LANES, tile * LANES + LANES)
-        taps = widen(short_filter, first_group + (step * (width // LANES) + tile) * groups, groups)
+        taps = widen(short_filter, first_group + tile * groups, groups)
         total = kv_rows[8 : 8 + 2 * rows, cols] * taps[0:1]
         for k in range(1, tap_count):
             total = total + agree[k] * kv_rows[8 - k : 8 - k + 2 * rows, cols] * taps[k : k + 1]
@@ -112,9 +111,10 @@
     doc_line = jnp.concatenate([first, second, jnp.zeros((1, width - 2 * rows), F32)], 1)
     tail = jnp.where(line == 0, jnp.broadcast_to(doc_line, (8, width)), kv_rows[2 * rows : 2 * rows + 8, :])
     packet[2 * rows :, :] = jnp.concatenate([tail, gate_rows[0:8, :]], 0).astype(BF16)
-
-
-def far_kernel(core, strips, packet, *refs, groups):
+    out[...] = packet[...]
+
+
+def far_kernel(core, strips, packet, *refs, groups, first_group):
     out, taps, keep = refs[-3:]
     rows = packet.shape[0] // 2 - SLAB // 2
     docs = packet[2 * rows :, 0 : 2 * rows].astype(F32)[0:1]
@@ -128,7 +128,7 @@
 
     for tile in range(out.shape[1] // LANES):
         cols = slice(tile * LANES, tile * LANES + LANES)
-        build(taps.at[tile], strips, tile, groups, rows, 2 * rows)
+        build(taps.at[tile], strips, first_group + tile * groups, groups, rows, 2 * rows)
         mixed = packet[0 : 2 * rows, cols]
         result = jnp.dot(taps[tile], mixed * keep[...], preferred_element_type=F32)
         total = pick([result[g * rows : g * rows + rows] for g in range(groups)])
@@ -212,8 +212,8 @@
     for tile in range(tiles):
         cols = slice(tile * LANES, tile * LANES + LANES)
         scratch = taps.at[tile % taps.shape[0]]
-        build(scratch, strips, tile, groups, rows, 4 * rows, 1)
-        short = widen(short_filter, first_group + (step * tiles + tile) * groups, groups)
+        build(scratch, strips, first_group + tile * groups, groups, rows, 4 * rows, 1)
+        short = widen(short_filter, first_group + tile * groups, groups)
         added = own_rim[8:, cols] * rim_sum(near_rim[0:8, cols], doc_ends[0], doc_ends[1], short, tap_count)
         lower, inner = own_products(
             scratch, 3 * rows, diag.at[tile % taps.shape[0]], tri, packet, added, cols, groups, rows
@@ -260,8 +260,8 @@
     for tile in range(tiles):
         cols = slice(tile * LANES, tile * LANES + LANES)
         scratch = taps.at[tile % taps.shape[0]]
-        build(scratch, strips, tile, groups, rows, 3 * rows)
-        short = widen(short_filter, first_group + (step * tiles + tile) * groups, groups)
+        build(scratch, strips, first_group + tile * groups, groups, rows, 3 * rows)
+        short = widen(short_filter, first_group + tile * groups, groups)
         added = near_rim[8:, cols] * rim_sum(far_rim[0:8, cols], doc_ends[0], doc_ends[1], short, tap_count)
         added = jnp.concatenate([added, jnp.zeros((rows - 8, LANES), F32)], 0).astype(BF16)
         source = jnp.concatenate([far[0:rows, cols], added], 0)
@@ -301,8 +301,7 @@
     share = half // PARTS
     group_width = chans // filters
     groups = LANES // group_width
-    block = share // STEPS
-    steps = share // block
+    block, steps = share, 1
     width = reach + 2 * rows
     core = lax.rem(lax.axis_index("ctx"), 2).astype(jnp.int32).reshape(1)
 
@@ -332,9 +331,7 @@
     def local(height):
         return pl.BlockSpec((height, block), lambda i, c: (0, i))
 
-    def strip_part(lanes, part):
-        return pl.BlockSpec((block // group_width, SLAB, lanes), lambda i, c: (part * steps + i, 0, 0))
-
+    strip_spec = whole((filters // 2, SLAB, width))
     anywhere = pl.BlockSpec(memory_space=pl.ANY)
     short_spec = pl.BlockSpec((tap_count, filters // 2), lambda i, c: (0, c[0]))
 
@@ -353,7 +350,7 @@
             core,
         )
 
-    gate_short, key_short, value_short, gate_long = map(stay, (gate_short, key_short, value_short, gate_long))
+    gate_short, key_short, value_short = map(stay, (gate_short, key_short, value_short))
     docs = stay(doc_ids.reshape(1, rows))
     se_filter = stay(se_filter)
 
@@ -392,8 +389,8 @@
                 short_spec,
             ]
             + [anywhere] * len(after),
-            local(2 * rows + SLAB),
-            shape(2 * rows + SLAB, share),
+            [local(2 * rows + SLAB)] * 2,
+            [shape(2 * rows + SLAB, share), jax.ShapeDtypeStruct((2 * rows + SLAB, share), BF16)],
             [
                 pltpu.VMEM((8 + 2 * rows, block), F32),
                 pltpu.VMEM((2 * rows, block), F32),
@@ -404,17 +401,17 @@
 
     def far_packet(part, strips, packet, after):
         return call(
-            functools.partial(far_kernel, groups=groups),
+            functools.partial(far_kernel, groups=groups, first_group=part * (share // group_width)),
             "far",
             (steps,),
-            [strip_part(3 * rows, part), local(2 * rows + SLAB)] + [anywhere] * len(after),
+            [strip_spec, local(2 * rows + SLAB)] + [anywhere] * len(after),
             local(rows + SLAB),
             shape(rows + SLAB, share),
             [
                 pltpu.VMEM((block // LANES, groups * rows, 2 * rows), BF16),
                 pltpu.VMEM((2 * rows, LANES), BF16),
             ],
-        )(strips, stay(packet), *after)
+        )(strips, packet, *after)
 
     def out_spec(part):
         return pl.BlockSpec((rows, block), lambda i, c: (0, (PARTS * c[0] + part) * steps + i))
@@ -424,7 +421,7 @@
             functools.partial(middle_kernel, groups=groups, first_group=part * (share // group_width)),
             "middle",
             (steps,),
-            [strip_part(width, part), local(2 * rows + SLAB), local(2 * rows + SLAB), short_spec],
+            [strip_spec, local(2 * rows + SLAB), local(2 * rows + SLAB), short_spec],
             local(2 * rows),
             jax.ShapeDtypeStruct((2 * rows, share), F32),
             [
@@ -435,7 +432,7 @@
                 pltpu.VMEM((2, rows, LANES), F32),
                 pltpu.VMEM((2, 8, LANES), F32),
             ],
-        )(strips, stay(packet), near, se_filter)
+        )(strips, packet, near, se_filter)
 
     def rest(part, strips, packet, near, far, sums, begun, after):
         rim = pl.BlockSpec((SLAB, block), lambda i, c: (2 * rows // SLAB, i))
@@ -444,7 +441,7 @@
             "rest",
             (steps,),
             [
-                strip_part(4 * rows, part),
+                strip_spec,
                 rim,
                 rim,
                 local(rows + SLAB),
@@ -463,7 +460,7 @@
                 pltpu.VMEM((2, 8, LANES), F32),
             ],
             aliases={8: 0} if begun else None,
-        )(strips, stay(packet), near, far, se_filter, gate_long, sums, *begun, *after)
+        )(strips, packet, near, far, se_filter, gate_long, sums, *begun, *after)
 
     def join(got, begun):
         there = pl.BlockSpec((rows, block), lambda i, c: (0, PARTS * steps * (1 - c[0]) + i))
@@ -482,16 +479,16 @@
         )(*got, gate_long, begun)
 
     siblings = [begin(part) for part in range(PARTS)]
-    packets = [short(part, siblings[part], []) for part in range(PARTS)]
-    nears = [send(packet, ahead) for packet in packets]
+    sendable, packets = zip(*[short(part, siblings[part], []) for part in range(PARTS)])
+    nears = [send(packet, ahead) for packet in sendable]
     strips = call(
         strip_kernel,
         "strips",
-        (2,),
-        [pl.BlockSpec((filters // 4, reach), lambda i, c: (2 * c[0] + i, 0)), anywhere],
-        pl.BlockSpec((filters // 4, SLAB, width), lambda i, c: (i, 0, 0)),
+        (1,),
+        [pl.BlockSpec((filters // 2, reach), lambda i, c: (c[0], 0)), anywhere],
+        strip_spec,
         jax.ShapeDtypeStruct((filters // 2, SLAB, width), BF16),
-    )(stay(long_filter), stay(packets[-1]))
+    )(long_filter, stay(sendable[-1]))
     fars = []
     for part in range(PARTS):
         beyond = far_packet(part, strips, packets[part], [])

time: 62.9 us -> 57.5 us (0.914)
  Pallas kernels: 44.5 us -> 39 us
    pallas_call x3, Pallas kernels: 9.84 us -> 6.51 us  [the longest x2 5.8 us: far_packet(): call(functools.partial(far_kernel, groups=groups, first_group=part * (sha...]
    pallas_call x1, Pallas kernels: 1.82 us -> 0.93 us  [join(): call(join_kernel, 'join', (PARTS * steps,), [got_spec(part) for part in r...]
    pallas_call x2, Pallas kernels: 11.8 us -> 11.2 us  [middle(): call(functools.partial(middle_kernel, groups=groups, first_group=part * (...]
  transfers between devices with their start and end apart: 8 -> 8, of which waited for: 2 -> 1; matrix products, arithmetic and copies ran while one was open for 0% -> 0% of each run, Pallas kernels for 58% -> 56%
where the time goes in v4:
time: 57.5 us; the launch traced here: 57 us
  Pallas kernels  39 us (68%)
  starting transfers between devices  16.4 us (29%)
  waiting for transfers between devices  1.41 us (2%)
    ppermute x8, starting transfers between devices, send(): return lax.ppermute(value, 'ctx', links)  16.4 us
    pallas_call x2, Pallas kernels, middle(): call(functools.partial(middle_kernel, groups=groups, first_group=part * (...  11.2 us
    pallas_call x2, Pallas kernels, rest(): call(functools.partial(rest_kernel, groups=groups, first_group=part * (sh...  8.35 us
    pallas_call x2, Pallas kernels, short(): call(functools.partial(short_kernel, groups=groups, first_group=part * (s...  8.08 us
    pallas_call x2, Pallas kernels, far_packet(): call(functools.partial(far_kernel, groups=groups, first_group=part * (sha...  5.8 us
    pallas_call x2, Pallas kernels, begin(): call(pack_kernel, 'pack', (steps,), [pl.BlockSpec((rows, block), lambda i...  3.96 us
    ppermute x8, waiting for transfers between devices, send(): return lax.ppermute(value, 'ctx', links)  1.41 us
  transfers between devices with their start and end apart: 8, of which 1 were waited for; matrix products, arithmetic and copies ran while one was open for 0% of the time, Pallas kernels for 56%

profile of v4, /device:TPU:0, one launch (start us, length us, event | category | flops | bytes accessed | tf_op | source)
XLA Modules:
  0.0 57.0 jit_solution(11294694077239613816)
XLA Ops:
  0.0 2.0 %pack.2 = bf16[272,1024]{1,0:T(8,128)(2,1)} custom-call(s32[1]{0:T(128)} %bitcast.core, bf16[128,4096]{1,0:T(8,128)(2,1)} %key.7, bf16[128,4096]{1,0:T(8,128)(2,1)} %value.7, bf16[128,4096]{1,0:T(8,128)(2,1)} %gate.7, s32[1,128]{1,0:T(1,128)} %bitcast.2), custom_call_target="tpu_custom_call" | custom-call | tf_op jit(solution)/shard_map/pack/pallas_call | solution.py:359
  2.0 0.5 collective-permute-start
  2.4 2.0 %pack.3 = bf16[272,1024]{1,0:T(8,128)(2,1)} custom-call(s32[1]{0:T(128)} %bitcast.core, bf16[128,4096]{1,0:T(8,128)(2,1)} %key.7, bf16[128,4096]{1,0:T(8,128)(2,1)} %value.7, bf16[128,4096]{1,0:T(8,128)(2,1)} %gate.7, s32[1,128]{1,0:T(1,128)} %bitcast.3), custom_call_target="tpu_custom_call" | custom-call | tf_op jit(solution)/shard_map/pack/pallas_call | solution.py:359
  4.4 0.0 copy-start.1
  4.4 0.1 collective-permute-start.1
  4.5 0.0 collective-permute-done.sib
  4.5 4.1 %short.2 = (bf16[272,1024]{1,0:T(8,128)(2,1)}, bf16[272,1024]{1,0:T(8,128)(2,1)S(1)}) custom-call(s32[1]{0:T(128)} %bitcast.core, s32[1,128]{1,0:T(1,128)} %bitcast.4, bf16[128,4096]{1,0:T(8,128)(2,1)} %key.7, bf16[128,4096]{1,0:T(8,128)(2,1)} %value.7, bf16[128,4096]{1,0:T(8,128)(2,1)} %gate.7, bf16[272,1024]{1,0:T(8,128)(2,1)S(1)} %collective-permute-done.sib, ...), custom_call_target="tpu_custom_call" | custom-call | tf_op jit(solution)/shard_map/short/pallas_call | solution.py:379
  8.5 4.9 %collective-permute-start.4 = (bf16[272,1024]{1,0:T(8,128)(2,1)}, bf16[272,1024]{1,0:T(8,128)(2,1)S(1)}, u32[]{:S(2)}, u32[]{:S(2)}) collective-permute-start(bf16[272,1024]{1,0:T(8,128)(2,1)} %get-tuple-element.13.after), channel_id=1, source_target_pairs={{0,2},{1,3},{2,4},{3,5},{4,6},{5,7},{6,8},{7,9},{8,10},{9,11},{10,... | collective-permute-start | bytes 1671176 | tf_op jit(solution)/shard_map/ppermute | solution.py:313
  13.4 0.0 collective-permute-done.1.sib
  13.4 4.0 %short.3 = (bf16[272,1024]{1,0:T(8,128)(2,1)}, bf16[272,1024]{1,0:T(8,128)(2,1)S(1)}) custom-call(s32[1]{0:T(128)} %bitcast.core, s32[1,128]{1,0:T(1,128)} %bitcast.5, bf16[128,4096]{1,0:T(8,128)(2,1)} %key.7, bf16[128,4096]{1,0:T(8,128)(2,1)} %value.7, bf16[128,4096]{1,0:T(8,128)(2,1)} %gate.7, bf16[272,1024]{1,0:T(8,128)(2,1)S(1)} %collective-permute-done.1.sib, ...), custom_call_target="tpu_custom_call" | custom-call | tf_op jit(solution)/shard_map/short/pallas_call | solution.py:379
  17.4 3.4 %collective-permute-start.2 = (bf16[272,1024]{1,0:T(8,128)(2,1)}, bf16[272,1024]{1,0:T(8,128)(2,1)S(1)}, u32[]{:S(2)}, u32[]{:S(2)}) collective-permute-start(bf16[272,1024]{1,0:T(8,128)(2,1)} %get-tuple-element.15), channel_id=1, source_target_pairs={{0,2},{1,3},{2,4},{3,5},{4,6},{5,7},{6,8},{7,9},{8,10},{9,11},{10,... | collective-permute-start | bytes 1671176 | tf_op jit(solution)/shard_map/ppermute | solution.py:313
  20.9 0.0 copy-done.1
  20.9 0.7 %strips.1 = bf16[128,16,768]{2,1,0:T(8,128)(2,1)S(1)} custom-call(s32[1]{0:T(128)} %bitcast.core, bf16[256,512]{1,0:T(8,128)(2,1)S(1)} %copy-done.1, bf16[272,1024]{1,0:T(8,128)(2,1)} %get-tuple-element.13.after), custom_call_target="tpu_custom_call" | custom-call | tf_op jit(solution)/shard_map/strips/pallas_call | solution.py:484
  21.6 2.9 %far.2 = bf16[144,1024]{1,0:T(8,128)(2,1)} custom-call(s32[1]{0:T(128)} %bitcast.core, bf16[128,16,768]{2,1,0:T(8,128)(2,1)S(1)} %strips.1, bf16[272,1024]{1,0:T(8,128)(2,1)S(1)} %get-tuple-element.14.packet), custom_call_target="tpu_custom_call" | custom-call | tf_op jit(solution)/shard_map/far/pallas_call | solution.py:403
  24.5 3.5 %collective-permute-start.3 = (bf16[144,1024]{1,0:T(8,128)(2,1)}, bf16[144,1024]{1,0:T(8,128)(2,1)S(1)}, u32[]{:S(2)}, u32[]{:S(2)}) collective-permute-start(bf16[144,1024]{1,0:T(8,128)(2,1)} %far.2), channel_id=1, source_target_pairs={{0,4},{1,5},{2,6},{3,7},{4,8},{5,9},{6,10},{7,11},{8,12},{9,13},{1... | collective-permute-start | bytes 884744 | tf_op jit(solution)/shard_map/ppermute | solution.py:313
  28.0 2.9 %far.3 = bf16[144,1024]{1,0:T(8,128)(2,1)} custom-call(s32[1]{0:T(128)} %bitcast.core, bf16[128,16,768]{2,1,0:T(8,128)(2,1)S(1)} %strips.1, bf16[272,1024]{1,0:T(8,128)(2,1)S(1)} %get-tuple-element.16.packet), custom_call_target="tpu_custom_call" | custom-call | tf_op jit(solution)/shard_map/far/pallas_call | solution.py:403
  30.9 3.7 %collective-permute-start.6 = (bf16[144,1024]{1,0:T(8,128)(2,1)}, bf16[144,1024]{1,0:T(8,128)(2,1)S(1)}, u32[]{:S(2)}, u32[]{:S(2)}) collective-permute-start(bf16[144,1024]{1,0:T(8,128)(2,1)} %far.3), channel_id=1, source_target_pairs={{0,4},{1,5},{2,6},{3,7},{4,8},{5,9},{6,10},{7,11},{8,12},{9,13},{1... | collective-permute-start | bytes 884744 | tf_op jit(solution)/shard_map/ppermute | solution.py:313
  34.5 0.0 collective-permute-done.4.near
  34.5 5.6 %middle.3.refs_0_.sums = f32[256,1024]{1,0:T(8,128)S(1)} custom-call(s32[1]{0:T(128)} %bitcast.core, bf16[128,16,768]{2,1,0:T(8,128)(2,1)S(1)} %strips.1, bf16[272,1024]{1,0:T(8,128)(2,1)S(1)} %get-tuple-element.16.packet, bf16[272,1024]{1,0:T(8,128)(2,1)S(1)} %collective-permute-done.4.near, f32[7,256]{1,0:T(8,128)} %short_filter.11), custom_call_target="tpu_custom_call" | custom-call | tf_op jit(solution)/shard_map/middle/pallas_call | solution.py:420
  40.1 0.0 copy-start
  40.1 0.0 collective-permute-done.2.near
  40.1 5.6 %middle.2.sums = f32[256,1024]{1,0:T(8,128)S(1)} custom-call(s32[1]{0:T(128)} %bitcast.core, bf16[128,16,768]{2,1,0:T(8,128)(2,1)S(1)} %strips.1, bf16[272,1024]{1,0:T(8,128)(2,1)S(1)} %get-tuple-element.14.packet, bf16[272,1024]{1,0:T(8,128)(2,1)S(1)} %collective-permute-done.2.near, f32[7,256]{1,0:T(8,128)} %short_filter.11), custom_call_target="tpu_custom_call" | custom-call | tf_op jit(solution)/shard_map/middle/pallas_call | solution.py:420
  45.8 0.0 collective-permute-done.3.far
  45.8 0.0 copy-done
  45.8 4.0 %rest.2 = (bf16[128,4096]{1,0:T(8,128)(2,1)}, bf16[128,1024]{1,0:T(8,128)(2,1)}) custom-call(s32[1]{0:T(128)} %bitcast.core, bf16[128,16,768]{2,1,0:T(8,128)(2,1)S(1)} %strips.1, bf16[272,1024]{1,0:T(8,128)(2,1)S(1)} %get-tuple-element.14.packet, bf16[272,1024]{1,0:T(8,128)(2,1)S(1)} %collective-permute-done.2.near, ...), custom_call_target="tpu_custom_call" | custom-call | tf_op jit(solution)/shard_map/rest/pallas_call | solution.py:439
  49.8 0.0 collective-permute-done.6.far
  49.8 0.0 copy-start.2
  49.8 4.3 %rest.3 = (bf16[128,4096]{1,0:T(8,128)(2,1)}, bf16[128,1024]{1,0:T(8,128)(2,1)}) custom-call(s32[1]{0:T(128)} %bitcast.core, bf16[128,16,768]{2,1,0:T(8,128)(2,1)S(1)} %strips.1, bf16[272,1024]{1,0:T(8,128)(2,1)S(1)} %get-tuple-element.16.packet, bf16[272,1024]{1,0:T(8,128)(2,1)S(1)} %collective-permute-done.4.near, ...), custom_call_target="tpu_custom_call", output_to_operand_aliasing={{0}: (8, {})} | custom-call | tf_op jit(solution)/shard_map/rest/pallas_call | solution.py:439
  54.1 0.0 collective-permute-start.7
  54.1 0.0 copy-done.2
  54.1 0.5 collective-permute-start.5
  54.7 1.4 %collective-permute-done.7.refs_1_ = bf16[128,1024]{1,0:T(8,128)(2,1)S(1)} collective-permute-done((bf16[128,1024]{1,0:T(8,128)(2,1)}, bf16[128,1024]{1,0:T(8,128)(2,1)S(1)}, u32[]{:S(2)}, u32[]{:S(2)}) %collective-permute-start.7) | collective-permute-done | bytes 262176 | tf_op jit(solution)/shard_map/ppermute | solution.py:313
  56.0 0.0 collective-permute-done.5.refs_0_
  56.1 0.9 %join.1 = bf16[128,4096]{1,0:T(8,128)(2,1)} custom-call(s32[1]{0:T(128)} %bitcast.core, bf16[128,1024]{1,0:T(8,128)(2,1)S(1)} %collective-permute-done.5.refs_0_, bf16[128,1024]{1,0:T(8,128)(2,1)S(1)} %collective-permute-done.7.refs_1_, bf16[128,4096]{1,0:T(8,128)(2,1)S(1)} %copy-done, ...), custom_call_target="tpu_custom_call", output_to_operand_aliasing={{}: (4, {})} | custom-call | tf_op jit(solution)/shard_map/join/pallas_call | solution.py:471
Async XLA Ops:
  2.0 2.5 %collective-permute-start = (bf16[272,1024]{1,0:T(8,128)(2,1)}, bf16[272,1024]{1,0:T(8,128)(2,1)S(1)}, u32[]{:S(2)}, u32[]{:S(2)}) collective-permute-start(bf16[272,1024]{1,0:T(8,128)(2,1)} %pack.2), channel_id=1, source_target_pairs={{0,1},{1,0},{2,3},{3,2},{4,5},{5,4},{6,7},{7,6},{8,9},{9,8},{10,11... | collective-permute-start | bytes 1671176 | tf_op jit(solution)/shard_map/ppermute | solution.py:313
  4.4 16.4 %copy-start.1 = (bf16[256,512]{1,0:T(8,128)(2,1)S(1)}, bf16[256,512]{1,0:T(8,128)(2,1)}, u32[]{:S(2)}) copy-start(bf16[256,512]{1,0:T(8,128)(2,1)} %filters.1) | copy-start | bytes 786436
  4.4 9.0 %collective-permute-start.1 = (bf16[272,1024]{1,0:T(8,128)(2,1)}, bf16[272,1024]{1,0:T(8,128)(2,1)S(1)}, u32[]{:S(2)}, u32[]{:S(2)}) collective-permute-start(bf16[272,1024]{1,0:T(8,128)(2,1)} %pack.3), channel_id=1, source_target_pairs={{0,1},{1,0},{2,3},{3,2},{4,5},{5,4},{6,7},{7,6},{8,9},{9,8},{10,11... | collective-permute-start | bytes 1671176 | tf_op jit(solution)/shard_map/ppermute | solution.py:313
  8.5 26.0 %collective-permute-start.4 = (bf16[272,1024]{1,0:T(8,128)(2,1)}, bf16[272,1024]{1,0:T(8,128)(2,1)S(1)}, u32[]{:S(2)}, u32[]{:S(2)}) collective-permute-start(bf16[272,1024]{1,0:T(8,128)(2,1)} %get-tuple-element.13.after), channel_id=1, source_target_pairs={{0,2},{1,3},{2,4},{3,5},{4,6},{5,7},{6,8},{7,9},{8,10},{9,11},{10,... | collective-permute-start | bytes 1671176 | tf_op jit(solution)/shard_map/ppermute | solution.py:313
  17.4 22.7 %collective-permute-start.2 = (bf16[272,1024]{1,0:T(8,128)(2,1)}, bf16[272,1024]{1,0:T(8,128)(2,1)S(1)}, u32[]{:S(2)}, u32[]{:S(2)}) collective-permute-start(bf16[272,1024]{1,0:T(8,128)(2,1)} %get-tuple-element.15), channel_id=1, source_target_pairs={{0,2},{1,3},{2,4},{3,5},{4,6},{5,7},{6,8},{7,9},{8,10},{9,11},{10,... | collective-permute-start | bytes 1671176 | tf_op jit(solution)/shard_map/ppermute | solution.py:313
  24.5 21.3 %collective-permute-start.3 = (bf16[144,1024]{1,0:T(8,128)(2,1)}, bf16[144,1024]{1,0:T(8,128)(2,1)S(1)}, u32[]{:S(2)}, u32[]{:S(2)}) collective-permute-start(bf16[144,1024]{1,0:T(8,128)(2,1)} %far.2), channel_id=1, source_target_pairs={{0,4},{1,5},{2,6},{3,7},{4,8},{5,9},{6,10},{7,11},{8,12},{9,13},{1... | collective-permute-start | bytes 884744 | tf_op jit(solution)/shard_map/ppermute | solution.py:313
  30.9 19.0 %collective-permute-start.6 = (bf16[144,1024]{1,0:T(8,128)(2,1)}, bf16[144,1024]{1,0:T(8,128)(2,1)S(1)}, u32[]{:S(2)}, u32[]{:S(2)}) collective-permute-start(bf16[144,1024]{1,0:T(8,128)(2,1)} %far.3), channel_id=1, source_target_pairs={{0,4},{1,5},{2,6},{3,7},{4,8},{5,9},{6,10},{7,11},{8,12},{9,13},{1... | collective-permute-start | bytes 884744 | tf_op jit(solution)/shard_map/ppermute | solution.py:313
  40.1 5.7 %copy-start = (bf16[128,4096]{1,0:T(8,128)(2,1)S(1)}, bf16[128,4096]{1,0:T(8,128)(2,1)}, u32[]{:S(2)}) copy-start(bf16[128,4096]{1,0:T(8,128)(2,1)} %refs_2_.1) | copy-start | bytes 3145732
  49.8 4.3 %copy-start.2 = (bf16[128,1024]{1,0:T(8,128)(2,1)S(1)}, bf16[128,1024]{1,0:T(8,128)(2,1)}, u32[]{:S(2)}) copy-start(bf16[128,1024]{1,0:T(8,128)(2,1)} %get-tuple-element.17) | copy-start | bytes 786436
  54.1 1.9 %collective-permute-start.7 = (bf16[128,1024]{1,0:T(8,128)(2,1)}, bf16[128,1024]{1,0:T(8,128)(2,1)S(1)}, u32[]{:S(2)}, u32[]{:S(2)}) collective-permute-start(bf16[128,1024]{1,0:T(8,128)(2,1)} %get-tuple-element.19), channel_id=1, source_target_pairs={{0,1},{1,0},{2,3},{3,2},{4,5},{5,4},{6,7},{7,6},{8,9},{9,8},{10,11... | collective-permute-start | bytes 786440 | tf_op jit(solution)/shard_map/ppermute | solution.py:313
  54.1 1.9 %collective-permute-start.5 = (bf16[128,1024]{1,0:T(8,128)(2,1)S(1)}, bf16[128,1024]{1,0:T(8,128)(2,1)S(1)}, u32[]{:S(2)}, u32[]{:S(2)}) collective-permute-start(bf16[128,1024]{1,0:T(8,128)(2,1)S(1)} %copy-done.2), channel_id=1, source_target_pairs={{0,1},{1,0},{2,3},{3,2},{4,5},{5,4},{6,7},{7,6},{8,9},{9,8},{10,11... | collective-permute-start | bytes 786440 | tf_op jit(solution)/shard_map/ppermute | solution.py:313

commit v5 on v4

--- a/solution.py
+++ b/solution.py
@@ -42,6 +42,13 @@
         same = (pltpu.roll(tail_docs, k, 0) == docs) & (line < k)
         total = total + jnp.where(same, pltpu.roll(tail, k, 0), 0.0) * taps[k : k + 1, :]
     return total
+
+
+def rim_rows(out, gates, tail, tail_docs, docs, short_filter, first_group, groups):
+    for tile in range(out.shape[1] // LANES):
+        cols = slice(tile * LANES, tile * LANES + LANES)
+        taps = widen(short_filter, first_group + tile * groups, groups)
+        out[:, cols] = gates[:, cols] * rim_sum(tail[:, cols], tail_docs, docs, taps, short_filter.shape[0])
 
 
 def build(taps, strips, first, groups, rows, width, nearer=0):
@@ -119,7 +126,8 @@
     rows = packet.shape[0] // 2 - SLAB // 2
     docs = packet[2 * rows :, 0 : 2 * rows].astype(F32)[0:1]
     last = jnp.broadcast_to(docs[:, 2 * rows - 1 :], (rows, LANES))
-    summed = jnp.broadcast_to(docs[:, rows - 1 : rows], (rows, LANES)) == last
+    summed = jnp.broadcast_to(docs[:, rows + 7 : rows + 8], (rows, LANES)) == last
+    tail = packet[2 * rows :, :].astype(F32)[0:8]
 
     @pl.when(pl.program_id(0) == 0)
     def _():
@@ -130,10 +138,14 @@
         cols = slice(tile * LANES, tile * LANES + LANES)
         build(taps.at[tile], strips, first_group + tile * groups, groups, rows, 2 * rows)
         mixed = packet[0 : 2 * rows, cols]
-        result = jnp.dot(taps[tile], mixed * keep[...], preferred_element_type=F32)
+        kept = mixed * keep[...]
+        result = jnp.dot(taps[tile], kept, preferred_element_type=F32)
         total = pick([result[g * rows : g * rows + rows] for g in range(groups)])
         out[0:rows, cols] = jnp.where(summed, total, mixed[rows:].astype(F32)).astype(BF16)
-    out[rows:, :] = packet[2 * rows :, :]
+        nearest = jnp.concatenate([taps[tile, g * rows : g * rows + SLAB, 0:rows] for g in range(groups)], 0)
+        result = jnp.dot(nearest, kept[rows:], preferred_element_type=F32)
+        more = pick([result[g * SLAB : g * SLAB + SLAB] for g in range(groups)])[0:8]
+        out[rows:, cols] = jnp.concatenate([tail[:, cols], more], 0).astype(BF16)
 
 
 def block_masks(docs, near_docs, far_docs):
@@ -156,7 +168,7 @@
 def far_state(far_docs):
     rows = far_docs.shape[1] // 2
     end = jnp.broadcast_to(far_docs[:, 2 * rows - 1 :], (rows, LANES))
-    return end, jnp.broadcast_to(far_docs[:, rows - 1 : rows], (rows, LANES)) == end
+    return end, jnp.broadcast_to(far_docs[:, rows + 7 : rows + 8], (rows, LANES)) == end
 
 
 def own_products(scratch, at, masked, tri, packet, added, cols, groups, rows):
@@ -178,6 +190,11 @@
     return pick([result[g * rows : g * rows + rows, side] for g in range(groups)])
 
 
+def half_filters(core, short_filter):
+    width = short_filter.shape[1] // 2
+    return short_filter[:, pl.ds(pl.multiple_of(core[0] * width, LANES), width)]
+
+
 def hand_out(core, total, gate_own, out_own, out_sib):
     rows = gate_own.shape[0]
     mine = pl.multiple_of(core[0] * rows, rows)
@@ -187,9 +204,9 @@
 
 
 def middle_kernel(core, strips, packet, near, short_filter, *refs, groups, first_group):
-    out, taps, diag, tri, keep, target, doc_ends = refs[-7:]
+    out, taps, diag, tri, keep, target, doc_ends, rim = refs[-8:]
+    short_filter = half_filters(core, short_filter)
     rows = out.shape[0] // 2
-    tap_count = short_filter.shape[0]
     step = pl.program_id(0)
 
     @pl.when(step == 0)
@@ -208,13 +225,13 @@
     blank = jnp.zeros((rows, LANES), BF16)
     own_rim = packet[2 * rows :, :].astype(F32)
     near_rim = near[2 * rows :, :].astype(F32)
+    rim_rows(rim, own_rim[8:], near_rim[0:8], doc_ends[0], doc_ends[1], short_filter, first_group, groups)
     tiles = out.shape[1] // LANES
     for tile in range(tiles):
         cols = slice(tile * LANES, tile * LANES + LANES)
         scratch = taps.at[tile % taps.shape[0]]
         build(scratch, strips, first_group + tile * groups, groups, rows, 4 * rows, 1)
-        short = widen(short_filter, first_group + tile * groups, groups)
-        added = own_rim[8:, cols] * rim_sum(near_rim[0:8, cols], doc_ends[0], doc_ends[1], short, tap_count)
+        added = rim[:, cols]
         lower, inner = own_products(
             scratch, 3 * rows, diag.at[tile % taps.shape[0]], tri, packet, added, cols, groups, rows
         )
@@ -233,53 +250,63 @@
             )
 
 
-def rest_kernel(core, strips, packet, near, far, short_filter, gate_own, sums, *refs, groups, first_group):
-    out_own, out_sib, taps, keep, target, total, doc_ends = refs[-7:]
+def rest_kernel(core, strips, packet, near, far, short_filter, gate_long, sums, *refs, groups, first_group, part):
+    out_own, out_sib, taps, keep, target, total, doc_ends, rim = refs[-8:]
+    short_filter = half_filters(core, short_filter)
     rows = far.shape[0] - SLAB
-    tap_count = short_filter.shape[0]
     step = pl.program_id(0)
 
     @pl.when(step == 0)
     def _():
-        docs = packet[0:SLAB, 0 : 2 * rows].astype(F32)[0:1]
+        docs = packet[2 * rows :, 0 : 2 * rows].astype(F32)[0:1]
         far_docs = far[rows:, 0 : 2 * rows].astype(F32)[0:1]
-        here, before, lead = block_masks(docs, near[0:SLAB, 0 : 2 * rows].astype(F32)[0:1], far_docs)
+        here, before, lead = block_masks(docs, near[2 * rows :, 0 : 2 * rows].astype(F32)[0:1], far_docs)
         end, summed = far_state(far_docs)
         for b in range(2):
             keep[b, 0:rows, :] = ((before[0] == lead[b]) & ~summed).astype(BF16)
-            keep[b, rows:, :] = (before[1] == lead[b]).astype(BF16)
             target[b] = (here[b] == lead[b]).astype(F32)
-        target[2] = ((here[0] == end) & summed).astype(F32)
+            target[2 + b] = ((here[b] == end) & summed).astype(F32)
+            doc_ends[2 + b] = (before[1] == lead[b]).astype(F32)[0:8]
         doc_ends[0] = before[0][rows - 8 :]
         doc_ends[1] = before[1][0:8]
 
-    blank = jnp.zeros((rows, LANES), BF16)
-    near_rim = near[...].astype(F32)
+    lanes = lax.broadcasted_iota(jnp.int32, (SLAB, LANES), 1)
+    near_rim = near[2 * rows :, :].astype(F32)
     far_rim = far[rows:, :].astype(F32)
+    rim_rows(rim, near_rim[8:], far_rim[0:8], doc_ends[0], doc_ends[1], short_filter, first_group, groups)
     tiles = far.shape[1] // LANES
     for tile in range(tiles):
         cols = slice(tile * LANES, tile * LANES + LANES)
         scratch = taps.at[tile % taps.shape[0]]
-        build(scratch, strips, first_group + tile * groups, groups, rows, 3 * rows)
-        short = widen(short_filter, first_group + tile * groups, groups)
-        added = near_rim[8:, cols] * rim_sum(far_rim[0:8, cols], doc_ends[0], doc_ends[1], short, tap_count)
-        added = jnp.concatenate([added, jnp.zeros((rows - 8, LANES), F32)], 0).astype(BF16)
-        source = jnp.concatenate([far[0:rows, cols], added], 0)
+        for g in range(groups):
+            for slab in range(rows // SLAB):
+                at = g * rows + slab * SLAB
+                begin = rows - SLAB * slab
+                wide = strips[first_group + tile * groups + g, :, begin : begin + 3 * rows]
+                scratch[at : at + SLAB, 0:rows] = jnp.where(lanes < 8, wide[:, 2 * rows :], wide[:, 0:rows])
+                scratch[at : at + SLAB, rows:] = wide[:, rows : 2 * rows]
+        added = rim[:, cols]
+        spread = [
+            jnp.concatenate([added * doc_ends[2 + b], jnp.zeros((rows - 8, LANES), F32)], 0).astype(BF16)
+            for b in range(2)
+        ]
+        source = far[0:rows, cols]
         paired = jnp.concatenate(
             [
-                jnp.concatenate([blank, source * keep[0]], 0),
-                jnp.concatenate([source * keep[1], blank], 0),
+                jnp.concatenate([spread[0], source * keep[0]], 0),
+                jnp.concatenate([source * keep[1], spread[1]], 0),
             ],
             1,
         )
         result = jnp.dot(scratch[...], paired, preferred_element_type=F32)
         total[0:rows, cols] = (
-            sums[0:rows, cols]
-            + target[0] * picked(result, 0, groups, rows)
-            + target[2] * far[0:rows, cols].astype(F32)
+            sums[0:rows, cols] + target[0] * picked(result, 0, groups, rows) + target[2] * source.astype(F32)
         )
         total[rows:, cols] = sums[rows:, cols] + target[1] * picked(result, 1, groups, rows)
-    hand_out(core, total, gate_own, out_own, out_sib)
+        total[rows : rows + 8, cols] += target[3, 0:8] * far_rim[8:, cols]
+    share = far.shape[1]
+    at = pl.multiple_of((PARTS * core[0] + part) * share, LANES)
+    hand_out(core, total, gate_long[:, pl.ds(at, share)], out_own, out_sib)
 
 
 def join_kernel(core, *refs):
@@ -352,7 +379,7 @@
 
     gate_short, key_short, value_short = map(stay, (gate_short, key_short, value_short))
     docs = stay(doc_ids.reshape(1, rows))
-    se_filter = stay(se_filter)
+    se_near, se_filter = se_filter, stay(se_filter)
 
     def begin(part):
         return send(
@@ -421,7 +448,7 @@
             functools.partial(middle_kernel, groups=groups, first_group=part * (share // group_width)),
             "middle",
             (steps,),
-            [strip_spec, local(2 * rows + SLAB), local(2 * rows + SLAB), short_spec],
+            [strip_spec, local(2 * rows + SLAB), local(2 * rows + SLAB), whole((tap_count, filters))],
             local(2 * rows),
             jax.ShapeDtypeStruct((2 * rows, share), F32),
             [
@@ -431,36 +458,37 @@
                 pltpu.VMEM((2, 3 * rows, LANES), BF16),
                 pltpu.VMEM((2, rows, LANES), F32),
                 pltpu.VMEM((2, 8, LANES), F32),
+                pltpu.VMEM((8, share), F32),
             ],
-        )(strips, packet, near, se_filter)
+        )(strips, packet, near, se_near)
 
     def rest(part, strips, packet, near, far, sums, begun, after):
-        rim = pl.BlockSpec((SLAB, block), lambda i, c: (2 * rows // SLAB, i))
         return call(
-            functools.partial(rest_kernel, groups=groups, first_group=part * (share // group_width)),
+            functools.partial(rest_kernel, groups=groups, first_group=part * (share // group_width), part=part),
             "rest",
             (steps,),
             [
                 strip_spec,
-                rim,
-                rim,
+                local(2 * rows + SLAB),
+                local(2 * rows + SLAB),
                 local(rows + SLAB),
-                short_spec,
-                mine(rows, part),
+                whole((tap_count, filters)),
+                whole((rows, chans)),
                 local(2 * rows),
             ]
             + [anywhere] * len(begun + after),
             [out_spec(part), local(rows)],
             [shape(rows, chans), shape(rows, share)],
             [
-                pltpu.VMEM((2, groups * rows, 3 * rows), BF16),
-                pltpu.VMEM((2, 2 * rows, LANES), BF16),
-                pltpu.VMEM((3, rows, LANES), F32),
+                pltpu.VMEM((2, groups * rows, 2 * rows), BF16),
+                pltpu.VMEM((2, rows, LANES), BF16),
+                pltpu.VMEM((4, rows, LANES), F32),
                 pltpu.VMEM((2 * rows, block), F32),
-                pltpu.VMEM((2, 8, LANES), F32),
+                pltpu.VMEM((4, 8, LANES), F32),
+                pltpu.VMEM((8, share), F32),
             ],
             aliases={8: 0} if begun else None,
-        )(strips, packet, near, far, se_filter, gate_long, sums, *begun, *after)
+        )(strips, packet, near, far, se_near, gate_long, sums, *begun, *after)
 
     def join(got, begun):
         there = pl.BlockSpec((rows, block), lambda i, c: (0, PARTS * steps * (1 - c[0]) + i))

time: 57.5 us -> 56.7 us (0.986)
  the two profiles are of different devices: /device:TPU:0 before, /device:TPU:13 now
where the time goes in v5:
time: 56.7 us; the launch traced here: 56.4 us
  Pallas kernels  36.1 us (64%)
  starting transfers between devices  13.5 us (24%)
  waiting for transfers between devices  6.67 us (12%)
    ppermute x8, starting transfers between devices, send(): return lax.ppermute(value, 'ctx', links)  13.5 us
    pallas_call x2, Pallas kernels, middle(): call(functools.partial(middle_kernel, groups=groups, first_group=part * (...  9.71 us
    pallas_call x2, Pallas kernels, short(): call(functools.partial(short_kernel, groups=groups, first_group=part * (s...  8.09 us
    pallas_call x2, Pallas kernels, rest(): call(functools.partial(rest_kernel, groups=groups, first_group=part * (sh...  6.9 us
    ppermute x8, waiting for transfers between devices, send(): return lax.ppermute(value, 'ctx', links)  6.67 us
    pallas_call x2, Pallas kernels, far_packet(): call(functools.partial(far_kernel, groups=groups, first_group=part * (sha...  5.79 us
    pallas_call x2, Pallas kernels, begin(): call(pack_kernel, 'pack', (steps,), [pl.BlockSpec((rows, block), lambda i...  3.96 us
  transfers between devices with their start and end apart: 8, of which 4 were waited for; matrix products, arithmetic and copies ran while one was open for 0% of the time, Pallas kernels for 53%

profile of v5, /device:TPU:13, one launch (start us, length us, event | category | flops | bytes accessed | tf_op | source)
XLA Modules:
  0.0 56.4 jit_solution(14414276646100185659)
XLA Ops:
  0.0 2.0 %pack.2 = bf16[272,1024]{1,0:T(8,128)(2,1)} custom-call(s32[1]{0:T(128)} %bitcast.core, bf16[128,4096]{1,0:T(8,128)(2,1)} %key.7, bf16[128,4096]{1,0:T(8,128)(2,1)} %value.7, bf16[128,4096]{1,0:T(8,128)(2,1)} %gate.7, s32[1,128]{1,0:T(1,128)} %bitcast.2), custom_call_target="tpu_custom_call" | custom-call | tf_op jit(solution)/shard_map/pack/pallas_call | solution.py:386
  2.0 0.7 %collective-permute-start = (bf16[272,1024]{1,0:T(8,128)(2,1)}, bf16[272,1024]{1,0:T(8,128)(2,1)S(1)}, u32[]{:S(2)}, u32[]{:S(2)}) collective-permute-start(bf16[272,1024]{1,0:T(8,128)(2,1)} %pack.2), channel_id=1, source_target_pairs={{0,1},{1,0},{2,3},{3,2},{4,5},{5,4},{6,7},{7,6},{8,9},{9,8},{10,11... | collective-permute-start | bytes 1671176 | tf_op jit(solution)/shard_map/ppermute | solution.py:340
  2.7 2.0 %pack.3 = bf16[272,1024]{1,0:T(8,128)(2,1)} custom-call(s32[1]{0:T(128)} %bitcast.core, bf16[128,4096]{1,0:T(8,128)(2,1)} %key.7, bf16[128,4096]{1,0:T(8,128)(2,1)} %value.7, bf16[128,4096]{1,0:T(8,128)(2,1)} %gate.7, s32[1,128]{1,0:T(1,128)} %bitcast.3), custom_call_target="tpu_custom_call" | custom-call | tf_op jit(solution)/shard_map/pack/pallas_call | solution.py:386
  4.6 0.0 copy-start.2
  4.6 0.0 collective-permute-start.1
  4.6 0.0 collective-permute-done.sib
  4.6 4.1 %short.2 = (bf16[272,1024]{1,0:T(8,128)(2,1)}, bf16[272,1024]{1,0:T(8,128)(2,1)S(1)}) custom-call(s32[1]{0:T(128)} %bitcast.core, s32[1,128]{1,0:T(1,128)} %bitcast.4, bf16[128,4096]{1,0:T(8,128)(2,1)} %key.7, bf16[128,4096]{1,0:T(8,128)(2,1)} %value.7, bf16[128,4096]{1,0:T(8,128)(2,1)} %gate.7, bf16[272,1024]{1,0:T(8,128)(2,1)S(1)} %collective-permute-done.sib, ...), custom_call_target="tpu_custom_call" | custom-call | tf_op jit(solution)/shard_map/short/pallas_call | solution.py:406
  8.7 3.1 %collective-permute-start.4 = (bf16[272,1024]{1,0:T(8,128)(2,1)}, bf16[272,1024]{1,0:T(8,128)(2,1)S(1)}, u32[]{:S(2)}, u32[]{:S(2)}) collective-permute-start(bf16[272,1024]{1,0:T(8,128)(2,1)} %get-tuple-element.13.after), channel_id=1, source_target_pairs={{0,2},{1,3},{2,4},{3,5},{4,6},{5,7},{6,8},{7,9},{8,10},{9,11},{10,... | collective-permute-start | bytes 1671176 | tf_op jit(solution)/shard_map/ppermute | solution.py:340
  11.9 0.0 collective-permute-done.1.sib
  11.9 4.0 %short.3 = (bf16[272,1024]{1,0:T(8,128)(2,1)}, bf16[272,1024]{1,0:T(8,128)(2,1)S(1)}) custom-call(s32[1]{0:T(128)} %bitcast.core, s32[1,128]{1,0:T(1,128)} %bitcast.5, bf16[128,4096]{1,0:T(8,128)(2,1)} %key.7, bf16[128,4096]{1,0:T(8,128)(2,1)} %value.7, bf16[128,4096]{1,0:T(8,128)(2,1)} %gate.7, bf16[272,1024]{1,0:T(8,128)(2,1)S(1)} %collective-permute-done.1.sib, ...), custom_call_target="tpu_custom_call" | custom-call | tf_op jit(solution)/shard_map/short/pallas_call | solution.py:406
  15.9 3.1 %collective-permute-start.2 = (bf16[272,1024]{1,0:T(8,128)(2,1)}, bf16[272,1024]{1,0:T(8,128)(2,1)S(1)}, u32[]{:S(2)}, u32[]{:S(2)}) collective-permute-start(bf16[272,1024]{1,0:T(8,128)(2,1)} %get-tuple-element.15), channel_id=1, source_target_pairs={{0,2},{1,3},{2,4},{3,5},{4,6},{5,7},{6,8},{7,9},{8,10},{9,11},{10,... | collective-permute-start | bytes 1671176 | tf_op jit(solution)/shard_map/ppermute | solution.py:340
  19.0 0.0 copy-done.2
  19.0 0.7 %strips.1 = bf16[128,16,768]{2,1,0:T(8,128)(2,1)S(1)} custom-call(s32[1]{0:T(128)} %bitcast.core, bf16[256,512]{1,0:T(8,128)(2,1)S(1)} %copy-done.2, bf16[272,1024]{1,0:T(8,128)(2,1)} %get-tuple-element.13.after), custom_call_target="tpu_custom_call" | custom-call | tf_op jit(solution)/shard_map/strips/pallas_call | solution.py:512
  19.8 0.0 copy-start.1
  19.8 2.9 %far.2 = bf16[144,1024]{1,0:T(8,128)(2,1)} custom-call(s32[1]{0:T(128)} %bitcast.core, bf16[128,16,768]{2,1,0:T(8,128)(2,1)S(1)} %strips.1, bf16[272,1024]{1,0:T(8,128)(2,1)S(1)} %get-tuple-element.14.packet), custom_call_target="tpu_custom_call" | custom-call | tf_op jit(solution)/shard_map/far/pallas_call | solution.py:430
  22.7 3.2 %collective-permute-start.3 = (bf16[144,1024]{1,0:T(8,128)(2,1)}, bf16[144,1024]{1,0:T(8,128)(2,1)S(1)}, u32[]{:S(2)}, u32[]{:S(2)}) collective-permute-start(bf16[144,1024]{1,0:T(8,128)(2,1)} %far.2), channel_id=1, source_target_pairs={{0,4},{1,5},{2,6},{3,7},{4,8},{5,9},{6,10},{7,11},{8,12},{9,13},{1... | collective-permute-start | bytes 884744 | tf_op jit(solution)/shard_map/ppermute | solution.py:340
  25.9 2.9 %far.3 = bf16[144,1024]{1,0:T(8,128)(2,1)} custom-call(s32[1]{0:T(128)} %bitcast.core, bf16[128,16,768]{2,1,0:T(8,128)(2,1)S(1)} %strips.1, bf16[272,1024]{1,0:T(8,128)(2,1)S(1)} %get-tuple-element.16.packet), custom_call_target="tpu_custom_call" | custom-call | tf_op jit(solution)/shard_map/far/pallas_call | solution.py:430
  28.8 2.1 %collective-permute-start.6 = (bf16[144,1024]{1,0:T(8,128)(2,1)}, bf16[144,1024]{1,0:T(8,128)(2,1)S(1)}, u32[]{:S(2)}, u32[]{:S(2)}) collective-permute-start(bf16[144,1024]{1,0:T(8,128)(2,1)} %far.3), channel_id=1, source_target_pairs={{0,4},{1,5},{2,6},{3,7},{4,8},{5,9},{6,10},{7,11},{8,12},{9,13},{1... | collective-permute-start | bytes 884744 | tf_op jit(solution)/shard_map/ppermute | solution.py:340
  30.9 0.0 collective-permute-done.4.near
  30.9 0.0 copy-done.1
  30.9 4.9 %middle.3.refs_0_.sums = f32[256,1024]{1,0:T(8,128)S(1)} custom-call(s32[1]{0:T(128)} %bitcast.core, bf16[128,16,768]{2,1,0:T(8,128)(2,1)S(1)} %strips.1, bf16[272,1024]{1,0:T(8,128)(2,1)S(1)} %get-tuple-element.16.packet, bf16[272,1024]{1,0:T(8,128)(2,1)S(1)} %collective-permute-done.4.near, f32[7,256]{1,0:T(8,128)S(1)} %copy-done.1), custom_call_target="tpu_custom_call" | custom-call | tf_op jit(solution)/shard_map/middle/pallas_call | solution.py:447
  35.8 0.0 copy-start
  35.8 0.7 %collective-permute-done.2.near = bf16[272,1024]{1,0:T(8,128)(2,1)S(1)} collective-permute-done((bf16[272,1024]{1,0:T(8,128)(2,1)}, bf16[272,1024]{1,0:T(8,128)(2,1)S(1)}, u32[]{:S(2)}, u32[]{:S(2)}) %collective-permute-start.2) | collective-permute-done | bytes 557088 | tf_op jit(solution)/shard_map/ppermute | solution.py:340
  36.5 4.9 %middle.2.sums = f32[256,1024]{1,0:T(8,128)S(1)} custom-call(s32[1]{0:T(128)} %bitcast.core, bf16[128,16,768]{2,1,0:T(8,128)(2,1)S(1)} %strips.1, bf16[272,1024]{1,0:T(8,128)(2,1)S(1)} %get-tuple-element.14.packet, bf16[272,1024]{1,0:T(8,128)(2,1)S(1)} %collective-permute-done.2.near, f32[7,256]{1,0:T(8,128)S(1)} %copy-done.1), custom_call_target="tpu_custom_call" | custom-call | tf_op jit(solution)/shard_map/middle/pallas_call | solution.py:447
  41.3 1.4 %collective-permute-done.3.far = bf16[144,1024]{1,0:T(8,128)(2,1)S(1)} collective-permute-done((bf16[144,1024]{1,0:T(8,128)(2,1)}, bf16[144,1024]{1,0:T(8,128)(2,1)S(1)}, u32[]{:S(2)}, u32[]{:S(2)}) %collective-permute-start.3) | collective-permute-done | bytes 294944 | tf_op jit(solution)/shard_map/ppermute | solution.py:340
  42.7 0.0 copy-done
  42.7 3.5 %rest.2 = (bf16[128,4096]{1,0:T(8,128)(2,1)}, bf16[128,1024]{1,0:T(8,128)(2,1)}) custom-call(s32[1]{0:T(128)} %bitcast.core, bf16[128,16,768]{2,1,0:T(8,128)(2,1)S(1)} %strips.1, bf16[272,1024]{1,0:T(8,128)(2,1)S(1)} %get-tuple-element.14.packet, bf16[272,1024]{1,0:T(8,128)(2,1)S(1)} %collective-permute-done.2.near, ...), custom_call_target="tpu_custom_call" | custom-call | tf_op jit(solution)/shard_map/rest/pallas_call | solution.py:466
  46.2 2.9 %collective-permute-done.6.far = bf16[144,1024]{1,0:T(8,128)(2,1)S(1)} collective-permute-done((bf16[144,1024]{1,0:T(8,128)(2,1)}, bf16[144,1024]{1,0:T(8,128)(2,1)S(1)}, u32[]{:S(2)}, u32[]{:S(2)}) %collective-permute-start.6) | collective-permute-done | bytes 294944 | tf_op jit(solution)/shard_map/ppermute | solution.py:340
  49.1 0.0 copy-start.3
  49.1 3.4 %rest.3 = (bf16[128,4096]{1,0:T(8,128)(2,1)}, bf16[128,1024]{1,0:T(8,128)(2,1)}) custom-call(s32[1]{0:T(128)} %bitcast.core, bf16[128,16,768]{2,1,0:T(8,128)(2,1)S(1)} %strips.1, bf16[272,1024]{1,0:T(8,128)(2,1)S(1)} %get-tuple-element.16.packet, bf16[272,1024]{1,0:T(8,128)(2,1)S(1)} %collective-permute-done.4.near, ...), custom_call_target="tpu_custom_call", output_to_operand_aliasing={{0}: (8, {})} | custom-call | tf_op jit(solution)/shard_map/rest/pallas_call | solution.py:466
  52.5 1.3 %collective-permute-start.7 = (bf16[128,1024]{1,0:T(8,128)(2,1)}, bf16[128,1024]{1,0:T(8,128)(2,1)S(1)}, u32[]{:S(2)}, u32[]{:S(2)}) collective-permute-start(bf16[128,1024]{1,0:T(8,128)(2,1)} %get-tuple-element.19), channel_id=1, source_target_pairs={{0,1},{1,0},{2,3},{3,2},{4,5},{5,4},{6,7},{7,6},{8,9},{9,8},{10,11... | collective-permute-start | bytes 786440 | tf_op jit(solution)/shard_map/ppermute | solution.py:340
  53.8 0.0 copy-done.3
  53.8 0.0 collective-permute-start.5
  53.8 1.7 %collective-permute-done.7.refs_1_ = bf16[128,1024]{1,0:T(8,128)(2,1)S(1)} collective-permute-done((bf16[128,1024]{1,0:T(8,128)(2,1)}, bf16[128,1024]{1,0:T(8,128)(2,1)S(1)}, u32[]{:S(2)}, u32[]{:S(2)}) %collective-permute-start.7) | collective-permute-done | bytes 262176 | tf_op jit(solution)/shard_map/ppermute | solution.py:340
  55.5 0.0 collective-permute-done.5.refs_0_
  55.5 0.9 %join.1 = bf16[128,4096]{1,0:T(8,128)(2,1)} custom-call(s32[1]{0:T(128)} %bitcast.core, bf16[128,1024]{1,0:T(8,128)(2,1)S(1)} %collective-permute-done.5.refs_0_, bf16[128,1024]{1,0:T(8,128)(2,1)S(1)} %collective-permute-done.7.refs_1_, bf16[128,4096]{1,0:T(8,128)(2,1)S(1)} %copy-done, ...), custom_call_target="tpu_custom_call", output_to_operand_aliasing={{}: (4, {})} | custom-call | tf_op jit(solution)/shard_map/join/pallas_call | solution.py:499
Async XLA Ops:
  2.0 2.7 %collective-permute-start = (bf16[272,1024]{1,0:T(8,128)(2,1)}, bf16[272,1024]{1,0:T(8,128)(2,1)S(1)}, u32[]{:S(2)}, u32[]{:S(2)}) collective-permute-start(bf16[272,1024]{1,0:T(8,128)(2,1)} %pack.2), channel_id=1, source_target_pairs={{0,1},{1,0},{2,3},{3,2},{4,5},{5,4},{6,7},{7,6},{8,9},{9,8},{10,11... | collective-permute-start | bytes 1671176 | tf_op jit(solution)/shard_map/ppermute | solution.py:340
  4.6 14.4 %copy-start.2 = (bf16[256,512]{1,0:T(8,128)(2,1)S(1)}, bf16[256,512]{1,0:T(8,128)(2,1)}, u32[]{:S(2)}) copy-start(bf16[256,512]{1,0:T(8,128)(2,1)} %filters.1) | copy-start | bytes 786436
  4.6 7.2 %collective-permute-start.1 = (bf16[272,1024]{1,0:T(8,128)(2,1)}, bf16[272,1024]{1,0:T(8,128)(2,1)S(1)}, u32[]{:S(2)}, u32[]{:S(2)}) collective-permute-start(bf16[272,1024]{1,0:T(8,128)(2,1)} %pack.3), channel_id=1, source_target_pairs={{0,1},{1,0},{2,3},{3,2},{4,5},{5,4},{6,7},{7,6},{8,9},{9,8},{10,11... | collective-permute-start | bytes 1671176 | tf_op jit(solution)/shard_map/ppermute | solution.py:340
  8.7 22.2 %collective-permute-start.4 = (bf16[272,1024]{1,0:T(8,128)(2,1)}, bf16[272,1024]{1,0:T(8,128)(2,1)S(1)}, u32[]{:S(2)}, u32[]{:S(2)}) collective-permute-start(bf16[272,1024]{1,0:T(8,128)(2,1)} %get-tuple-element.13.after), channel_id=1, source_target_pairs={{0,2},{1,3},{2,4},{3,5},{4,6},{5,7},{6,8},{7,9},{8,10},{9,11},{10,... | collective-permute-start | bytes 1671176 | tf_op jit(solution)/shard_map/ppermute | solution.py:340
  15.9 20.6 %collective-permute-start.2 = (bf16[272,1024]{1,0:T(8,128)(2,1)}, bf16[272,1024]{1,0:T(8,128)(2,1)S(1)}, u32[]{:S(2)}, u32[]{:S(2)}) collective-permute-start(bf16[272,1024]{1,0:T(8,128)(2,1)} %get-tuple-element.15), channel_id=1, source_target_pairs={{0,2},{1,3},{2,4},{3,5},{4,6},{5,7},{6,8},{7,9},{8,10},{9,11},{10,... | collective-permute-start | bytes 1671176 | tf_op jit(solution)/shard_map/ppermute | solution.py:340
  19.8 11.1 %copy-start.1 = (f32[7,256]{1,0:T(8,128)S(1)}, f32[7,256]{1,0:T(8,128)}, u32[]{:S(2)}) copy-start(f32[7,256]{1,0:T(8,128)} %short_filter.11) | copy-start | bytes 21508
  22.7 20.1 %collective-permute-start.3 = (bf16[144,1024]{1,0:T(8,128)(2,1)}, bf16[144,1024]{1,0:T(8,128)(2,1)S(1)}, u32[]{:S(2)}, u32[]{:S(2)}) collective-permute-start(bf16[144,1024]{1,0:T(8,128)(2,1)} %far.2), channel_id=1, source_target_pairs={{0,4},{1,5},{2,6},{3,7},{4,8},{5,9},{6,10},{7,11},{8,12},{9,13},{1... | collective-permute-start | bytes 884744 | tf_op jit(solution)/shard_map/ppermute | solution.py:340
  28.8 20.3 %collective-permute-start.6 = (bf16[144,1024]{1,0:T(8,128)(2,1)}, bf16[144,1024]{1,0:T(8,128)(2,1)S(1)}, u32[]{:S(2)}, u32[]{:S(2)}) collective-permute-start(bf16[144,1024]{1,0:T(8,128)(2,1)} %far.3), channel_id=1, source_target_pairs={{0,4},{1,5},{2,6},{3,7},{4,8},{5,9},{6,10},{7,11},{8,12},{9,13},{1... | collective-permute-start | bytes 884744 | tf_op jit(solution)/shard_map/ppermute | solution.py:340
  35.8 7.0 %copy-start = (bf16[128,4096]{1,0:T(8,128)(2,1)S(1)}, bf16[128,4096]{1,0:T(8,128)(2,1)}, u32[]{:S(2)}) copy-start(bf16[128,4096]{1,0:T(8,128)(2,1)} %refs_2_.1) | copy-start | bytes 3145732
  49.1 4.8 %copy-start.3 = (bf16[128,1024]{1,0:T(8,128)(2,1)S(1)}, bf16[128,1024]{1,0:T(8,128)(2,1)}, u32[]{:S(2)}) copy-start(bf16[128,1024]{1,0:T(8,128)(2,1)} %get-tuple-element.17) | copy-start | bytes 786436
  52.5 3.0 %collective-permute-start.7 = (bf16[128,1024]{1,0:T(8,128)(2,1)}, bf16[128,1024]{1,0:T(8,128)(2,1)S(1)}, u32[]{:S(2)}, u32[]{:S(2)}) collective-permute-start(bf16[128,1024]{1,0:T(8,128)(2,1)} %get-tuple-element.19), channel_id=1, source_target_pairs={{0,1},{1,0},{2,3},{3,2},{4,5},{5,4},{6,7},{7,6},{8,9},{9,8},{10,11... | collective-permute-start | bytes 786440 | tf_op jit(solution)/shard_map/ppermute | solution.py:340
  53.8 1.7 %collective-permute-start.5 = (bf16[128,1024]{1,0:T(8,128)(2,1)S(1)}, bf16[128,1024]{1,0:T(8,128)(2,1)S(1)}, u32[]{:S(2)}, u32[]{:S(2)}) collective-permute-start(bf16[128,1024]{1,0:T(8,128)(2,1)S(1)} %copy-done.3), channel_id=1, source_target_pairs={{0,1},{1,0},{2,3},{3,2},{4,5},{5,4},{6,7},{7,6},{8,9},{9,8},{10,11... | collective-permute-start | bytes 786440 | tf_op jit(solution)/shard_map/ppermute | solution.py:340

commit v6 on v5

--- a/solution.py
+++ b/solution.py
@@ -51,11 +51,11 @@
         out[:, cols] = gates[:, cols] * rim_sum(tail[:, cols], tail_docs, docs, taps, short_filter.shape[0])
 
 
-def build(taps, strips, first, groups, rows, width, nearer=0):
+def build(taps, strips, first, groups, rows, width):
     for g in range(groups):
         for s in range(rows // SLAB):
             at = g * rows + s * SLAB
-            begin = (1 + nearer) * rows - SLAB * s
+            begin = rows - SLAB * s
             taps[at : at + SLAB, 0:width] = strips[first + g, :, begin : begin + width]
 
 
@@ -171,11 +171,20 @@
     return end, jnp.broadcast_to(far_docs[:, rows + 7 : rows + 8], (rows, LANES)) == end
 
 
-def own_products(scratch, at, masked, tri, packet, added, cols, groups, rows):
+def build_middle(scratch, masked, tri, strips, first, groups, rows):
     for g in range(groups):
-        here = slice(g * rows, g * rows + rows)
-        masked[here, 0:rows] = scratch[here, at:] * tri[0]
-        masked[here, rows:] = scratch[here, at:] * tri[1]
+        for slab in range(rows // SLAB):
+            at = g * rows + slab * SLAB
+            begin = 2 * rows - SLAB * slab
+            wide = strips[first + g, :, begin : begin + 4 * rows]
+            scratch[at : at + SLAB, :] = wide[:, 0 : 3 * rows]
+            inside = wide[:, 3 * rows :]
+            for b in range(2):
+                side = slice(b * rows, b * rows + rows)
+                masked[at : at + SLAB, side] = inside * tri[b, slab * SLAB : slab * SLAB + SLAB, :]
+
+
+def own_products(masked, packet, added, cols, rows):
     lower = packet[0:rows, cols].astype(F32)
     lower = jnp.concatenate([lower[0:8] + added, lower[8:]], 0).astype(BF16)
     blank = jnp.zeros((rows, LANES), BF16)
@@ -230,11 +239,10 @@
     for tile in range(tiles):
         cols = slice(tile * LANES, tile * LANES + LANES)
         scratch = taps.at[tile % taps.shape[0]]
-        build(scratch, strips, first_group + tile * groups, groups, rows, 4 * rows, 1)
+        masked = diag.at[tile % taps.shape[0]]
+        build_middle(scratch, masked, tri, strips, first_group + tile * groups, groups, rows)
         added = rim[:, cols]
-        lower, inner = own_products(
-            scratch, 3 * rows, diag.at[tile % taps.shape[0]], tri, packet, added, cols, groups, rows
-        )
+        lower, inner = own_products(masked, packet, added, cols, rows)
         source = near[0 : 2 * rows, cols]
         paired = jnp.concatenate(
             [
@@ -243,14 +251,30 @@
             ],
             1,
         )
-        outer = jnp.dot(scratch[:, 0 : 3 * rows], paired, preferred_element_type=F32)
+        outer = jnp.dot(scratch[...], paired, preferred_element_type=F32)
         for b in range(2):
             out[b * rows : b * rows + rows, cols] = (
                 picked(inner, b, groups, rows) + target[b] * picked(outer, b, groups, rows)
             )
 
 
-def rest_kernel(core, strips, packet, near, far, short_filter, gate_long, sums, *refs, groups, first_group, part):
+def build_rest(scratch, strips, first, groups, rows):
+    lanes = lax.broadcasted_iota(jnp.int32, (SLAB, LANES), 1)
+    for g in range(groups):
+        for slab in range(rows // SLAB):
+            at = g * rows + slab * SLAB
+            begin = rows - SLAB * slab
+            wide = strips[first + g, :, begin : begin + 3 * rows]
+            scratch[at : at + SLAB, 0:rows] = jnp.where(lanes < 8, wide[:, 2 * rows :], wide[:, 0:rows])
+            scratch[at : at + SLAB, rows:] = wide[:, rows : 2 * rows]
+
+
+def ready_kernel(core, strips, after, taps, groups, first_group):
+    for tile in range(taps.shape[0]):
+        build_rest(taps.at[tile], strips, first_group + tile * groups, groups, taps.shape[1] // groups)
+
+
+def rest_kernel(core, strips, packet, near, far, short_filter, gate_long, sums, *refs, groups, first_group, part, built):
     out_own, out_sib, taps, keep, target, total, doc_ends, rim = refs[-8:]
     short_filter = half_filters(core, short_filter)
     rows = far.shape[0] - SLAB
@@ -270,21 +294,17 @@
         doc_ends[0] = before[0][rows - 8 :]
         doc_ends[1] = before[1][0:8]
 
-    lanes = lax.broadcasted_iota(jnp.int32, (SLAB, LANES), 1)
     near_rim = near[2 * rows :, :].astype(F32)
     far_rim = far[rows:, :].astype(F32)
     rim_rows(rim, near_rim[8:], far_rim[0:8], doc_ends[0], doc_ends[1], short_filter, first_group, groups)
     tiles = far.shape[1] // LANES
     for tile in range(tiles):
         cols = slice(tile * LANES, tile * LANES + LANES)
-        scratch = taps.at[tile % taps.shape[0]]
-        for g in range(groups):
-            for slab in range(rows // SLAB):
-                at = g * rows + slab * SLAB
-                begin = rows - SLAB * slab
-                wide = strips[first_group + tile * groups + g, :, begin : begin + 3 * rows]
-                scratch[at : at + SLAB, 0:rows] = jnp.where(lanes < 8, wide[:, 2 * rows :], wide[:, 0:rows])
-                scratch[at : at + SLAB, rows:] = wide[:, rows : 2 * rows]
+        if built:
+            scratch = strips.at[tile]
+        else:
+            scratch = taps.at[tile % taps.shape[0]]
+            build_rest(scratch, strips, first_group + tile * groups, groups, rows)
         added = rim[:, cols]
         spread = [
             jnp.concatenate([added * doc_ends[2 + b], jnp.zeros((rows - 8, LANES), F32)], 0).astype(BF16)
@@ -316,7 +336,9 @@
 
         @pl.when(step // (pl.num_programs(0) // PARTS) == part)
         def _():
-            out[...] = (refs[PARTS][...].astype(F32) * refs[part][...].astype(F32)).astype(BF16)
+            width = out.shape[1]
+            at = pl.multiple_of((PARTS * (1 - core[0]) + part) * width, LANES)
+            out[...] = (refs[PARTS][:, pl.ds(at, width)].astype(F32) * refs[part][...].astype(F32)).astype(BF16)
 
 
 def body(gate_short, key_short, value_short, gate_long, doc_ids, se_filter, long_filter):
@@ -443,16 +465,17 @@
     def out_spec(part):
         return pl.BlockSpec((rows, block), lambda i, c: (0, (PARTS * c[0] + part) * steps + i))
 
-    def middle(part, strips, packet, near):
+    def middle(part, strips, packet, near, after):
         return call(
             functools.partial(middle_kernel, groups=groups, first_group=part * (share // group_width)),
             "middle",
             (steps,),
-            [strip_spec, local(2 * rows + SLAB), local(2 * rows + SLAB), whole((tap_count, filters))],
+            [strip_spec, local(2 * rows + SLAB), local(2 * rows + SLAB), whole((tap_count, filters))]
+            + [anywhere] * len(after),
             local(2 * rows),
             jax.ShapeDtypeStruct((2 * rows, share), F32),
             [
-                pltpu.VMEM((2, groups * rows, 4 * rows), BF16),
+                pltpu.VMEM((2, groups * rows, 3 * rows), BF16),
                 pltpu.VMEM((2, groups * rows, 2 * rows), BF16),
                 pltpu.VMEM((2, rows, rows), BF16),
                 pltpu.VMEM((2, 3 * rows, LANES), BF16),
@@ -460,15 +483,26 @@
                 pltpu.VMEM((2, 8, LANES), F32),
                 pltpu.VMEM((8, share), F32),
             ],
-        )(strips, packet, near, se_near)
+        )(strips, packet, near, se_near, *after)
+
+    def ready(part, strips, after):
+        size = (share // LANES, groups * rows, 2 * rows)
+        return call(
+            functools.partial(ready_kernel, groups=groups, first_group=part * (share // group_width)),
+            "ready",
+            (1,),
+            [strip_spec, anywhere],
+            whole(size),
+            jax.ShapeDtypeStruct(size, BF16),
+        )(strips, after)
 
     def rest(part, strips, packet, near, far, sums, begun, after):
         return call(
-            functools.partial(rest_kernel, groups=groups, first_group=part * (share // group_width), part=part),
+            functools.partial(rest_kernel, groups=groups, first_group=part * (share // group_width), part=part, built=part > 0),
             "rest",
             (steps,),
             [
-                strip_spec,
+                whole(strips.shape),
                 local(2 * rows + SLAB),
                 local(2 * rows + SLAB),
                 local(rows + SLAB),
@@ -480,7 +514,7 @@
             [out_spec(part), local(rows)],
             [shape(rows, chans), shape(rows, share)],
             [
-                pltpu.VMEM((2, groups * rows, 2 * rows), BF16),
+                pltpu.VMEM((2, groups * rows if part == 0 else SLAB, 2 * rows), BF16),
                 pltpu.VMEM((2, rows, LANES), BF16),
                 pltpu.VMEM((4, rows, LANES), F32),
                 pltpu.VMEM((2 * rows, block), F32),
@@ -500,7 +534,7 @@
             join_kernel,
             "join",
             (PARTS * steps,),
-            [got_spec(part) for part in range(PARTS)] + [there, anywhere],
+            [got_spec(part) for part in range(PARTS)] + [whole((rows, chans)), anywhere],
             there,
             shape(rows, chans),
             aliases={2 + PARTS: 0},
@@ -521,13 +555,13 @@
     for part in range(PARTS):
         beyond = far_packet(part, strips, packets[part], [])
         fars.append(send(beyond, ahead_two))
-    sums = [middle(part, strips, packets[part], nears[part]) for part in range(PARTS)]
-    got, begun = [], ()
-    for part in range(PARTS):
-        out, other = rest(part, strips, packets[part], nears[part], fars[part], sums[part], begun, tuple(sums[part + 1 :]))
-        got.append(send(other, swap))
-        begun = (out,)
-    return join(got, out)
+    sums_b = middle(1, strips, packets[1], nears[1], ())
+    taps = ready(1, strips, sums_b)
+    sums_a = middle(0, strips, packets[0], nears[0], (taps,))
+    out, other_a = rest(0, strips, packets[0], nears[0], fars[0], sums_a, (), (sums_b,))
+    got_a = send(other_a, swap)
+    out, other_b = rest(1, taps, packets[1], nears[1], fars[1], sums_b, (out,), ())
+    return join([got_a, send(other_b, swap)], out)
 
 
 def solution(mesh):

time: 56.7 us -> 55.6 us (0.981)
  the two profiles are of different devices: /device:TPU:13 before, /device:TPU:0 now
where the time goes in v6:
time: 55.6 us; the launch traced here: 55.3 us
  Pallas kernels  37.2 us (67%)
  starting transfers between devices  16.4 us (29%)
  waiting for transfers between devices  1.56 us (3%)
    ppermute x8, starting transfers between devices, send(): return lax.ppermute(value, 'ctx', links)  16.4 us
    pallas_call x2, Pallas kernels, middle(): call(functools.partial(middle_kernel, groups=groups, first_group=part * (...  9.64 us
    pallas_call x2, Pallas kernels, short(): call(functools.partial(short_kernel, groups=groups, first_group=part * (s...  8.07 us
    pallas_call x2, Pallas kernels, rest(): call(functools.partial(rest_kernel, groups=groups, first_group=part * (sh...  6.12 us
    pallas_call x2, Pallas kernels, far_packet(): call(functools.partial(far_kernel, groups=groups, first_group=part * (sha...  5.81 us
    pallas_call x2, Pallas kernels, begin(): call(pack_kernel, 'pack', (steps,), [pl.BlockSpec((rows, block), lambda i...  3.96 us
    pallas_call x1, Pallas kernels, ready(): call(functools.partial(ready_kernel, groups=groups, first_group=part * (s...  1.99 us
    ppermute x8, waiting for transfers between devices, send(): return lax.ppermute(value, 'ctx', links)  1.56 us
  transfers between devices with their start and end apart: 8, of which 1 were waited for; matrix products, arithmetic and copies ran while one was open for 0% of the time, Pallas kernels for 58%

profile of v6, /device:TPU:0, one launch (start us, length us, event | category | flops | bytes accessed | tf_op | source)
XLA Modules:
  0.0 55.3 jit_solution(15257907757279076272)
XLA Ops:
  0.0 2.0 %pack.2 = bf16[272,1024]{1,0:T(8,128)(2,1)} custom-call(s32[1]{0:T(128)} %bitcast.core, bf16[128,4096]{1,0:T(8,128)(2,1)} %key.7, bf16[128,4096]{1,0:T(8,128)(2,1)} %value.7, bf16[128,4096]{1,0:T(8,128)(2,1)} %gate.7, s32[1,128]{1,0:T(1,128)} %bitcast.2), custom_call_target="tpu_custom_call" | custom-call | tf_op jit(solution)/shard_map/pack/pallas_call | solution.py:408
  2.0 0.5 collective-permute-start
  2.4 2.0 %pack.3 = bf16[272,1024]{1,0:T(8,128)(2,1)} custom-call(s32[1]{0:T(128)} %bitcast.core, bf16[128,4096]{1,0:T(8,128)(2,1)} %key.7, bf16[128,4096]{1,0:T(8,128)(2,1)} %value.7, bf16[128,4096]{1,0:T(8,128)(2,1)} %gate.7, s32[1,128]{1,0:T(1,128)} %bitcast.3), custom_call_target="tpu_custom_call" | custom-call | tf_op jit(solution)/shard_map/pack/pallas_call | solution.py:408
  4.4 0.0 copy-start.2
  4.4 0.1 collective-permute-start.1
  4.5 0.0 collective-permute-done.sib
  4.5 4.1 %short.2 = (bf16[272,1024]{1,0:T(8,128)(2,1)}, bf16[272,1024]{1,0:T(8,128)(2,1)S(1)}) custom-call(s32[1]{0:T(128)} %bitcast.core, s32[1,128]{1,0:T(1,128)} %bitcast.4, bf16[128,4096]{1,0:T(8,128)(2,1)} %key.7, bf16[128,4096]{1,0:T(8,128)(2,1)} %value.7, bf16[128,4096]{1,0:T(8,128)(2,1)} %gate.7, bf16[272,1024]{1,0:T(8,128)(2,1)S(1)} %collective-permute-done.sib, ...), custom_call_target="tpu_custom_call" | custom-call | tf_op jit(solution)/shard_map/short/pallas_call | solution.py:428
  8.5 4.9 %collective-permute-start.4 = (bf16[272,1024]{1,0:T(8,128)(2,1)}, bf16[272,1024]{1,0:T(8,128)(2,1)S(1)}, u32[]{:S(2)}, u32[]{:S(2)}) collective-permute-start(bf16[272,1024]{1,0:T(8,128)(2,1)} %get-tuple-element.13.after), channel_id=1, source_target_pairs={{0,2},{1,3},{2,4},{3,5},{4,6},{5,7},{6,8},{7,9},{8,10},{9,11},{10,... | collective-permute-start | bytes 1671176 | tf_op jit(solution)/shard_map/ppermute | solution.py:362
  13.4 0.0 collective-permute-done.1.sib
  13.4 4.0 %short.3 = (bf16[272,1024]{1,0:T(8,128)(2,1)}, bf16[272,1024]{1,0:T(8,128)(2,1)S(1)}) custom-call(s32[1]{0:T(128)} %bitcast.core, s32[1,128]{1,0:T(1,128)} %bitcast.5, bf16[128,4096]{1,0:T(8,128)(2,1)} %key.7, bf16[128,4096]{1,0:T(8,128)(2,1)} %value.7, bf16[128,4096]{1,0:T(8,128)(2,1)} %gate.7, bf16[272,1024]{1,0:T(8,128)(2,1)S(1)} %collective-permute-done.1.sib, ...), custom_call_target="tpu_custom_call" | custom-call | tf_op jit(solution)/shard_map/short/pallas_call | solution.py:428
  17.4 3.4 %collective-permute-start.2 = (bf16[272,1024]{1,0:T(8,128)(2,1)}, bf16[272,1024]{1,0:T(8,128)(2,1)S(1)}, u32[]{:S(2)}, u32[]{:S(2)}) collective-permute-start(bf16[272,1024]{1,0:T(8,128)(2,1)} %get-tuple-element.15), channel_id=1, source_target_pairs={{0,2},{1,3},{2,4},{3,5},{4,6},{5,7},{6,8},{7,9},{8,10},{9,11},{10,... | collective-permute-start | bytes 1671176 | tf_op jit(solution)/shard_map/ppermute | solution.py:362
  20.9 0.0 copy-done.2
  20.9 0.7 %strips.1 = bf16[128,16,768]{2,1,0:T(8,128)(2,1)S(1)} custom-call(s32[1]{0:T(128)} %bitcast.core, bf16[256,512]{1,0:T(8,128)(2,1)S(1)} %copy-done.2, bf16[272,1024]{1,0:T(8,128)(2,1)} %get-tuple-element.13.after), custom_call_target="tpu_custom_call" | custom-call | tf_op jit(solution)/shard_map/strips/pallas_call | solution.py:546
  21.6 0.0 copy-start.1
  21.6 2.9 %far.2 = bf16[144,1024]{1,0:T(8,128)(2,1)} custom-call(s32[1]{0:T(128)} %bitcast.core, bf16[128,16,768]{2,1,0:T(8,128)(2,1)S(1)} %strips.1, bf16[272,1024]{1,0:T(8,128)(2,1)S(1)} %get-tuple-element.14.packet), custom_call_target="tpu_custom_call" | custom-call | tf_op jit(solution)/shard_map/far/pallas_call | solution.py:452
  24.5 3.5 %collective-permute-start.3 = (bf16[144,1024]{1,0:T(8,128)(2,1)}, bf16[144,1024]{1,0:T(8,128)(2,1)S(1)}, u32[]{:S(2)}, u32[]{:S(2)}) collective-permute-start(bf16[144,1024]{1,0:T(8,128)(2,1)} %far.2), channel_id=1, source_target_pairs={{0,4},{1,5},{2,6},{3,7},{4,8},{5,9},{6,10},{7,11},{8,12},{9,13},{1... | collective-permute-start | bytes 884744 | tf_op jit(solution)/shard_map/ppermute | solution.py:362
  28.0 2.9 %far.3 = bf16[144,1024]{1,0:T(8,128)(2,1)} custom-call(s32[1]{0:T(128)} %bitcast.core, bf16[128,16,768]{2,1,0:T(8,128)(2,1)S(1)} %strips.1, bf16[272,1024]{1,0:T(8,128)(2,1)S(1)} %get-tuple-element.16.packet), custom_call_target="tpu_custom_call" | custom-call | tf_op jit(solution)/shard_map/far/pallas_call | solution.py:452
  30.9 3.7 %collective-permute-start.6 = (bf16[144,1024]{1,0:T(8,128)(2,1)}, bf16[144,1024]{1,0:T(8,128)(2,1)S(1)}, u32[]{:S(2)}, u32[]{:S(2)}) collective-permute-start(bf16[144,1024]{1,0:T(8,128)(2,1)} %far.3), channel_id=1, source_target_pairs={{0,4},{1,5},{2,6},{3,7},{4,8},{5,9},{6,10},{7,11},{8,12},{9,13},{1... | collective-permute-start | bytes 884744 | tf_op jit(solution)/shard_map/ppermute | solution.py:362
  34.5 0.0 collective-permute-done.4.near
  34.5 0.0 copy-done.1
  34.5 4.8 %middle.2.after.refs_0_.sums = f32[256,1024]{1,0:T(8,128)S(1)} custom-call(s32[1]{0:T(128)} %bitcast.core, bf16[128,16,768]{2,1,0:T(8,128)(2,1)S(1)} %strips.1, bf16[272,1024]{1,0:T(8,128)(2,1)S(1)} %get-tuple-element.16.packet, bf16[272,1024]{1,0:T(8,128)(2,1)S(1)} %collective-permute-done.4.near, f32[7,256]{1,0:T(8,128)S(1)} %copy-done.1), custom_call_target="tpu_custom_call" | custom-call | tf_op jit(solution)/shard_map/middle/pallas_call | solution.py:469
  39.4 2.0 %ready.1.refs_0_.strips = bf16[8,1024,256]{2,1,0:T(8,128)(2,1)S(1)} custom-call(s32[1]{0:T(128)} %bitcast.core, bf16[128,16,768]{2,1,0:T(8,128)(2,1)S(1)} %strips.1, f32[256,1024]{1,0:T(8,128)S(1)} %middle.2.after.refs_0_.sums), custom_call_target="tpu_custom_call" | custom-call | tf_op jit(solution)/shard_map/ready/pallas_call | solution.py:490
  41.4 0.0 copy-start
  41.4 0.0 collective-permute-done.2.near
  41.4 4.8 %middle.3.sums = f32[256,1024]{1,0:T(8,128)S(1)} custom-call(s32[1]{0:T(128)} %bitcast.core, bf16[128,16,768]{2,1,0:T(8,128)(2,1)S(1)} %strips.1, bf16[272,1024]{1,0:T(8,128)(2,1)S(1)} %get-tuple-element.14.packet, bf16[272,1024]{1,0:T(8,128)(2,1)S(1)} %collective-permute-done.2.near, f32[7,256]{1,0:T(8,128)S(1)} %copy-done.1, ...), custom_call_target="tpu_custom_call" | custom-call | tf_op jit(solution)/shard_map/middle/pallas_call | solution.py:469
  46.2 0.0 collective-permute-done.3.far
  46.2 0.0 copy-done
  46.2 3.7 %rest.2 = (bf16[128,4096]{1,0:T(8,128)(2,1)}, bf16[128,1024]{1,0:T(8,128)(2,1)}) custom-call(s32[1]{0:T(128)} %bitcast.core, bf16[128,16,768]{2,1,0:T(8,128)(2,1)S(1)} %strips.1, bf16[272,1024]{1,0:T(8,128)(2,1)S(1)} %get-tuple-element.14.packet, bf16[272,1024]{1,0:T(8,128)(2,1)S(1)} %collective-permute-done.2.near, ...), custom_call_target="tpu_custom_call" | custom-call | tf_op jit(solution)/shard_map/rest/pallas_call | solution.py:500
  49.9 0.0 collective-permute-done.6.far
  49.9 0.0 copy-start.3
  49.9 2.4 %rest.3 = (bf16[128,4096]{1,0:T(8,128)(2,1)}, bf16[128,1024]{1,0:T(8,128)(2,1)}) custom-call(s32[1]{0:T(128)} %bitcast.core, bf16[8,1024,256]{2,1,0:T(8,128)(2,1)S(1)} %ready.1.refs_0_.strips, bf16[272,1024]{1,0:T(8,128)(2,1)S(1)} %get-tuple-element.16.packet, bf16[272,1024]{1,0:T(8,128)(2,1)S(1)} %collective-permute-done.4.near, ...), custom_call_target="tpu_custom_call", output_to_operand_aliasing={{0}: (8, {})} | custom-call | tf_op jit(solution)/shard_map/rest/pallas_call | solution.py:500
  52.4 0.0 collective-permute-start.7
  52.4 0.0 copy-done.3
  52.4 0.5 collective-permute-start.5
  52.9 1.5 %collective-permute-done.7.refs_1_ = bf16[128,1024]{1,0:T(8,128)(2,1)S(1)} collective-permute-done((bf16[128,1024]{1,0:T(8,128)(2,1)}, bf16[128,1024]{1,0:T(8,128)(2,1)S(1)}, u32[]{:S(2)}, u32[]{:S(2)}) %collective-permute-start.7) | collective-permute-done | bytes 262176 | tf_op jit(solution)/shard_map/ppermute | solution.py:362
  54.4 0.0 collective-permute-done.5.refs_0_
  54.4 0.9 %join.1 = bf16[128,4096]{1,0:T(8,128)(2,1)} custom-call(s32[1]{0:T(128)} %bitcast.core, bf16[128,1024]{1,0:T(8,128)(2,1)S(1)} %collective-permute-done.5.refs_0_, bf16[128,1024]{1,0:T(8,128)(2,1)S(1)} %collective-permute-done.7.refs_1_, bf16[128,4096]{1,0:T(8,128)(2,1)S(1)} %copy-done, ...), custom_call_target="tpu_custom_call", output_to_operand_aliasing={{}: (4, {})} | custom-call | tf_op jit(solution)/shard_map/join/pallas_call | solution.py:533
Async XLA Ops:
  2.0 2.5 %collective-permute-start = (bf16[272,1024]{1,0:T(8,128)(2,1)}, bf16[272,1024]{1,0:T(8,128)(2,1)S(1)}, u32[]{:S(2)}, u32[]{:S(2)}) collective-permute-start(bf16[272,1024]{1,0:T(8,128)(2,1)} %pack.2), channel_id=1, source_target_pairs={{0,1},{1,0},{2,3},{3,2},{4,5},{5,4},{6,7},{7,6},{8,9},{9,8},{10,11... | collective-permute-start | bytes 1671176 | tf_op jit(solution)/shard_map/ppermute | solution.py:362
  4.4 16.4 %copy-start.2 = (bf16[256,512]{1,0:T(8,128)(2,1)S(1)}, bf16[256,512]{1,0:T(8,128)(2,1)}, u32[]{:S(2)}) copy-start(bf16[256,512]{1,0:T(8,128)(2,1)} %filters.1) | copy-start | bytes 786436
  4.4 9.0 %collective-permute-start.1 = (bf16[272,1024]{1,0:T(8,128)(2,1)}, bf16[272,1024]{1,0:T(8,128)(2,1)S(1)}, u32[]{:S(2)}, u32[]{:S(2)}) collective-permute-start(bf16[272,1024]{1,0:T(8,128)(2,1)} %pack.3), channel_id=1, source_target_pairs={{0,1},{1,0},{2,3},{3,2},{4,5},{5,4},{6,7},{7,6},{8,9},{9,8},{10,11... | collective-permute-start | bytes 1671176 | tf_op jit(solution)/shard_map/ppermute | solution.py:362
  8.5 26.0 %collective-permute-start.4 = (bf16[272,1024]{1,0:T(8,128)(2,1)}, bf16[272,1024]{1,0:T(8,128)(2,1)S(1)}, u32[]{:S(2)}, u32[]{:S(2)}) collective-permute-start(bf16[272,1024]{1,0:T(8,128)(2,1)} %get-tuple-element.13.after), channel_id=1, source_target_pairs={{0,2},{1,3},{2,4},{3,5},{4,6},{5,7},{6,8},{7,9},{8,10},{9,11},{10,... | collective-permute-start | bytes 1671176 | tf_op jit(solution)/shard_map/ppermute | solution.py:362
  17.4 23.9 %collective-permute-start.2 = (bf16[272,1024]{1,0:T(8,128)(2,1)}, bf16[272,1024]{1,0:T(8,128)(2,1)S(1)}, u32[]{:S(2)}, u32[]{:S(2)}) collective-permute-start(bf16[272,1024]{1,0:T(8,128)(2,1)} %get-tuple-element.15), channel_id=1, source_target_pairs={{0,2},{1,3},{2,4},{3,5},{4,6},{5,7},{6,8},{7,9},{8,10},{9,11},{10,... | collective-permute-start | bytes 1671176 | tf_op jit(solution)/shard_map/ppermute | solution.py:362
  21.6 13.0 %copy-start.1 = (f32[7,256]{1,0:T(8,128)S(1)}, f32[7,256]{1,0:T(8,128)}, u32[]{:S(2)}) copy-start(f32[7,256]{1,0:T(8,128)} %short_filter.11) | copy-start | bytes 21508
  24.5 21.7 %collective-permute-start.3 = (bf16[144,1024]{1,0:T(8,128)(2,1)}, bf16[144,1024]{1,0:T(8,128)(2,1)S(1)}, u32[]{:S(2)}, u32[]{:S(2)}) collective-permute-start(bf16[144,1024]{1,0:T(8,128)(2,1)} %far.2), channel_id=1, source_target_pairs={{0,4},{1,5},{2,6},{3,7},{4,8},{5,9},{6,10},{7,11},{8,12},{9,13},{1... | collective-permute-start | bytes 884744 | tf_op jit(solution)/shard_map/ppermute | solution.py:362
  30.9 19.1 %collective-permute-start.6 = (bf16[144,1024]{1,0:T(8,128)(2,1)}, bf16[144,1024]{1,0:T(8,128)(2,1)S(1)}, u32[]{:S(2)}, u32[]{:S(2)}) collective-permute-start(bf16[144,1024]{1,0:T(8,128)(2,1)} %far.3), channel_id=1, source_target_pairs={{0,4},{1,5},{2,6},{3,7},{4,8},{5,9},{6,10},{7,11},{8,12},{9,13},{1... | collective-permute-start | bytes 884744 | tf_op jit(solution)/shard_map/ppermute | solution.py:362
  41.4 4.9 %copy-start = (bf16[128,4096]{1,0:T(8,128)(2,1)S(1)}, bf16[128,4096]{1,0:T(8,128)(2,1)}, u32[]{:S(2)}) copy-start(bf16[128,4096]{1,0:T(8,128)(2,1)} %refs_2_.1) | copy-start | bytes 3145732
  49.9 2.4 %copy-start.3 = (bf16[128,1024]{1,0:T(8,128)(2,1)S(1)}, bf16[128,1024]{1,0:T(8,128)(2,1)}, u32[]{:S(2)}) copy-start(bf16[128,1024]{1,0:T(8,128)(2,1)} %get-tuple-element.17) | copy-start | bytes 786436
  52.4 2.1 %collective-permute-start.7 = (bf16[128,1024]{1,0:T(8,128)(2,1)}, bf16[128,1024]{1,0:T(8,128)(2,1)S(1)}, u32[]{:S(2)}, u32[]{:S(2)}) collective-permute-start(bf16[128,1024]{1,0:T(8,128)(2,1)} %get-tuple-element.19), channel_id=1, source_target_pairs={{0,1},{1,0},{2,3},{3,2},{4,5},{5,4},{6,7},{7,6},{8,9},{9,8},{10,11... | collective-permute-start | bytes 786440 | tf_op jit(solution)/shard_map/ppermute | solution.py:362
  52.4 2.1 %collective-permute-start.5 = (bf16[128,1024]{1,0:T(8,128)(2,1)S(1)}, bf16[128,1024]{1,0:T(8,128)(2,1)S(1)}, u32[]{:S(2)}, u32[]{:S(2)}) collective-permute-start(bf16[128,1024]{1,0:T(8,128)(2,1)S(1)} %copy-done.3), channel_id=1, source_target_pairs={{0,1},{1,0},{2,3},{3,2},{4,5},{5,4},{6,7},{7,6},{8,9},{9,8},{10,11... | collective-permute-start | bytes 786440 | tf_op jit(solution)/shard_map/ppermute | solution.py:362

commit v7 on v6

--- a/solution.py
+++ b/solution.py
@@ -107,7 +107,7 @@
     gate_rows[pl.ds(other, rows), :] = sib[rows : 2 * rows, :].astype(F32)
     for tile in range(width // LANES):
         cols = slice(tile * LANES, tile * LANES + LANES)
-        taps = widen(short_filter, first_group + tile * groups, groups)
+        taps = widen(short_filter, first_group + (step * (width // LANES) + tile) * groups, groups)
         total = kv_rows[8 : 8 + 2 * rows, cols] * taps[0:1]
         for k in range(1, tap_count):
             total = total + agree[k] * kv_rows[8 - k : 8 - k + 2 * rows, cols] * taps[k : k + 1]
@@ -425,24 +425,26 @@
         )
 
     def short(part, sibling, after):
+        piece = pl.BlockSpec((2 * rows + SLAB, share // 2), lambda i, c: (0, i))
+        ours = pl.BlockSpec((rows, share // 2), lambda i, c: (0, (PARTS * c[0] + part) * 2 + i))
         return call(
             functools.partial(short_kernel, groups=groups, first_group=part * (share // group_width)),
             "short",
-            (steps,),
+            (2,),
             [
                 whole((1, rows)),
-                mine(rows, part),
-                mine(rows, part),
-                mine(rows, part),
-                local(2 * rows + SLAB),
+                ours,
+                ours,
+                ours,
+                piece,
                 short_spec,
             ]
             + [anywhere] * len(after),
-            [local(2 * rows + SLAB)] * 2,
+            [piece] * 2,
             [shape(2 * rows + SLAB, share), jax.ShapeDtypeStruct((2 * rows + SLAB, share), BF16)],
             [
-                pltpu.VMEM((8 + 2 * rows, block), F32),
-                pltpu.VMEM((2 * rows, block), F32),
+                pltpu.VMEM((8 + 2 * rows, share // 2), F32),
+                pltpu.VMEM((2 * rows, share // 2), F32),
                 pltpu.VMEM((tap_count, 2 * rows, LANES), F32),
                 pltpu.VMEM((8 + 2 * rows, LANES), F32),
             ],

time: 55.6 us -> 55.5 us (level)
  no operation moved by 1% of the time
where the time goes in v7:
time: 55.5 us; the launch traced here: 55 us
  Pallas kernels  36.9 us (66%)
  starting transfers between devices  16.4 us (30%)
  waiting for transfers between devices  1.56 us (3%)
    ppermute x8, starting transfers between devices, send(): return lax.ppermute(value, 'ctx', links)  16.4 us
    pallas_call x2, Pallas kernels, middle(): call(functools.partial(middle_kernel, groups=groups, first_group=part * (...  9.63 us
    pallas_call x2, Pallas kernels, short(): call(functools.partial(short_kernel, groups=groups, first_group=part * (s...  7.82 us
    pallas_call x2, Pallas kernels, rest(): call(functools.partial(rest_kernel, groups=groups, first_group=part * (sh...  6.12 us
    pallas_call x2, Pallas kernels, far_packet(): call(functools.partial(far_kernel, groups=groups, first_group=part * (sha...  5.81 us
    pallas_call x2, Pallas kernels, begin(): call(pack_kernel, 'pack', (steps,), [pl.BlockSpec((rows, block), lambda i...  3.96 us
    pallas_call x1, Pallas kernels, ready(): call(functools.partial(ready_kernel, groups=groups, first_group=part * (s...  1.99 us
    ppermute x8, waiting for transfers between devices, send(): return lax.ppermute(value, 'ctx', links)  1.56 us
  transfers between devices with their start and end apart: 8, of which 1 were waited for; matrix products, arithmetic and copies ran while one was open for 0% of the time, Pallas kernels for 58%

profile of v7, /device:TPU:0, one launch (start us, length us, event | category | flops | bytes accessed | tf_op | source)
XLA Modules:
  0.0 55.0 jit_solution(12589336450032283291)
XLA Ops:
  0.0 2.0 %pack.2 = bf16[272,1024]{1,0:T(8,128)(2,1)} custom-call(s32[1]{0:T(128)} %bitcast.core, bf16[128,4096]{1,0:T(8,128)(2,1)} %key.7, bf16[128,4096]{1,0:T(8,128)(2,1)} %value.7, bf16[128,4096]{1,0:T(8,128)(2,1)} %gate.7, s32[1,128]{1,0:T(1,128)} %bitcast.2), custom_call_target="tpu_custom_call" | custom-call | tf_op jit(solution)/shard_map/pack/pallas_call | solution.py:408
  2.0 0.5 collective-permute-start
  2.4 2.0 %pack.3 = bf16[272,1024]{1,0:T(8,128)(2,1)} custom-call(s32[1]{0:T(128)} %bitcast.core, bf16[128,4096]{1,0:T(8,128)(2,1)} %key.7, bf16[128,4096]{1,0:T(8,128)(2,1)} %value.7, bf16[128,4096]{1,0:T(8,128)(2,1)} %gate.7, s32[1,128]{1,0:T(1,128)} %bitcast.3), custom_call_target="tpu_custom_call" | custom-call | tf_op jit(solution)/shard_map/pack/pallas_call | solution.py:408
  4.4 0.0 copy-start.2
  4.4 0.1 collective-permute-start.1
  4.5 0.0 collective-permute-done.sib
  4.5 3.9 %short.2 = (bf16[272,1024]{1,0:T(8,128)(2,1)}, bf16[272,1024]{1,0:T(8,128)(2,1)S(1)}) custom-call(s32[1]{0:T(128)} %bitcast.core, s32[1,128]{1,0:T(1,128)} %bitcast.4, bf16[128,4096]{1,0:T(8,128)(2,1)} %key.7, bf16[128,4096]{1,0:T(8,128)(2,1)} %value.7, bf16[128,4096]{1,0:T(8,128)(2,1)} %gate.7, bf16[272,1024]{1,0:T(8,128)(2,1)S(1)} %collective-permute-done.sib, ...), custom_call_target="tpu_custom_call" | custom-call | tf_op jit(solution)/shard_map/short/pallas_call | solution.py:430
  8.4 4.9 %collective-permute-start.4 = (bf16[272,1024]{1,0:T(8,128)(2,1)}, bf16[272,1024]{1,0:T(8,128)(2,1)S(1)}, u32[]{:S(2)}, u32[]{:S(2)}) collective-permute-start(bf16[272,1024]{1,0:T(8,128)(2,1)} %get-tuple-element.13.after), channel_id=1, source_target_pairs={{0,2},{1,3},{2,4},{3,5},{4,6},{5,7},{6,8},{7,9},{8,10},{9,11},{10,... | collective-permute-start | bytes 1671176 | tf_op jit(solution)/shard_map/ppermute | solution.py:362
  13.2 0.0 collective-permute-done.1.sib
  13.2 3.9 %short.3 = (bf16[272,1024]{1,0:T(8,128)(2,1)}, bf16[272,1024]{1,0:T(8,128)(2,1)S(1)}) custom-call(s32[1]{0:T(128)} %bitcast.core, s32[1,128]{1,0:T(1,128)} %bitcast.5, bf16[128,4096]{1,0:T(8,128)(2,1)} %key.7, bf16[128,4096]{1,0:T(8,128)(2,1)} %value.7, bf16[128,4096]{1,0:T(8,128)(2,1)} %gate.7, bf16[272,1024]{1,0:T(8,128)(2,1)S(1)} %collective-permute-done.1.sib, ...), custom_call_target="tpu_custom_call" | custom-call | tf_op jit(solution)/shard_map/short/pallas_call | solution.py:430
  17.2 3.4 %collective-permute-start.2 = (bf16[272,1024]{1,0:T(8,128)(2,1)}, bf16[272,1024]{1,0:T(8,128)(2,1)S(1)}, u32[]{:S(2)}, u32[]{:S(2)}) collective-permute-start(bf16[272,1024]{1,0:T(8,128)(2,1)} %get-tuple-element.15), channel_id=1, source_target_pairs={{0,2},{1,3},{2,4},{3,5},{4,6},{5,7},{6,8},{7,9},{8,10},{9,11},{10,... | collective-permute-start | bytes 1671176 | tf_op jit(solution)/shard_map/ppermute | solution.py:362
  20.6 0.0 copy-done.2
  20.6 0.7 %strips.1 = bf16[128,16,768]{2,1,0:T(8,128)(2,1)S(1)} custom-call(s32[1]{0:T(128)} %bitcast.core, bf16[256,512]{1,0:T(8,128)(2,1)S(1)} %copy-done.2, bf16[272,1024]{1,0:T(8,128)(2,1)} %get-tuple-element.13.after), custom_call_target="tpu_custom_call" | custom-call | tf_op jit(solution)/shard_map/strips/pallas_call | solution.py:548
  21.3 0.0 copy-start.1
  21.4 2.9 %far.2 = bf16[144,1024]{1,0:T(8,128)(2,1)} custom-call(s32[1]{0:T(128)} %bitcast.core, bf16[128,16,768]{2,1,0:T(8,128)(2,1)S(1)} %strips.1, bf16[272,1024]{1,0:T(8,128)(2,1)S(1)} %get-tuple-element.14.packet), custom_call_target="tpu_custom_call" | custom-call | tf_op jit(solution)/shard_map/far/pallas_call | solution.py:454
  24.3 3.5 %collective-permute-start.3 = (bf16[144,1024]{1,0:T(8,128)(2,1)}, bf16[144,1024]{1,0:T(8,128)(2,1)S(1)}, u32[]{:S(2)}, u32[]{:S(2)}) collective-permute-start(bf16[144,1024]{1,0:T(8,128)(2,1)} %far.2), channel_id=1, source_target_pairs={{0,4},{1,5},{2,6},{3,7},{4,8},{5,9},{6,10},{7,11},{8,12},{9,13},{1... | collective-permute-start | bytes 884744 | tf_op jit(solution)/shard_map/ppermute | solution.py:362
  27.7 2.9 %far.3 = bf16[144,1024]{1,0:T(8,128)(2,1)} custom-call(s32[1]{0:T(128)} %bitcast.core, bf16[128,16,768]{2,1,0:T(8,128)(2,1)S(1)} %strips.1, bf16[272,1024]{1,0:T(8,128)(2,1)S(1)} %get-tuple-element.16.packet), custom_call_target="tpu_custom_call" | custom-call | tf_op jit(solution)/shard_map/far/pallas_call | solution.py:454
  30.6 3.7 %collective-permute-start.6 = (bf16[144,1024]{1,0:T(8,128)(2,1)}, bf16[144,1024]{1,0:T(8,128)(2,1)S(1)}, u32[]{:S(2)}, u32[]{:S(2)}) collective-permute-start(bf16[144,1024]{1,0:T(8,128)(2,1)} %far.3), channel_id=1, source_target_pairs={{0,4},{1,5},{2,6},{3,7},{4,8},{5,9},{6,10},{7,11},{8,12},{9,13},{1... | collective-permute-start | bytes 884744 | tf_op jit(solution)/shard_map/ppermute | solution.py:362
  34.3 0.0 collective-permute-done.4.near
  34.3 0.0 copy-done.1
  34.3 4.8 %middle.2.after.refs_0_.sums = f32[256,1024]{1,0:T(8,128)S(1)} custom-call(s32[1]{0:T(128)} %bitcast.core, bf16[128,16,768]{2,1,0:T(8,128)(2,1)S(1)} %strips.1, bf16[272,1024]{1,0:T(8,128)(2,1)S(1)} %get-tuple-element.16.packet, bf16[272,1024]{1,0:T(8,128)(2,1)S(1)} %collective-permute-done.4.near, f32[7,256]{1,0:T(8,128)S(1)} %copy-done.1), custom_call_target="tpu_custom_call" | custom-call | tf_op jit(solution)/shard_map/middle/pallas_call | solution.py:471
  39.1 2.0 %ready.1.refs_0_.strips = bf16[8,1024,256]{2,1,0:T(8,128)(2,1)S(1)} custom-call(s32[1]{0:T(128)} %bitcast.core, bf16[128,16,768]{2,1,0:T(8,128)(2,1)S(1)} %strips.1, f32[256,1024]{1,0:T(8,128)S(1)} %middle.2.after.refs_0_.sums), custom_call_target="tpu_custom_call" | custom-call | tf_op jit(solution)/shard_map/ready/pallas_call | solution.py:492
  41.1 0.0 copy-start
  41.1 0.0 collective-permute-done.2.near
  41.1 4.8 %middle.3.sums = f32[256,1024]{1,0:T(8,128)S(1)} custom-call(s32[1]{0:T(128)} %bitcast.core, bf16[128,16,768]{2,1,0:T(8,128)(2,1)S(1)} %strips.1, bf16[272,1024]{1,0:T(8,128)(2,1)S(1)} %get-tuple-element.14.packet, bf16[272,1024]{1,0:T(8,128)(2,1)S(1)} %collective-permute-done.2.near, f32[7,256]{1,0:T(8,128)S(1)} %copy-done.1, ...), custom_call_target="tpu_custom_call" | custom-call | tf_op jit(solution)/shard_map/middle/pallas_call | solution.py:471
  46.0 0.0 collective-permute-done.3.far
  46.0 0.0 copy-done
  46.0 3.7 %rest.2 = (bf16[128,4096]{1,0:T(8,128)(2,1)}, bf16[128,1024]{1,0:T(8,128)(2,1)}) custom-call(s32[1]{0:T(128)} %bitcast.core, bf16[128,16,768]{2,1,0:T(8,128)(2,1)S(1)} %strips.1, bf16[272,1024]{1,0:T(8,128)(2,1)S(1)} %get-tuple-element.14.packet, bf16[272,1024]{1,0:T(8,128)(2,1)S(1)} %collective-permute-done.2.near, ...), custom_call_target="tpu_custom_call" | custom-call | tf_op jit(solution)/shard_map/rest/pallas_call | solution.py:502
  49.7 0.0 collective-permute-done.6.far
  49.7 0.0 copy-start.3
  49.7 2.4 %rest.3 = (bf16[128,4096]{1,0:T(8,128)(2,1)}, bf16[128,1024]{1,0:T(8,128)(2,1)}) custom-call(s32[1]{0:T(128)} %bitcast.core, bf16[8,1024,256]{2,1,0:T(8,128)(2,1)S(1)} %ready.1.refs_0_.strips, bf16[272,1024]{1,0:T(8,128)(2,1)S(1)} %get-tuple-element.16.packet, bf16[272,1024]{1,0:T(8,128)(2,1)S(1)} %collective-permute-done.4.near, ...), custom_call_target="tpu_custom_call", output_to_operand_aliasing={{0}: (8, {})} | custom-call | tf_op jit(solution)/shard_map/rest/pallas_call | solution.py:502
  52.1 0.0 collective-permute-start.7
  52.1 0.0 copy-done.3
  52.1 0.5 collective-permute-start.5
  52.6 1.5 %collective-permute-done.7.refs_1_ = bf16[128,1024]{1,0:T(8,128)(2,1)S(1)} collective-permute-done((bf16[128,1024]{1,0:T(8,128)(2,1)}, bf16[128,1024]{1,0:T(8,128)(2,1)S(1)}, u32[]{:S(2)}, u32[]{:S(2)}) %collective-permute-start.7) | collective-permute-done | bytes 262176 | tf_op jit(solution)/shard_map/ppermute | solution.py:362
  54.2 0.0 collective-permute-done.5.refs_0_
  54.2 0.9 %join.1 = bf16[128,4096]{1,0:T(8,128)(2,1)} custom-call(s32[1]{0:T(128)} %bitcast.core, bf16[128,1024]{1,0:T(8,128)(2,1)S(1)} %collective-permute-done.5.refs_0_, bf16[128,1024]{1,0:T(8,128)(2,1)S(1)} %collective-permute-done.7.refs_1_, bf16[128,4096]{1,0:T(8,128)(2,1)S(1)} %copy-done, ...), custom_call_target="tpu_custom_call", output_to_operand_aliasing={{}: (4, {})} | custom-call | tf_op jit(solution)/shard_map/join/pallas_call | solution.py:535
Async XLA Ops:
  2.0 2.5 %collective-permute-start = (bf16[272,1024]{1,0:T(8,128)(2,1)}, bf16[272,1024]{1,0:T(8,128)(2,1)S(1)}, u32[]{:S(2)}, u32[]{:S(2)}) collective-permute-start(bf16[272,1024]{1,0:T(8,128)(2,1)} %pack.2), channel_id=1, source_target_pairs={{0,1},{1,0},{2,3},{3,2},{4,5},{5,4},{6,7},{7,6},{8,9},{9,8},{10,11... | collective-permute-start | bytes 1671176 | tf_op jit(solution)/shard_map/ppermute | solution.py:362
  4.4 16.2 %copy-start.2 = (bf16[256,512]{1,0:T(8,128)(2,1)S(1)}, bf16[256,512]{1,0:T(8,128)(2,1)}, u32[]{:S(2)}) copy-start(bf16[256,512]{1,0:T(8,128)(2,1)} %filters.1) | copy-start | bytes 786436
  4.4 8.8 %collective-permute-start.1 = (bf16[272,1024]{1,0:T(8,128)(2,1)}, bf16[272,1024]{1,0:T(8,128)(2,1)S(1)}, u32[]{:S(2)}, u32[]{:S(2)}) collective-permute-start(bf16[272,1024]{1,0:T(8,128)(2,1)} %pack.3), channel_id=1, source_target_pairs={{0,1},{1,0},{2,3},{3,2},{4,5},{5,4},{6,7},{7,6},{8,9},{9,8},{10,11... | collective-permute-start | bytes 1671176 | tf_op jit(solution)/shard_map/ppermute | solution.py:362
  8.4 25.9 %collective-permute-start.4 = (bf16[272,1024]{1,0:T(8,128)(2,1)}, bf16[272,1024]{1,0:T(8,128)(2,1)S(1)}, u32[]{:S(2)}, u32[]{:S(2)}) collective-permute-start(bf16[272,1024]{1,0:T(8,128)(2,1)} %get-tuple-element.13.after), channel_id=1, source_target_pairs={{0,2},{1,3},{2,4},{3,5},{4,6},{5,7},{6,8},{7,9},{8,10},{9,11},{10,... | collective-permute-start | bytes 1671176 | tf_op jit(solution)/shard_map/ppermute | solution.py:362
  17.2 23.9 %collective-permute-start.2 = (bf16[272,1024]{1,0:T(8,128)(2,1)}, bf16[272,1024]{1,0:T(8,128)(2,1)S(1)}, u32[]{:S(2)}, u32[]{:S(2)}) collective-permute-start(bf16[272,1024]{1,0:T(8,128)(2,1)} %get-tuple-element.15), channel_id=1, source_target_pairs={{0,2},{1,3},{2,4},{3,5},{4,6},{5,7},{6,8},{7,9},{8,10},{9,11},{10,... | collective-permute-start | bytes 1671176 | tf_op jit(solution)/shard_map/ppermute | solution.py:362
  21.3 13.0 %copy-start.1 = (f32[7,256]{1,0:T(8,128)S(1)}, f32[7,256]{1,0:T(8,128)}, u32[]{:S(2)}) copy-start(f32[7,256]{1,0:T(8,128)} %short_filter.11) | copy-start | bytes 21508
  24.3 21.7 %collective-permute-start.3 = (bf16[144,1024]{1,0:T(8,128)(2,1)}, bf16[144,1024]{1,0:T(8,128)(2,1)S(1)}, u32[]{:S(2)}, u32[]{:S(2)}) collective-permute-start(bf16[144,1024]{1,0:T(8,128)(2,1)} %far.2), channel_id=1, source_target_pairs={{0,4},{1,5},{2,6},{3,7},{4,8},{5,9},{6,10},{7,11},{8,12},{9,13},{1... | collective-permute-start | bytes 884744 | tf_op jit(solution)/shard_map/ppermute | solution.py:362
  30.6 19.1 %collective-permute-start.6 = (bf16[144,1024]{1,0:T(8,128)(2,1)}, bf16[144,1024]{1,0:T(8,128)(2,1)S(1)}, u32[]{:S(2)}, u32[]{:S(2)}) collective-permute-start(bf16[144,1024]{1,0:T(8,128)(2,1)} %far.3), channel_id=1, source_target_pairs={{0,4},{1,5},{2,6},{3,7},{4,8},{5,9},{6,10},{7,11},{8,12},{9,13},{1... | collective-permute-start | bytes 884744 | tf_op jit(solution)/shard_map/ppermute | solution.py:362
  41.1 4.9 %copy-start = (bf16[128,4096]{1,0:T(8,128)(2,1)S(1)}, bf16[128,4096]{1,0:T(8,128)(2,1)}, u32[]{:S(2)}) copy-start(bf16[128,4096]{1,0:T(8,128)(2,1)} %refs_2_.1) | copy-start | bytes 3145732
  49.7 2.4 %copy-start.3 = (bf16[128,1024]{1,0:T(8,128)(2,1)S(1)}, bf16[128,1024]{1,0:T(8,128)(2,1)}, u32[]{:S(2)}) copy-start(bf16[128,1024]{1,0:T(8,128)(2,1)} %get-tuple-element.17) | copy-start | bytes 786436
  52.1 2.1 %collective-permute-start.7 = (bf16[128,1024]{1,0:T(8,128)(2,1)}, bf16[128,1024]{1,0:T(8,128)(2,1)S(1)}, u32[]{:S(2)}, u32[]{:S(2)}) collective-permute-start(bf16[128,1024]{1,0:T(8,128)(2,1)} %get-tuple-element.19), channel_id=1, source_target_pairs={{0,1},{1,0},{2,3},{3,2},{4,5},{5,4},{6,7},{7,6},{8,9},{9,8},{10,11... | collective-permute-start | bytes 786440 | tf_op jit(solution)/shard_map/ppermute | solution.py:362
  52.1 2.1 %collective-permute-start.5 = (bf16[128,1024]{1,0:T(8,128)(2,1)S(1)}, bf16[128,1024]{1,0:T(8,128)(2,1)S(1)}, u32[]{:S(2)}, u32[]{:S(2)}) collective-permute-start(bf16[128,1024]{1,0:T(8,128)(2,1)S(1)} %copy-done.3), channel_id=1, source_target_pairs={{0,1},{1,0},{2,3},{3,2},{4,5},{5,4},{6,7},{7,6},{8,9},{9,8},{10,11... | collective-permute-start | bytes 786440 | tf_op jit(solution)/shard_map/ppermute | solution.py:362
